TPU v7x, 512 devices: a whole 4x8x8 slice. The times are simulated.
512 devices in a mesh: dp: 32 (over x_hi, y, core), expert: 16 (over z, x_lo).
Axes of the slice: x: 4 (x_hi: 2, x_lo: 2; x = x_hi * 2 + x_lo), y: 8, z: 8, core: 2. Of those that a mesh axis runs over, the one named last changes fastest.
Arguments:
- tokens: bfloat16 [512, 256, 1408], P(('dp', 'expert')), may hold values from -12 to 12
- cotangent: bfloat16 [512, 256, 1408], P(('dp', 'expert')), may hold values from -6 to 6
- slot_outputs: bfloat16 [512, 16, 1408], P(('dp', 'expert')), may hold values from -0.29882812 to 0.29882812
- slot_params: bfloat16 [1408, 16], replicated, may hold values from -0.5 to 0.5
- lift_weight: bfloat16 [16, 6144, 1408], P('expert', 'dp'), may hold values from -0.15625 to 0.15625
- drop_weight: bfloat16 [16, 6144, 1408], P('expert', 'dp'), may hold values from -0.078125 to 0.078125
Outputs:
- token_grad: bfloat16 [512, 256, 1408], P(('dp', 'expert'))
- param_grad: float32 [1408, 16], replicated
- lift_grad: bfloat16 [16, 6144, 1408], P('expert', 'dp')
- drop_grad: bfloat16 [16, 6144, 1408], P('expert', 'dp')
All inputs are finite; a program needn't handle non-finite values.
Results may differ from a plain program's by a relative error of at most 0.04.
Values may be sent and summed in bfloat16 or wider, within the bound.
No kernel may reach another device: no remote copies, remote signals or barrier semaphores. Data moves between devices by JAX's collectives and lax.ppermute only.
A program may use at most 64 MiB of HBM per device.

v0:
```python
import jax
import jax.numpy as jnp
from jax import lax
from jax.sharding import PartitionSpec as P


def gelu_value(values):
    return 0.5 * values * (1.0 + jax.scipy.special.erf(values * 0.7071067811865476))


def gelu_slope(values):
    return (
        0.5 * (1.0 + jax.scipy.special.erf(values * 0.7071067811865476))
        + values * jnp.exp(-0.5 * values * values) * 0.3989422804014327
    )


def expert_rows(inputs, upstream, lift_weight, drop_weight):
    preact = jnp.einsum("ned,efd->nef", inputs, lift_weight, preferred_element_type=jnp.float32)
    activated = gelu_value(preact).astype(jnp.bfloat16)
    activated_grad = jnp.einsum(
        "ned,efd->nef", upstream, drop_weight, preferred_element_type=jnp.float32
    )
    preact_grad = (activated_grad * gelu_slope(preact)).astype(jnp.bfloat16)
    drop_sum = jnp.einsum("nef,ned->efd", activated, upstream, preferred_element_type=jnp.float32)
    lift_sum = jnp.einsum("nef,ned->efd", preact_grad, inputs, preferred_element_type=jnp.float32)
    backward = jnp.einsum(
        "nef,efd->ned", preact_grad, lift_weight, preferred_element_type=jnp.float32
    )
    return (lift_sum, drop_sum, backward)


def shards(tokens, cotangent, slot_outputs, slot_params, lift_weight, drop_weight):
    highest_precision_mode = lax.Precision.HIGHEST
    logits = jnp.einsum("bpd,ds->bps", tokens, slot_params, preferred_element_type=jnp.float32)
    dispatch = jax.nn.softmax(logits, axis=1)
    combine_weight_rows = jax.nn.softmax(logits, axis=2)
    dispatch_half = dispatch.astype(jnp.bfloat16)
    combine_half = combine_weight_rows.astype(jnp.bfloat16)
    slot_input_rows = jnp.einsum(
        "bps,bpd->bsd", dispatch_half, tokens, preferred_element_type=jnp.float32
    ).astype(jnp.bfloat16)
    slot_upstream = jnp.einsum(
        "bps,bpd->bsd", combine_half, cotangent, preferred_element_type=jnp.float32
    ).astype(jnp.bfloat16)
    combine_grad = jnp.einsum(
        "bpd,bsd->bps", cotangent, slot_outputs, preferred_element_type=jnp.float32
    )
    stacked = jnp.stack([slot_input_rows, slot_upstream])
    routed = lax.all_to_all(stacked, "expert", split_axis=2, concat_axis=1, tiled=True)
    gathered = lax.all_gather(routed, "dp", axis=1, tiled=True)
    lift_sum, drop_sum, partial_value = expert_rows(
        gathered[0], gathered[1], lift_weight, drop_weight
    )
    reduced = lax.psum_scatter(
        partial_value.astype(jnp.bfloat16), "dp", scatter_dimension=0, tiled=True
    )
    slot_grad = lax.all_to_all(reduced, "expert", split_axis=0, concat_axis=1, tiled=True)
    dispatch_grad = jnp.einsum(
        "bpd,bsd->bps", tokens, slot_grad, preferred_element_type=jnp.float32
    )
    logits_gradient = combine_weight_rows * (
        combine_grad - jnp.sum(combine_grad * combine_weight_rows, axis=2, keepdims=True)
    )
    logits_gradient = logits_gradient + dispatch * (
        dispatch_grad - jnp.sum(dispatch_grad * dispatch, axis=1, keepdims=True)
    )
    local_params = jnp.einsum(
        "bpd,bps->ds", tokens.astype(jnp.float32), logits_gradient, precision=highest_precision_mode
    )
    param_grad = lax.psum(local_params, ("dp", "expert"))
    token_grad = jnp.einsum(
        "bps,bsd->bpd", dispatch_half, slot_grad, preferred_element_type=jnp.float32
    )
    token_grad = token_grad + jnp.einsum(
        "bps,ds->bpd",
        logits_gradient,
        slot_params.astype(jnp.float32),
        precision=highest_precision_mode,
    )
    return (
        token_grad.astype(jnp.bfloat16),
        param_grad,
        lift_sum.astype(jnp.bfloat16),
        drop_sum.astype(jnp.bfloat16),
    )


def solution(mesh):
    placed = (
        P(("dp", "expert"), None, None),
        P(("dp", "expert"), None, None),
        P(("dp", "expert"), None, None),
        P(),
        P("expert", "dp", None),
        P("expert", "dp", None),
    )
    return jax.shard_map(
        shards,
        mesh=mesh,
        in_specs=placed,
        out_specs=(
            P(("dp", "expert"), None, None),
            P(),
            P("expert", "dp", None),
            P("expert", "dp", None),
        ),
        check_vma=False,
    )
```

profile of v0, /device:TPU:1, one launch (start us, length us, event | category | flops | bytes accessed | tf_op | source)
XLA Modules:
  0.0 526.5 jit_solution(3059643035178187676)
XLA Ops:
  7.2 0.0 all-gather.3.cloned.1.call-start
  7.2 1.0 copy-done
  8.3 1.2 fusion.49
  9.5 0.2 fusion.39
  9.7 0.3 fusion.5
  10.0 0.2 fusion.6
  10.2 0.1 copy.15
  10.3 20.0 %all_to_all.21 = bf16[2,1,16,1408]{3,0,1,2:T(2,128)(2,1)S(1)} all-to-all(bf16[2,1,16,1408]{3,0,1,2:T(2,128)(2,1)S(1)} %copy.15), channel_id=1, replica_groups=mesh['dp'=32,'expert'=16] {'expert'}, dimensions={2} | all-to-all | bytes 180224 | tf_op jit(solution)/shard_map/all_to_all | solution.py:50
  30.3 0.6 copy.16
  30.9 0.0 reduce-scatter.2.cloned.1.call-start
  31.0 85.7 %all-gather.3.cloned.1.call-done = bf16[2,1,512,1408]{3,2,1,0:T(8,128)(2,1)} async-done(((bf16[2,1,16,1408]{3,2,1,0:T(8,128)(2,1)}), bf16[2,1,512,1408]{3,2,1,0:T(8,128)(2,1)}) %all-gather.3.cloned.1.call-update) | async-done | bytes 2883600 | tf_op jit(solution)/shard_map/all_gather | solution.py:51
  116.7 2.1 fusion.9
  118.8 0.1 copy-done.5
  118.9 0.7 fusion.13
  119.6 1.7 fusion
  121.3 2.7 fusion.4
  124.0 112.8 %reduce-scatter.2.cloned.1.call-done = bf16[16,1,1408]{2,0,1:T(8,128)(2,1)} async-done(((bf16[512,1,1408]{2,0,1:T(8,128)(2,1)}), bf16[16,1,1408]{2,0,1:T(8,128)(2,1)}) %reduce-scatter.2.cloned.1.call-update) | async-done | bytes 45072 | tf_op jit(solution)/shard_map/reduce_scatter | solution.py:55
  236.8 0.5 broadcast.48
  237.3 1.4 reduce.12
  238.8 0.7 reshape.150
  239.5 7.2 %all-to-all-start.1 = ((bf16[16,2,704]{2,1,0:T(2,128)(2,1)}), bf16[16,2,704]{2,1,0:T(2,128)(2,1)S(1)}, u32[]{:S(2)}, u32[]{:S(2)}) async-start(bf16[16,2,704]{2,1,0:T(2,128)(2,1)} %reshape.150), calls=%async_computation.2 | async-start | bytes 98304 | tf_op jit(solution)/shard_map/all_to_all | solution.py:58
  246.7 0.0 all-reduce.2.cloned.1.call-start
  246.8 2.6 fusion.3
  249.4 5.1 all-to-all-done.1
  254.5 0.1 reshape.151
  254.6 0.3 convolution_bitcast_fusion.1
  254.8 0.5 fusion.33
  255.4 0.3 multiply_reduce_fusion.1
  255.7 1.1 convolution_bitcast_fusion
  256.9 1.7 fusion.2
  258.6 259.8 %all-reduce.2.cloned.1.call-done = f32[1408,16]{0,1:T(8,128)} async-done(((f32[1408,16]{0,1:T(8,128)}), f32[1408,16]{0,1:T(8,128)}) %all-reduce.2.cloned.1.call-update) | async-done | bytes 90128 | tf_op jit(solution)/shard_map/psum | solution.py:71
  518.4 1.5 copy.29
  (16 shorter events, 0.1 us)
Async XLA Ops:
  7.2 1.1 copy-start
  7.2 2.8 copy-start.1
  7.2 109.5 %copy-start.2 = (bf16[1,192,1408]{2,1,0:T(8,128)(2,1)S(1)}, bf16[1,192,1408]{2,1,0:T(8,128)(2,1)}, u32[]{:S(2)}) copy-start(bf16[1,192,1408]{2,1,0:T(8,128)(2,1)} %param.10) | copy-start | bytes 1622020
  7.2 109.5 %all-gather.3.cloned.1.call-start = ((), (), s32[]{:S(2)}) async-start(), calls=%async_computation.5 | async-start | bytes 2973696 | tf_op jit(solution)/shard_map/all_gather | solution.py:51
  10.2 108.6 %copy-start.6 = (bf16[1,192,1408]{2,1,0:T(8,128)(2,1)S(1)}, bf16[1,192,1408]{2,1,0:T(8,128)(2,1)}, u32[]{:S(2)}) copy-start(bf16[1,192,1408]{2,1,0:T(8,128)(2,1)} %param.11) | copy-start | bytes 1622020
  30.9 205.9 %reduce-scatter.2.cloned.1.call-start = ((), (), s32[]{:S(2)}) async-start(), calls=%async_computation.3 | async-start | bytes 1486848 | tf_op jit(solution)/shard_map/reduce_scatter | solution.py:55
  116.7 2.2 copy-start.5
  239.5 15.0 %all-to-all-start.1 = ((bf16[16,2,704]{2,1,0:T(2,128)(2,1)}), bf16[16,2,704]{2,1,0:T(2,128)(2,1)S(1)}, u32[]{:S(2)}, u32[]{:S(2)}) async-start(bf16[16,2,704]{2,1,0:T(2,128)(2,1)} %reshape.150), calls=%async_computation.2 | async-start | bytes 98304 | tf_op jit(solution)/shard_map/all_to_all | solution.py:58
  246.7 271.7 %all-reduce.2.cloned.1.call-start = ((), (), s32[]{:S(2)}) async-start(), calls=%async_computation.4 | async-start | bytes 180224 | tf_op jit(solution)/shard_map/psum | solution.py:71
  249.4 6.0 %copy-start.4 = (bf16[1,16,1408]{2,1,0:T(8,128)(2,1)S(1)}, bf16[1,16,1408]{2,1,0:T(8,128)(2,1)}, u32[]{:S(2)}) copy-start(bf16[1,16,1408]{2,1,0:T(8,128)(2,1)} %param.8) | copy-start | bytes 135172
  254.8 2.0 copy-start.3
Sparse Core Ops, SparseCore 0:
  31.1 85.5 all-gather.2
  121.5 115.3 reduce-scatter.1
  257.0 261.4 all-reduce.1
where the time goes:
time: 527 us; the launch traced here: 526 us
  waiting for transfers between devices  463 us (88%)
  blocking collectives  20 us (4%)
  matrix products  15.4 us (3%)
  between operations  13.9 us (3%)
  starting transfers between devices  7.32 us (1%)
    psum x1, waiting for transfers between devices, shards(): param_grad = lax.psum(local_params, ('dp', 'expert'))  260 us
    reduce_scatter x1, waiting for transfers between devices, shards(): lax.psum_scatter(partial_value.astype(jnp.bfloat16), 'dp', scatter_dimens...  113 us
    all_gather x1, waiting for transfers between devices, shards(): gathered = lax.all_gather(routed, 'dp', axis=1, tiled=True)  85.7 us
    all_to_all x1, blocking collectives, shards(): lax.all_to_all(stacked, 'expert', split_axis=2, concat_axis=1, tiled=True)  20 us
  transfers between devices with their start and end apart: 4, of which 4 were waited for; matrix products, arithmetic and copies ran while one was open for 1% of the time, Pallas kernels for 0%

commit v1 on v0

v1 whole, which is shorter than its diff:
```python
import jax
import jax.numpy as jnp
from jax import lax
from jax.sharding import Mesh, PartitionSpec as P

AXES = ("xhi", "y", "core", "z", "xlo")
DP = ("xhi", "y", "core")
EXPERT = ("z", "xlo")
HIDDEN = ("y", "z", "xlo")
SWAP = [(0, 1), (1, 0)]
BF16 = jnp.bfloat16
F32 = jnp.float32


def gelu_value(values):
    return 0.5 * values * (1.0 + jax.scipy.special.erf(values * 0.7071067811865476))


def gelu_slope(values):
    return (
        0.5 * (1.0 + jax.scipy.special.erf(values * 0.7071067811865476))
        + values * jnp.exp(-0.5 * values * values) * 0.3989422804014327
    )


def mm(spec, a, b):
    return jnp.einsum(spec, a, b, preferred_element_type=F32)


def fold(rows):
    head = rows[:, :768]
    tail = jnp.pad(rows[:, 768:], ((0, 0), (0, 128)))
    return jnp.stack([head, tail], axis=1)


def unfold(blocks):
    return jnp.concatenate([blocks[:, 0, :], blocks[:, 1, :640]], axis=1)


def exchange(blocks, axes):
    return lax.all_to_all(blocks, axes, split_axis=0, concat_axis=0, tiled=True)


def split_float(values):
    high = values.astype(BF16)
    return high, (values - high.astype(F32)).astype(BF16)


def shards(tokens, cotangent, slot_outputs, slot_params, lift_weight, drop_weight):
    tokens, cotangent, slot_outputs = tokens[0], cotangent[0], slot_outputs[0]
    own = jnp.concatenate([lift_weight[0], drop_weight[0]], axis=0)
    over_x = lax.ppermute(own, "xhi", SWAP)
    over_core = lax.ppermute(own, "core", SWAP)
    over_both = lax.ppermute(over_x, "core", SWAP)

    params_t = slot_params.T
    logits = mm("sd,pd->sp", params_t, tokens)
    dispatch = jax.nn.softmax(logits, axis=1)
    combine = jax.nn.softmax(logits, axis=0)
    dispatch_half = dispatch.astype(BF16)
    slot_inputs = mm("sp,pd->sd", dispatch_half, tokens).astype(BF16)
    slot_upstream = mm("sp,pd->sd", combine.astype(BF16), cotangent).astype(BF16)
    sent = jnp.stack([slot_inputs, slot_upstream], axis=1)
    sent = jnp.broadcast_to(sent[None], (8, 16, 2, 1408)).reshape(128, 2, 1408)
    routed = exchange(sent, HIDDEN)
    inputs, upstream = routed[:, 0, :], routed[:, 1, :]

    combine_grad = mm("sd,pd->sp", slot_outputs, cotangent)
    combine_part = combine * (
        combine_grad - jnp.sum(combine_grad * combine, axis=0, keepdims=True)
    )

    hidden = []
    backward = None
    for block in (own, over_x, over_core, over_both):
        lift, drop = block[:192], block[192:]
        preact = mm("nd,fd->nf", inputs, lift)
        activated_grad = mm("nd,fd->nf", upstream, drop)
        activated = gelu_value(preact).astype(BF16)
        preact_grad = (activated_grad * gelu_slope(preact)).astype(BF16)
        hidden.append((activated, preact_grad))
        part = mm("nf,fd->nd", preact_grad, lift)
        backward = part if backward is None else backward + part
    returned = exchange(fold(backward.astype(BF16)), HIDDEN)
    slot_grad = jnp.sum(returned.astype(F32).reshape(8, 16, 2, 768), axis=0)
    slot_grad = unfold(slot_grad.astype(BF16))

    sums = [
        jnp.concatenate(
            [mm("nf,nd->fd", preact_grad, inputs), mm("nf,nd->fd", activated, upstream)], axis=0
        )
        for activated, preact_grad in hidden
    ]
    from_core = lax.ppermute(
        jnp.concatenate([sums[2], sums[3]], axis=0).astype(BF16), "core", SWAP
    ).astype(F32)
    from_x = lax.ppermute((sums[1] + from_core[384:]).astype(BF16), "xhi", SWAP)
    weight_grads = (sums[0] + from_core[:384] + from_x.astype(F32)).astype(BF16)

    dispatch_grad = mm("sd,pd->sp", slot_grad, tokens)
    logit_grad = combine_part + dispatch * (
        dispatch_grad - jnp.sum(dispatch_grad * dispatch, axis=1, keepdims=True)
    )
    high, low = split_float(logit_grad)
    local = mm("sp,pd->sd", jnp.concatenate([high, low], axis=0), tokens)
    local = local[:16] + local[16:]
    by_slot = exchange(fold(local.astype(BF16)), EXPERT)
    by_slot = jnp.sum(by_slot.astype(F32), axis=0).astype(BF16)
    by_group = exchange(jnp.broadcast_to(by_slot[None], (32, 2, 768)), DP)
    total = jnp.sum(by_group.astype(F32), axis=0).astype(BF16)
    columns = exchange(jnp.broadcast_to(total[None], (16, 2, 768)), EXPERT)
    param_grad = unfold(columns).astype(F32).T

    token_grad = mm(
        "kp,kd->pd",
        jnp.concatenate([dispatch_half, high, low], axis=0),
        jnp.concatenate([slot_grad, params_t, params_t], axis=0),
    ).astype(BF16)
    return (token_grad[None], param_grad, weight_grads[None, :192], weight_grads[None, 192:])


def solution(mesh):
    split = Mesh(mesh.devices.reshape(2, 8, 2, 8, 2), AXES)
    images = P(AXES, None, None)
    hidden = P(EXPERT, DP, None)
    return jax.shard_map(
        shards,
        mesh=split,
        in_specs=(images, images, images, P(), hidden, hidden),
        out_specs=(images, P(), hidden, hidden),
        check_vma=False,
    )
```

time: 527 us -> 183 us (0.35)
  waiting for transfers between devices: 463 us -> 51.5 us
  starting transfers between devices: 7.32 us -> 60.8 us
  between operations: 13.9 us -> 1.2 us
  other arithmetic: 1.66 us -> 12.3 us
  matrix products: 15.4 us -> 24.3 us
    psum x1 -> x0, waiting for transfers between devices: 260 us -> none  [shards(): param_grad = lax.psum(local_params, ('dp', 'expert'))]
    reduce_scatter x1 -> x0, waiting for transfers between devices: 113 us -> none  [shards(): lax.psum_scatter(partial_value.astype(jnp.bfloat16), 'dp', scatter_dimens...]
    all_gather x1 -> x0, waiting for transfers between devices: 85.7 us -> none  [shards(): gathered = lax.all_gather(routed, 'dp', axis=1, tiled=True)]
    all_to_all x1 -> x4, starting transfers between devices: 7.2 us -> 43.8 us  [exchange(): return lax.all_to_all(blocks, axes, split_axis=0, concat_axis=0, tiled=True)]
    ppermute x0 -> x5, waiting for transfers between devices: none -> 27.6 us  [the longest x1 27.6 us: shards(): over_x = lax.ppermute(own, 'xhi', SWAP)]
    all_to_all x1 -> x4, waiting for transfers between devices: 5.05 us -> 23.9 us  [exchange(): return lax.all_to_all(blocks, axes, split_axis=0, concat_axis=0, tiled=True)]
    ppermute x0 -> x5, starting transfers between devices: none -> 17.1 us  [the longest x1 4.35 us: shards(): over_x = lax.ppermute(own, 'xhi', SWAP)]
    dot_general x13 -> x27, matrix products: 15.4 us -> 24.3 us  [mm(): return jnp.einsum(spec, a, b, preferred_element_type=F32)]
  transfers between devices with their start and end apart: 4 -> 9, of which waited for: 4 -> 4; matrix products, arithmetic and copies ran while one was open for 1% -> 14% of each run, Pallas kernels for 0% -> 0%
where the time goes in v1:
time: 183 us; the launch traced here: 182 us
  starting transfers between devices  60.8 us (33%)
  waiting for transfers between devices  51.5 us (28%)
  matrix products  24.3 us (13%)
  blocking collectives  23.2 us (13%)
  other arithmetic  12.3 us (7%)
  local copies, waits for them, and re-layouts  8.65 us (5%)
    all_to_all x4, starting transfers between devices, exchange(): return lax.all_to_all(blocks, axes, split_axis=0, concat_axis=0, tiled=True)  43.8 us
    ppermute x1, waiting for transfers between devices, shards(): over_x = lax.ppermute(own, 'xhi', SWAP)  27.6 us
    dot_general x27, matrix products, mm(): return jnp.einsum(spec, a, b, preferred_element_type=F32)  24.3 us
    all_to_all x4, waiting for transfers between devices, exchange(): return lax.all_to_all(blocks, axes, split_axis=0, concat_axis=0, tiled=True)  23.9 us
    all_to_all x1, blocking collectives, exchange(): return lax.all_to_all(blocks, axes, split_axis=0, concat_axis=0, tiled=True)  23.2 us
    ppermute x1, starting transfers between devices, shards(): over_x = lax.ppermute(own, 'xhi', SWAP)  4.35 us
    ppermute x1, starting transfers between devices, shards(): from_x = lax.ppermute((sums[1] + from_core[384:]).astype(BF16), 'xhi', SWAP)  4 us
  transfers between devices with their start and end apart: 9, of which 4 were waited for; matrix products, arithmetic and copies ran while one was open for 14% of the time, Pallas kernels for 0%

profile of v1, /device:TPU:1, one launch (start us, length us, event | category | flops | bytes accessed | tf_op | source)
XLA Modules:
  0.0 182.0 jit_solution(4730470791597563070)
XLA Ops:
  4.2 1.2 broadcast_in_dim.12
  5.5 19.3 %all-to-all-start = ((bf16[128,2,1408]{2,1,0:T(2,128)(2,1)}), bf16[128,2,1408]{2,1,0:T(2,128)(2,1)S(1)}, u32[]{:S(2)}, u32[]{:S(2)}) async-start(bf16[128,2,1408]{2,1,0:T(2,128)(2,1)} %bitcast.5), calls=%async_computation | async-start | bytes 1441792 | tf_op jit(solution)/shard_map/all_to_all | solution.py:41
  25.8 4.3 %collective-permute-start = (bf16[384,1408]{1,0:T(8,128)(2,1)}, bf16[384,1408]{1,0:T(8,128)(2,1)}, u32[]{:S(2)}, u32[]{:S(2)}) collective-permute-start(bf16[384,1408]{1,0:T(8,128)(2,1)} %pad_maximum_fusion.1), channel_id=1, source_target_pairs={{0,256},{256,0},{1,257},{257,1},{2,258},{258,2},{3,259},{259,3},{4... | collective-permute-start | bytes 3244040 | tf_op jit(solution)/shard_map/ppermute | solution.py:52
  30.2 3.1 %collective-permute-start.1 = (bf16[384,1408]{1,0:T(8,128)(2,1)}, bf16[384,1408]{1,0:T(8,128)(2,1)}, u32[]{:S(2)}, u32[]{:S(2)}) collective-permute-start(bf16[384,1408]{1,0:T(8,128)(2,1)} %pad_maximum_fusion.1), channel_id=1, source_target_pairs={{0,16},{16,0},{1,17},{17,1},{2,18},{18,2},{3,19},{19,3},{4,20},{20... | collective-permute-start | bytes 3244040 | tf_op jit(solution)/shard_map/ppermute | solution.py:53
  33.4 27.6 %collective-permute-done = bf16[384,1408]{1,0:T(8,128)(2,1)} collective-permute-done((bf16[384,1408]{1,0:T(8,128)(2,1)}, bf16[384,1408]{1,0:T(8,128)(2,1)}, u32[]{:S(2)}, u32[]{:S(2)}) %collective-permute-start) | collective-permute-done | bytes 1081376 | tf_op jit(solution)/shard_map/ppermute | solution.py:52
  61.0 3.2 %collective-permute-start.2 = (bf16[384,1408]{1,0:T(8,128)(2,1)}, bf16[384,1408]{1,0:T(8,128)(2,1)}, u32[]{:S(2)}, u32[]{:S(2)}) collective-permute-start(bf16[384,1408]{1,0:T(8,128)(2,1)} %collective-permute-done), channel_id=1, source_target_pairs={{0,16},{16,0},{1,17},{17,1},{2,18},{18,2},{3,19},{19,3},{4,20},{20... | collective-permute-start | bytes 3244040 | tf_op jit(solution)/shard_map/ppermute | solution.py:54
  65.9 1.4 fusion.28
  67.6 1.4 fusion.31
  69.0 1.4 fusion.9
  71.5 1.4 fusion.8
  73.1 1.3 convolution_add_fusion.2
  74.5 1.3 convolution_add_fusion.1
  75.8 1.4 fusion.25
  77.2 1.4 fusion.10
  78.5 1.3 fusion.1
  83.4 12.9 %all-to-all-start.1 = ((bf16[128,2,768]{2,1,0:T(2,128)(2,1)}), bf16[128,2,768]{2,1,0:T(2,128)(2,1)}, u32[]{:S(2)}, u32[]{:S(2)}) async-start(bf16[128,2,768]{2,1,0:T(2,128)(2,1)} %copy.47), calls=%async_computation.1 | async-start | bytes 786432 | tf_op jit(solution)/shard_map/all_to_all | solution.py:41
  96.3 2.7 %pad_maximum_fusion = bf16[768,1408]{1,0:T(8,128)(2,1)} fusion(bf16[192,1408]{1,0:T(8,128)(2,1)} %convolution_convert_fusion.1, bf16[192,1408]{1,0:T(8,128)(2,1)} %convolution_convert_fusion.2, bf16[192,1408]{1,0:T(8,128)(2,1)S(1)} %convolution_convert_fusion.3, bf16[192,1408]{1,0:T(8,128)(2,1)S(1)} %copy-done.5), kind=kLoop, calls=%fused_computation.19 | loop fusion | flops 8650752 | bytes 4325376 | tf_op jit(solution)/shard_map/concatenate | solution.py:95
  99.0 2.4 %collective-permute-start.3 = (bf16[768,1408]{1,0:T(8,128)(2,1)}, bf16[768,1408]{1,0:T(8,128)(2,1)}, u32[]{:S(2)}, u32[]{:S(2)}) collective-permute-start(bf16[768,1408]{1,0:T(8,128)(2,1)} %pad_maximum_fusion), channel_id=1, source_target_pairs={{0,16},{16,0},{1,17},{17,1},{2,18},{18,2},{3,19},{19,3},{4,20},{20... | collective-permute-start | bytes 6488072 | tf_op jit(solution)/shard_map/ppermute | solution.py:94
  101.7 1.3 fusion.58
  103.0 9.0 %all-to-all-done.1 = bf16[128,2,768]{2,1,0:T(2,128)(2,1)} async-done(((bf16[128,2,768]{2,1,0:T(2,128)(2,1)}), bf16[128,2,768]{2,1,0:T(2,128)(2,1)}, u32[]{:S(2)}, u32[]{:S(2)}) %all-to-all-start.1) | async-done | bytes 393248 | tf_op jit(solution)/shard_map/all_to_all | solution.py:41
  112.0 1.4 reduce.2
  115.3 2.0 %convert_element_type.98 = f32[768,1408]{1,0:T(8,128)S(1)} convert(bf16[768,1408]{1,0:T(8,128)(2,1)} %collective-permute-done.3) | non-fusion elementwise | flops 1081344 | bytes 6488064 | tf_op jit(solution)/shard_map/convert_element_type | solution.py:96
  117.3 1.4 fusion.4
  119.6 4.0 %collective-permute-start.4 = (bf16[384,1408]{1,0:T(8,128)(2,1)}, bf16[384,1408]{1,0:T(8,128)(2,1)}, u32[]{:S(2)}, u32[]{:S(2)}) collective-permute-start(bf16[384,1408]{1,0:T(8,128)(2,1)} %fusion.4), channel_id=1, source_target_pairs={{0,256},{256,0},{1,257},{257,1},{2,258},{258,2},{3,259},{259,3},{4... | collective-permute-start | bytes 3244040 | tf_op jit(solution)/shard_map/ppermute | solution.py:97
  123.7 23.2 %all_to_all.25 = bf16[16,2,768]{2,1,0:T(2,128)(2,1)S(1)} all-to-all(bf16[16,2,768]{2,1,0:T(2,128)(2,1)S(1)} %copy.48), channel_id=1, replica_groups=mesh['xhi'=2,'y'=8,'core'=2,'z'=8,'xlo'=2] {'z','xlo'}, dimensions={0} | all-to-all | bytes 98304 | tf_op jit(solution)/shard_map/all_to_all | solution.py:41
  147.6 8.1 %all-to-all-start.3 = ((bf16[32,2,768]{2,1,0:T(2,128)(2,1)}), bf16[32,2,768]{2,1,0:T(2,128)(2,1)S(1)}, u32[]{:S(2)}, u32[]{:S(2)}) async-start(bf16[32,2,768]{2,1,0:T(2,128)(2,1)} %broadcast_in_dim.14), calls=%async_computation.3 | async-start | bytes 196608 | tf_op jit(solution)/shard_map/all_to_all | solution.py:41
  156.1 9.6 %all-to-all-done.3 = bf16[32,2,768]{2,1,0:T(2,128)(2,1)S(1)} async-done(((bf16[32,2,768]{2,1,0:T(2,128)(2,1)}), bf16[32,2,768]{2,1,0:T(2,128)(2,1)S(1)}, u32[]{:S(2)}, u32[]{:S(2)}) %all-to-all-start.3) | async-done | bytes 98336 | tf_op jit(solution)/shard_map/all_to_all | solution.py:41
  166.5 3.5 %all-to-all-start.4 = ((bf16[16,2,768]{2,1,0:T(2,128)(2,1)}), bf16[16,2,768]{2,1,0:T(2,128)(2,1)S(1)}, u32[]{:S(2)}, u32[]{:S(2)}) async-start(bf16[16,2,768]{2,1,0:T(2,128)(2,1)} %broadcast_in_dim.15), calls=%async_computation.4 | async-start | bytes 98304 | tf_op jit(solution)/shard_map/all_to_all | solution.py:41
  170.0 1.3 fusion.96
  171.3 1.2 fusion
  172.5 5.2 %all-to-all-done.4 = bf16[16,2,768]{2,1,0:T(2,128)(2,1)S(1)} async-done(((bf16[16,2,768]{2,1,0:T(2,128)(2,1)}), bf16[16,2,768]{2,1,0:T(2,128)(2,1)S(1)}, u32[]{:S(2)}, u32[]{:S(2)}) %all-to-all-start.4) | async-done | bytes 49184 | tf_op jit(solution)/shard_map/all_to_all | solution.py:41
  178.4 2.5 %fusion.6 = bf16[384,1408]{1,0:T(8,128)(2,1)S(1)} fusion(f32[768,1408]{1,0:T(8,128)} %copy-done.1, f32[192,1408]{1,0:T(8,128)S(1)} %fusion.57, f32[192,1408]{1,0:T(8,128)} %fusion.96, bf16[384,1408]{1,0:T(8,128)(2,1)} %collective-permute-done.4), kind=kLoop, calls=%fused_computation.18 | loop fusion | flops 2703360 | bytes 6488064 | tf_op jit(solution)/shard_map/convert_element_type | solution.py:98
  (89 shorter events, 18.0 us)
Async XLA Ops:
  0.6 1.1 copy-start
  0.6 3.2 %copy-start.4 = (bf16[1,256,1408]{2,1,0:T(8,128)(2,1)S(1)}, bf16[1,256,1408]{2,1,0:T(8,128)(2,1)}, u32[]{:S(2)}) copy-start(bf16[1,256,1408]{2,1,0:T(8,128)(2,1)} %param.7) | copy-start | bytes 2162692
  3.0 0.5 copy-start.11
  3.0 0.5 copy-start.15
  3.2 0.6 copy-start.13
  3.2 0.6 copy-start.17
  3.3 0.6 copy-start.8
  4.2 20.6 %copy-start.2 = (bf16[1,192,1408]{2,1,0:T(8,128)(2,1)S(1)}, bf16[1,192,1408]{2,1,0:T(8,128)(2,1)}, u32[]{:S(2)}) copy-start(bf16[1,192,1408]{2,1,0:T(8,128)(2,1)} %param.10) | copy-start | bytes 1622020
  4.2 20.5 %copy-start.6 = (bf16[1,192,1408]{2,1,0:T(8,128)(2,1)S(1)}, bf16[1,192,1408]{2,1,0:T(8,128)(2,1)}, u32[]{:S(2)}) copy-start(bf16[1,192,1408]{2,1,0:T(8,128)(2,1)} %param.11) | copy-start | bytes 1622020
  5.5 58.7 %all-to-all-start = ((bf16[128,2,1408]{2,1,0:T(2,128)(2,1)}), bf16[128,2,1408]{2,1,0:T(2,128)(2,1)S(1)}, u32[]{:S(2)}, u32[]{:S(2)}) async-start(bf16[128,2,1408]{2,1,0:T(2,128)(2,1)} %bitcast.5), calls=%async_computation | async-start | bytes 1441792 | tf_op jit(solution)/shard_map/all_to_all | solution.py:41
  25.8 35.1 %collective-permute-start = (bf16[384,1408]{1,0:T(8,128)(2,1)}, bf16[384,1408]{1,0:T(8,128)(2,1)}, u32[]{:S(2)}, u32[]{:S(2)}) collective-permute-start(bf16[384,1408]{1,0:T(8,128)(2,1)} %pad_maximum_fusion.1), channel_id=1, source_target_pairs={{0,256},{256,0},{1,257},{257,1},{2,258},{258,2},{3,259},{259,3},{4... | collective-permute-start | bytes 3244040 | tf_op jit(solution)/shard_map/ppermute | solution.py:52
  30.2 35.7 %collective-permute-start.1 = (bf16[384,1408]{1,0:T(8,128)(2,1)}, bf16[384,1408]{1,0:T(8,128)(2,1)}, u32[]{:S(2)}, u32[]{:S(2)}) collective-permute-start(bf16[384,1408]{1,0:T(8,128)(2,1)} %pad_maximum_fusion.1), channel_id=1, source_target_pairs={{0,16},{16,0},{1,17},{17,1},{2,18},{18,2},{3,19},{19,3},{4,20},{20... | collective-permute-start | bytes 3244040 | tf_op jit(solution)/shard_map/ppermute | solution.py:53
  61.0 14.8 %collective-permute-start.2 = (bf16[384,1408]{1,0:T(8,128)(2,1)}, bf16[384,1408]{1,0:T(8,128)(2,1)}, u32[]{:S(2)}, u32[]{:S(2)}) collective-permute-start(bf16[384,1408]{1,0:T(8,128)(2,1)} %collective-permute-done), channel_id=1, source_target_pairs={{0,16},{16,0},{1,17},{17,1},{2,18},{18,2},{3,19},{19,3},{4,20},{20... | collective-permute-start | bytes 3244040 | tf_op jit(solution)/shard_map/ppermute | solution.py:54
  82.2 14.1 %copy-start.5 = (bf16[192,1408]{1,0:T(8,128)(2,1)S(1)}, bf16[192,1408]{1,0:T(8,128)(2,1)}, u32[]{:S(2)}) copy-start(bf16[192,1408]{1,0:T(8,128)(2,1)} %convolution_convert_fusion.4) | copy-start | bytes 1622020
  83.4 28.6 %all-to-all-start.1 = ((bf16[128,2,768]{2,1,0:T(2,128)(2,1)}), bf16[128,2,768]{2,1,0:T(2,128)(2,1)}, u32[]{:S(2)}, u32[]{:S(2)}) async-start(bf16[128,2,768]{2,1,0:T(2,128)(2,1)} %copy.47), calls=%async_computation.1 | async-start | bytes 786432 | tf_op jit(solution)/shard_map/all_to_all | solution.py:41
  99.0 16.3 %collective-permute-start.3 = (bf16[768,1408]{1,0:T(8,128)(2,1)}, bf16[768,1408]{1,0:T(8,128)(2,1)}, u32[]{:S(2)}, u32[]{:S(2)}) collective-permute-start(bf16[768,1408]{1,0:T(8,128)(2,1)} %pad_maximum_fusion), channel_id=1, source_target_pairs={{0,16},{16,0},{1,17},{17,1},{2,18},{18,2},{3,19},{19,3},{4,20},{20... | collective-permute-start | bytes 6488072 | tf_op jit(solution)/shard_map/ppermute | solution.py:94
  103.0 10.8 %copy-start.10 = (bf16[1,16,1408]{2,1,0:T(8,128)(2,1)S(1)}, bf16[1,16,1408]{2,1,0:T(8,128)(2,1)}, u32[]{:S(2)}) copy-start(bf16[1,16,1408]{2,1,0:T(8,128)(2,1)} %param.8) | copy-start | bytes 135172
  103.0 10.8 %copy-start.12 = (f32[256]{0:T(256)S(1)}, f32[256]{0:T(256)}, u32[]{:S(2)}) copy-start(f32[256]{0:T(256)} %copy-done.11) | copy-start | bytes 3076
  103.0 10.8 %copy-start.14 = (f32[256]{0:T(256)S(1)}, f32[256]{0:T(256)}, u32[]{:S(2)}) copy-start(f32[256]{0:T(256)} %copy-done.13) | copy-start | bytes 3076
  113.4 1.5 copy-start.16
  113.4 1.5 copy-start.18
  115.3 2.0 %copy-start.3 = (f32[192,1408]{1,0:T(8,128)S(1)}, f32[192,1408]{1,0:T(8,128)}, u32[]{:S(2)}) copy-start(f32[192,1408]{1,0:T(8,128)} %fusion.58) | copy-start | bytes 3244036
  117.3 2.3 %copy-start.1 = (f32[768,1408]{1,0:T(8,128)}, f32[768,1408]{1,0:T(8,128)S(1)}, u32[]{:S(2)}) copy-start(f32[768,1408]{1,0:T(8,128)S(1)} %convert_element_type.98) | copy-start | bytes 12976132
  119.6 58.8 %collective-permute-start.4 = (bf16[384,1408]{1,0:T(8,128)(2,1)}, bf16[384,1408]{1,0:T(8,128)(2,1)}, u32[]{:S(2)}, u32[]{:S(2)}) collective-permute-start(bf16[384,1408]{1,0:T(8,128)(2,1)} %fusion.4), channel_id=1, source_target_pairs={{0,256},{256,0},{1,257},{257,1},{2,258},{258,2},{3,259},{259,3},{4... | collective-permute-start | bytes 3244040 | tf_op jit(solution)/shard_map/ppermute | solution.py:97
  147.6 18.1 %all-to-all-start.3 = ((bf16[32,2,768]{2,1,0:T(2,128)(2,1)}), bf16[32,2,768]{2,1,0:T(2,128)(2,1)S(1)}, u32[]{:S(2)}, u32[]{:S(2)}) async-start(bf16[32,2,768]{2,1,0:T(2,128)(2,1)} %broadcast_in_dim.14), calls=%async_computation.3 | async-start | bytes 196608 | tf_op jit(solution)/shard_map/all_to_all | solution.py:41
  156.1 15.2 %copy-start.7 = (bf16[1408,16]{0,1:T(8,128)(2,1)S(1)}, bf16[1408,16]{0,1:T(8,128)(2,1)}, u32[]{:S(2)}) copy-start(bf16[1408,16]{0,1:T(8,128)(2,1)} %param.9) | copy-start | bytes 135172
  156.1 15.2 %copy-start.9 = (bf16[16,256]{1,0:T(8,128)(2,1)S(1)}, bf16[16,256]{1,0:T(8,128)(2,1)}, u32[]{:S(2)}) copy-start(bf16[16,256]{1,0:T(8,128)(2,1)} %copy-done.8) | copy-start | bytes 24580
  166.5 11.3 %all-to-all-start.4 = ((bf16[16,2,768]{2,1,0:T(2,128)(2,1)}), bf16[16,2,768]{2,1,0:T(2,128)(2,1)S(1)}, u32[]{:S(2)}, u32[]{:S(2)}) async-start(bf16[16,2,768]{2,1,0:T(2,128)(2,1)} %broadcast_in_dim.15), calls=%async_computation.4 | async-start | bytes 98304 | tf_op jit(solution)/shard_map/all_to_all | solution.py:41

commit v2 on v1

v2 whole, which is shorter than its diff:
```python
import jax
import jax.numpy as jnp
from jax import lax
from jax.experimental import pallas as pl
from jax.experimental.pallas import tpu as pltpu
from jax.sharding import Mesh, PartitionSpec as P

AXES = ("xhi", "y", "core", "z", "xlo")
DP = ("xhi", "y", "core")
NEAR = ("core", "z")
FAR = ("xhi", "y", "xlo")
EXPERT = ("z", "xlo")
HIDDEN = ("y", "z", "xlo")
SWAP = [(0, 1), (1, 0)]
BF16 = jnp.bfloat16
F32 = jnp.float32


def mm(spec, a, b):
    return jnp.einsum(spec, a, b, preferred_element_type=F32)


def dot(a, b, contract):
    return lax.dot_general(a, b, (contract, ((), ())), preferred_element_type=F32)


def call(kernel, out, args, macs):
    return pl.pallas_call(
        kernel,
        out_shape=out,
        in_specs=[pl.BlockSpec(memory_space=pltpu.VMEM)] * len(args),
        out_specs=jax.tree.map(lambda _: pl.BlockSpec(memory_space=pltpu.VMEM), out),
        compiler_params=pltpu.CompilerParams(vmem_limit_bytes=40 * 2**20),
        cost_estimate=pl.CostEstimate(
            flops=2 * macs,
            bytes_accessed=sum(a.size * a.dtype.itemsize for a in list(args) + list(out)),
            transcendentals=0,
        ),
    )(*args)


def hidden_kernel(x_ref, g_ref, w0, w1, w2, w3, back_ref, act_ref, slope_ref):
    total = None
    for k, w in enumerate((w0, w1, w2, w3)):
        lift = w[:192, :]
        preact = dot(lift, x_ref[...], ((1,), (1,)))
        activated_grad = dot(w[192:, :], g_ref[...], ((1,), (1,)))
        rise = 0.5 * (1.0 + lax.erf(preact * 0.7071067811865476))
        bell = preact * jnp.exp(-0.5 * preact * preact) * 0.3989422804014327
        act_ref[pl.ds(192 * k, 192), :] = (preact * rise).astype(BF16)
        preact_grad = (activated_grad * (rise + bell)).astype(BF16)
        slope_ref[pl.ds(192 * k, 192), :] = preact_grad
        part = dot(preact_grad, lift, ((0,), (0,)))
        total = part if total is None else total + part
    back_ref[...] = total.astype(BF16)


def block_grads(k, x_ref, g_ref, act_ref, slope_ref):
    rows = pl.ds(192 * k, 192)
    lift = dot(slope_ref[rows, :], x_ref[...], ((1,), (0,)))
    drop = dot(act_ref[rows, :], g_ref[...], ((1,), (0,)))
    return lift, drop


def copy_kernel(src_ref, dst_ref):
    dst_ref[...] = src_ref[...]


def core_kernel(x_ref, g_ref, act_ref, slope_ref, out_ref):
    for k in (2, 3):
        lift, drop = block_grads(k, x_ref, g_ref, act_ref, slope_ref)
        out_ref[pl.ds(384 * (k - 2), 192), :] = lift.astype(BF16)
        out_ref[pl.ds(384 * (k - 2) + 192, 192), :] = drop.astype(BF16)


def x_kernel(x_ref, g_ref, act_ref, slope_ref, core_ref, out_ref):
    lift, drop = block_grads(1, x_ref, g_ref, act_ref, slope_ref)
    out_ref[:192, :] = (lift + core_ref[384:576, :].astype(F32)).astype(BF16)
    out_ref[192:, :] = (drop + core_ref[576:, :].astype(F32)).astype(BF16)


def own_kernel(x_ref, g_ref, act_ref, slope_ref, core_ref, over_ref, lift_ref, drop_ref):
    lift, drop = block_grads(0, x_ref, g_ref, act_ref, slope_ref)
    lift_ref[...] = (
        lift + core_ref[:192, :].astype(F32) + over_ref[:192, :].astype(F32)
    ).astype(BF16)
    drop_ref[...] = (
        drop + core_ref[192:384, :].astype(F32) + over_ref[192:, :].astype(F32)
    ).astype(BF16)


def fold(rows):
    head = rows[:, :768]
    tail = jnp.pad(rows[:, 768:], ((0, 0), (0, 128)))
    return jnp.stack([head, tail], axis=1)


def unfold(blocks):
    return jnp.concatenate([blocks[:, 0, :], blocks[:, 1, :640]], axis=1)


def exchange(blocks, axes):
    return lax.all_to_all(blocks, axes, split_axis=0, concat_axis=0, tiled=True)


def split_float(values):
    high = values.astype(BF16)
    return high, (values - high.astype(F32)).astype(BF16)


def shards(tokens, cotangent, slot_outputs, slot_params, lift_weight, drop_weight):
    tokens, cotangent, slot_outputs = tokens[0], cotangent[0], slot_outputs[0]
    own = jnp.concatenate([lift_weight[0], drop_weight[0]], axis=0)
    over_x = lax.ppermute(own, "xhi", SWAP)
    over_core = lax.ppermute(own, "core", SWAP)
    over_x = pl.pallas_call(
        copy_kernel,
        out_shape=jax.ShapeDtypeStruct((384, 1408), BF16),
        cost_estimate=pl.CostEstimate(flops=2 * 10**10, bytes_accessed=4, transcendentals=0),
    )(over_x)
    over_both = lax.ppermute(over_x, "core", SWAP)

    params_t = slot_params.T
    logits = mm("sd,pd->sp", params_t, tokens)
    dispatch = jax.nn.softmax(logits, axis=1)
    combine = jax.nn.softmax(logits, axis=0)
    dispatch_half = dispatch.astype(BF16)
    slot_inputs = mm("sp,pd->sd", dispatch_half, tokens).astype(BF16)
    slot_upstream = mm("sp,pd->sd", combine.astype(BF16), cotangent).astype(BF16)
    sent = jnp.stack([slot_inputs, slot_upstream], axis=1)
    sent = jnp.broadcast_to(sent[None], (8, 16, 2, 1408)).reshape(128, 2, 1408)
    routed = exchange(sent, HIDDEN)
    inputs, upstream = routed[:, 0, :], routed[:, 1, :]

    combine_grad = mm("sd,pd->sp", slot_outputs, cotangent)
    combine_part = combine * (
        combine_grad - jnp.sum(combine_grad * combine, axis=0, keepdims=True)
    )

    shape = jax.ShapeDtypeStruct
    units = shape((768, 128), BF16)
    backward, activated, slopes = call(
        hidden_kernel,
        (shape((128, 1408), BF16), units, units),
        (inputs, upstream, own, over_x, over_core, over_both),
        3 * 128 * 768 * 1408,
    )
    returned = exchange(fold(backward), HIDDEN)
    slot_grad = jnp.sum(returned.astype(F32).reshape(8, 16, 2, 768), axis=0)
    slot_grad = unfold(slot_grad.astype(BF16))

    rows = (inputs, upstream, activated, slopes)
    to_core = call(core_kernel, (shape((768, 1408), BF16),), rows, 4 * 192 * 128 * 1408)[0]
    from_core = lax.ppermute(to_core, "core", SWAP)
    to_x = call(
        x_kernel, (shape((384, 1408), BF16),), rows + (from_core,), 2 * 192 * 128 * 1408
    )[0]
    from_x = lax.ppermute(to_x, "xhi", SWAP)
    half = shape((192, 1408), BF16)
    lift_grad, drop_grad = call(
        own_kernel, (half, half), rows + (from_core, from_x), 2 * 192 * 128 * 1408
    )

    dispatch_grad = mm("sd,pd->sp", slot_grad, tokens)
    logit_grad = combine_part + dispatch * (
        dispatch_grad - jnp.sum(dispatch_grad * dispatch, axis=1, keepdims=True)
    )
    high, low = split_float(logit_grad)
    local = mm("sp,pd->sd", jnp.concatenate([high, low], axis=0), tokens)
    local = local[:16] + local[16:]
    by_slot = exchange(fold(local.astype(BF16)), NEAR)
    by_slot = jnp.sum(by_slot.astype(F32), axis=0).astype(BF16)
    by_group = exchange(jnp.broadcast_to(by_slot[None], (32, 2, 768)), FAR)
    total = jnp.sum(by_group.astype(F32), axis=0).astype(BF16)
    columns = exchange(jnp.broadcast_to(total[None], (16, 2, 768)), NEAR)
    param_grad = unfold(columns).astype(F32).T

    token_grad = mm(
        "kp,kd->pd",
        jnp.concatenate([dispatch_half, high, low], axis=0),
        jnp.concatenate([slot_grad, params_t, params_t], axis=0),
    ).astype(BF16)
    return (token_grad[None], param_grad, lift_grad[None], drop_grad[None])


def solution(mesh):
    split = Mesh(mesh.devices.reshape(2, 8, 2, 8, 2), AXES)
    images = P(AXES, None, None)
    hidden = P(EXPERT, DP, None)
    return jax.shard_map(
        shards,
        mesh=split,
        in_specs=(images, images, images, P(), hidden, hidden),
        out_specs=(images, P(), hidden, hidden),
        check_vma=False,
    )
```

time: 183 us -> 141 us (0.77)
  waiting for transfers between devices: 51.5 us -> 22.2 us
  blocking collectives: 23.2 us -> 48.1 us
  matrix products: 24.3 us -> 2.93 us
  starting transfers between devices: 60.8 us -> 43.7 us
  Pallas kernels: 0 us -> 14.2 us
  other arithmetic: 12.3 us -> 3.01 us
  local copies, waits for them, and re-layouts: 8.65 us -> 4.9 us
    ppermute x1, waiting for transfers between devices: 27.6 us -> 0.01 us  [shards(): over_x = lax.ppermute(own, 'xhi', SWAP)]
    all_to_all x1 -> x3, blocking collectives: 23.2 us -> 48.1 us  [exchange(): return lax.all_to_all(blocks, axes, split_axis=0, concat_axis=0, tiled=True)]
    all_to_all x4 -> x2, starting transfers between devices: 43.8 us -> 20.4 us  [exchange(): return lax.all_to_all(blocks, axes, split_axis=0, concat_axis=0, tiled=True)]
    dot_general x27 -> x7, matrix products: 24.3 us -> 2.93 us  [mm(): return jnp.einsum(spec, a, b, preferred_element_type=F32)]
    pallas_call x0 -> x5, Pallas kernels: none -> 14.2 us  [the longest x4 11.9 us: call(): pl.pallas_call(kernel, out_shape=out, in_specs=[pl.BlockSpec(memory_space...]
    convert_element_type x4 -> x1, other arithmetic: 5.89 us -> 0.01 us  [shards(): by_slot = exchange(fold(local.astype(BF16)), NEAR)]
    concatenate x1 -> x0, other arithmetic: 2.72 us -> none  [shards(): jnp.concatenate([sums[2], sums[3]], axis=0).astype(BF16)]
    ppermute x2, starting transfers between devices: 6.36 us -> 8.57 us  [the longest x1 4.44 us: shards(): from_x = lax.ppermute(to_x, 'xhi', SWAP)]
  transfers between devices with their start and end apart: 9 -> 7, of which waited for: 4 -> 2; matrix products, arithmetic and copies ran while one was open for 14% -> 6% of each run, Pallas kernels for 0% -> 2%
where the time goes in v2:
time: 141 us; the launch traced here: 140 us
  blocking collectives  48.1 us (34%)
  starting transfers between devices  43.7 us (31%)
  waiting for transfers between devices  22.2 us (16%)
  Pallas kernels  14.2 us (10%)
  local copies, waits for them, and re-layouts  4.9 us (3%)
  other arithmetic  3.01 us (2%)
  matrix products  2.93 us (2%)
    all_to_all x3, blocking collectives, exchange(): return lax.all_to_all(blocks, axes, split_axis=0, concat_axis=0, tiled=True)  48.1 us
    all_to_all x2, waiting for transfers between devices, exchange(): return lax.all_to_all(blocks, axes, split_axis=0, concat_axis=0, tiled=True)  22.2 us
    all_to_all x2, starting transfers between devices, exchange(): return lax.all_to_all(blocks, axes, split_axis=0, concat_axis=0, tiled=True)  20.4 us
    pallas_call x4, Pallas kernels, call(): pl.pallas_call(kernel, out_shape=out, in_specs=[pl.BlockSpec(memory_space...  11.9 us
    ppermute x1, starting transfers between devices, shards(): over_x = lax.ppermute(own, 'xhi', SWAP)  5.61 us
    ppermute x1, starting transfers between devices, shards(): over_core = lax.ppermute(own, 'core', SWAP)  5.23 us
    ppermute x1, starting transfers between devices, shards(): from_x = lax.ppermute(to_x, 'xhi', SWAP)  4.44 us
    ppermute x1, starting transfers between devices, shards(): from_core = lax.ppermute(to_core, 'core', SWAP)  4.13 us
  transfers between devices with their start and end apart: 7, of which 2 were waited for; matrix products, arithmetic and copies ran while one was open for 6% of the time, Pallas kernels for 2%

profile of v2, /device:TPU:1, one launch (start us, length us, event | category | flops | bytes accessed | tf_op | source)
XLA Modules:
  0.0 139.9 jit_solution(13041187151696745534)
XLA Ops:
  0.7 1.4 pad_maximum_fusion.w0
  2.0 5.6 %collective-permute-start = (bf16[384,1408]{1,0:T(8,128)(2,1)S(1)}, bf16[384,1408]{1,0:T(8,128)(2,1)}, u32[]{:S(2)}, u32[]{:S(2)}) collective-permute-start(bf16[384,1408]{1,0:T(8,128)(2,1)S(1)} %pad_maximum_fusion.w0), channel_id=1, source_target_pairs={{0,256},{256,0},{1,257},{257,1},{2,258},{258,2},{3,259},{259,3},{4... | collective-permute-start | bytes 3244040 | tf_op jit(solution)/shard_map/ppermute | solution.py:114
  7.7 5.2 %collective-permute-start.1 = (bf16[384,1408]{1,0:T(8,128)(2,1)S(1)}, bf16[384,1408]{1,0:T(8,128)(2,1)}, u32[]{:S(2)}, u32[]{:S(2)}) collective-permute-start(bf16[384,1408]{1,0:T(8,128)(2,1)S(1)} %pad_maximum_fusion.w0), channel_id=1, source_target_pairs={{0,16},{16,0},{1,17},{17,1},{2,18},{18,2},{3,19},{19,3},{4,20},{20... | collective-permute-start | bytes 3244040 | tf_op jit(solution)/shard_map/ppermute | solution.py:115
  12.9 0.4 fusion.43
  13.6 0.2 fusion.1
  13.8 0.2 fusion.2
  14.2 1.2 broadcast_in_dim.12
  15.4 15.2 %all-to-all-start = ((bf16[128,2,1408]{2,1,0:T(2,128)(2,1)}), bf16[128,2,1408]{2,1,0:T(2,128)(2,1)S(1)}, u32[]{:S(2)}, u32[]{:S(2)}) async-start(bf16[128,2,1408]{2,1,0:T(2,128)(2,1)} %bitcast.66), calls=%async_computation | async-start | bytes 1441792 | tf_op jit(solution)/shard_map/all_to_all | solution.py:103
  30.6 2.3 %shard_map.93.w1 = bf16[384,1408]{1,0:T(8,128)(2,1)} custom-call(bf16[384,1408]{1,0:T(8,128)(2,1)} %collective-permute-done.src_ref), custom_call_target="tpu_custom_call" | custom-call | flops 20000000000 | bytes 4 | tf_op jit(solution)/shard_map/pallas_call | solution.py:116
  32.9 3.8 %collective-permute-start.2 = (bf16[384,1408]{1,0:T(8,128)(2,1)}, bf16[384,1408]{1,0:T(8,128)(2,1)}, u32[]{:S(2)}, u32[]{:S(2)}) collective-permute-start(bf16[384,1408]{1,0:T(8,128)(2,1)} %shard_map.93.w1), channel_id=1, source_target_pairs={{0,16},{16,0},{1,17},{17,1},{2,18},{18,2},{3,19},{19,3},{4,20},{20... | collective-permute-start | bytes 3244040 | tf_op jit(solution)/shard_map/ppermute | solution.py:121
  36.8 16.4 %all-to-all-done = bf16[128,2,1408]{2,1,0:T(2,128)(2,1)S(1)} async-done(((bf16[128,2,1408]{2,1,0:T(2,128)(2,1)}), bf16[128,2,1408]{2,1,0:T(2,128)(2,1)S(1)}, u32[]{:S(2)}, u32[]{:S(2)}) %all-to-all-start) | async-done | bytes 720928 | tf_op jit(solution)/shard_map/all_to_all | solution.py:103
  53.2 1.0 fusion.44
  54.3 1.1 copy-done.1
  55.4 3.8 %shard_map.94 = (bf16[128,1408]{1,0:T(8,128)(2,1)S(1)}, bf16[768,128]{1,0:T(8,128)(2,1)S(1)}, bf16[768,128]{1,0:T(8,128)(2,1)S(1)}) custom-call(bf16[128,1408]{1,0:T(8,128)(2,1)S(1)} %get-tuple-element.27.x_ref, bf16[128,1408]{1,0:T(8,128)(2,1)S(1)} %get-tuple-element.26.g_ref, bf16[384,1408]{1,0:T(8,128)(2,1)S(1)} %pad_maximum_fusion.w0, ...), custom_call_target="tpu_custom_call" | custom-call | flops 830472192 | bytes 5799936 | tf_op jit(solution)/shard_map/pallas_call | solution.py:28
  59.2 2.0 %shard_map.95 = bf16[768,1408]{1,0:T(8,128)(2,1)} custom-call(bf16[128,1408]{1,0:T(8,128)(2,1)S(1)} %get-tuple-element.27.x_ref, bf16[128,1408]{1,0:T(8,128)(2,1)S(1)} %get-tuple-element.26.g_ref, bf16[768,128]{1,0:T(8,128)(2,1)S(1)} %get-tuple-element.10.act_ref, bf16[768,128]{1,0:T(8,128)(2,1)S(1)} %get-tuple-element.11.slope_ref), custom_call_target="tpu_custom_call" | custom-call | flops 276824064 | bytes 3276800 | tf_op jit(solution)/shard_map/pallas_call | solution.py:28
  61.3 4.1 %collective-permute-start.3 = (bf16[768,1408]{1,0:T(8,128)(2,1)}, bf16[768,1408]{1,0:T(8,128)(2,1)}, u32[]{:S(2)}, u32[]{:S(2)}) collective-permute-start(bf16[768,1408]{1,0:T(8,128)(2,1)} %shard_map.95), channel_id=1, source_target_pairs={{0,16},{16,0},{1,17},{17,1},{2,18},{18,2},{3,19},{19,3},{4,20},{20... | collective-permute-start | bytes 6488072 | tf_op jit(solution)/shard_map/ppermute | solution.py:154
  65.5 0.4 copy.46
  66.0 22.6 %all_to_all.25 = bf16[128,2,768]{2,1,0:T(2,128)(2,1)S(1)} all-to-all(bf16[128,2,768]{2,1,0:T(2,128)(2,1)S(1)} %copy.46), channel_id=1, replica_groups=mesh['xhi'=2,'y'=8,'core'=2,'z'=8,'xlo'=2] {'y','z','xlo'}, dimensions={0} | all-to-all | bytes 786432 | tf_op jit(solution)/shard_map/all_to_all | solution.py:103
  88.6 0.4 reduce.2
  89.1 0.3 fusion.8
  89.4 0.4 multiply_reduce_fusion.1
  89.8 0.2 fusion.6
  90.1 3.0 %shard_map.96 = bf16[384,1408]{1,0:T(8,128)(2,1)} custom-call(bf16[128,1408]{1,0:T(8,128)(2,1)S(1)} %get-tuple-element.27.x_ref, bf16[128,1408]{1,0:T(8,128)(2,1)S(1)} %get-tuple-element.26.g_ref, bf16[768,128]{1,0:T(8,128)(2,1)S(1)} %get-tuple-element.10.act_ref, bf16[768,128]{1,0:T(8,128)(2,1)S(1)} %get-tuple-element.11.slope_ref, ...), custom_call_target="tpu_custom_call" | custom-call | flops 138412032 | bytes 4358144 | tf_op jit(solution)/shard_map/pallas_call | solution.py:28
  93.1 4.4 %collective-permute-start.4 = (bf16[384,1408]{1,0:T(8,128)(2,1)}, bf16[384,1408]{1,0:T(8,128)(2,1)S(1)}, u32[]{:S(2)}, u32[]{:S(2)}) collective-permute-start(bf16[384,1408]{1,0:T(8,128)(2,1)} %shard_map.96), channel_id=1, source_target_pairs={{0,256},{256,0},{1,257},{257,1},{2,258},{258,2},{3,259},{259,3},{4... | collective-permute-start | bytes 3244040 | tf_op jit(solution)/shard_map/ppermute | solution.py:158
  97.7 12.9 %all_to_all.26 = bf16[16,2,768]{2,1,0:T(2,128)(2,1)S(1)} all-to-all(bf16[16,2,768]{2,1,0:T(2,128)(2,1)S(1)} %copy.47), channel_id=1, replica_groups=mesh['xhi'=2,'y'=8,'core'=2,'z'=8,'xlo'=2] {'core','z'}, dimensions={0} | all-to-all | bytes 98304 | tf_op jit(solution)/shard_map/all_to_all | solution.py:103
  110.7 12.6 %all_to_all.27 = bf16[32,2,768]{2,1,0:T(2,128)(2,1)S(1)} all-to-all(bf16[32,2,768]{2,1,0:T(2,128)(2,1)S(1)} %broadcast_in_dim.14), channel_id=1, replica_groups=mesh['xhi'=2,'y'=8,'core'=2,'z'=8,'xlo'=2] {'xhi','y','xlo'}, dimensions={0} | all-to-all | bytes 196608 | tf_op jit(solution)/shard_map/all_to_all | solution.py:103
  123.3 0.7 broadcast_in_dim.15
  124.0 5.2 %all-to-all-start.4 = ((bf16[16,2,768]{2,1,0:T(2,128)(2,1)}), bf16[16,2,768]{2,1,0:T(2,128)(2,1)S(1)}, u32[]{:S(2)}, u32[]{:S(2)}) async-start(bf16[16,2,768]{2,1,0:T(2,128)(2,1)} %broadcast_in_dim.15), calls=%async_computation.4 | async-start | bytes 98304 | tf_op jit(solution)/shard_map/all_to_all | solution.py:103
  129.2 1.2 fusion
  130.5 5.8 %all-to-all-done.4 = bf16[16,2,768]{2,1,0:T(2,128)(2,1)S(1)} async-done(((bf16[16,2,768]{2,1,0:T(2,128)(2,1)}), bf16[16,2,768]{2,1,0:T(2,128)(2,1)S(1)}, u32[]{:S(2)}, u32[]{:S(2)}) %all-to-all-start.4) | async-done | bytes 49184 | tf_op jit(solution)/shard_map/all_to_all | solution.py:103
  136.3 0.6 convert_bitcast_fusion
  137.0 2.9 %shard_map.97 = (bf16[192,1408]{1,0:T(8,128)(2,1)}, bf16[192,1408]{1,0:T(8,128)(2,1)}) custom-call(bf16[128,1408]{1,0:T(8,128)(2,1)S(1)} %get-tuple-element.27.x_ref, bf16[128,1408]{1,0:T(8,128)(2,1)S(1)} %get-tuple-element.26.g_ref, bf16[768,128]{1,0:T(8,128)(2,1)S(1)} %get-tuple-element.10.act_ref, bf16[768,128]{1,0:T(8,128)(2,1)S(1)} %get-tuple-element.11.slope_ref, ...), custom_call_target="tpu_custom_call" | custom-call | flops 138412032 | bytes 5439488 | tf_op jit(solution)/shard_map/pallas_call | solution.py:28
  (41 shorter events, 1.1 us)
Async XLA Ops:
  0.6 12.3 %copy-start = (bf16[1,256,1408]{2,1,0:T(8,128)(2,1)S(1)}, bf16[1,256,1408]{2,1,0:T(8,128)(2,1)}, u32[]{:S(2)}) copy-start(bf16[1,256,1408]{2,1,0:T(8,128)(2,1)} %param.6) | copy-start | bytes 2162692
  0.6 12.3 %copy-start.4 = (bf16[1408,16]{0,1:T(8,128)(2,1)S(1)}, bf16[1408,16]{0,1:T(8,128)(2,1)}, u32[]{:S(2)}) copy-start(bf16[1408,16]{0,1:T(8,128)(2,1)} %param.9) | copy-start | bytes 135172
  2.0 11.8 %copy-start.2 = (bf16[1,256,1408]{2,1,0:T(8,128)(2,1)S(1)}, bf16[1,256,1408]{2,1,0:T(8,128)(2,1)}, u32[]{:S(2)}) copy-start(bf16[1,256,1408]{2,1,0:T(8,128)(2,1)} %param.7) | copy-start | bytes 2162692
  2.0 28.6 %collective-permute-start = (bf16[384,1408]{1,0:T(8,128)(2,1)S(1)}, bf16[384,1408]{1,0:T(8,128)(2,1)}, u32[]{:S(2)}, u32[]{:S(2)}) collective-permute-start(bf16[384,1408]{1,0:T(8,128)(2,1)S(1)} %pad_maximum_fusion.w0), channel_id=1, source_target_pairs={{0,256},{256,0},{1,257},{257,1},{2,258},{258,2},{3,259},{259,3},{4... | collective-permute-start | bytes 3244040 | tf_op jit(solution)/shard_map/ppermute | solution.py:114
  7.7 46.6 %collective-permute-start.1 = (bf16[384,1408]{1,0:T(8,128)(2,1)S(1)}, bf16[384,1408]{1,0:T(8,128)(2,1)}, u32[]{:S(2)}, u32[]{:S(2)}) collective-permute-start(bf16[384,1408]{1,0:T(8,128)(2,1)S(1)} %pad_maximum_fusion.w0), channel_id=1, source_target_pairs={{0,16},{16,0},{1,17},{17,1},{2,18},{18,2},{3,19},{19,3},{4,20},{20... | collective-permute-start | bytes 3244040 | tf_op jit(solution)/shard_map/ppermute | solution.py:115
  15.4 37.8 %all-to-all-start = ((bf16[128,2,1408]{2,1,0:T(2,128)(2,1)}), bf16[128,2,1408]{2,1,0:T(2,128)(2,1)S(1)}, u32[]{:S(2)}, u32[]{:S(2)}) async-start(bf16[128,2,1408]{2,1,0:T(2,128)(2,1)} %bitcast.66), calls=%async_computation | async-start | bytes 1441792 | tf_op jit(solution)/shard_map/all_to_all | solution.py:103
  32.9 21.4 %collective-permute-start.2 = (bf16[384,1408]{1,0:T(8,128)(2,1)}, bf16[384,1408]{1,0:T(8,128)(2,1)}, u32[]{:S(2)}, u32[]{:S(2)}) collective-permute-start(bf16[384,1408]{1,0:T(8,128)(2,1)} %shard_map.93.w1), channel_id=1, source_target_pairs={{0,16},{16,0},{1,17},{17,1},{2,18},{18,2},{3,19},{19,3},{4,20},{20... | collective-permute-start | bytes 3244040 | tf_op jit(solution)/shard_map/ppermute | solution.py:121
  54.2 1.2 copy-start.1
  61.3 28.8 %collective-permute-start.3 = (bf16[768,1408]{1,0:T(8,128)(2,1)}, bf16[768,1408]{1,0:T(8,128)(2,1)}, u32[]{:S(2)}, u32[]{:S(2)}) collective-permute-start(bf16[768,1408]{1,0:T(8,128)(2,1)} %shard_map.95), channel_id=1, source_target_pairs={{0,16},{16,0},{1,17},{17,1},{2,18},{18,2},{3,19},{19,3},{4,20},{20... | collective-permute-start | bytes 6488072 | tf_op jit(solution)/shard_map/ppermute | solution.py:154
  66.0 23.4 %copy-start.3 = (bf16[1,256,1408]{2,1,0:T(8,128)(2,1)S(1)}, bf16[1,256,1408]{2,1,0:T(8,128)(2,1)}, u32[]{:S(2)}) copy-start(bf16[1,256,1408]{2,1,0:T(8,128)(2,1)} %param.7) | copy-start | bytes 2162692
  66.0 23.4 %copy-start.5 = (bf16[1,16,1408]{2,1,0:T(8,128)(2,1)S(1)}, bf16[1,16,1408]{2,1,0:T(8,128)(2,1)}, u32[]{:S(2)}) copy-start(bf16[1,16,1408]{2,1,0:T(8,128)(2,1)} %param.8) | copy-start | bytes 135172
  93.1 43.9 %collective-permute-start.4 = (bf16[384,1408]{1,0:T(8,128)(2,1)}, bf16[384,1408]{1,0:T(8,128)(2,1)S(1)}, u32[]{:S(2)}, u32[]{:S(2)}) collective-permute-start(bf16[384,1408]{1,0:T(8,128)(2,1)} %shard_map.96), channel_id=1, source_target_pairs={{0,256},{256,0},{1,257},{257,1},{2,258},{258,2},{3,259},{259,3},{4... | collective-permute-start | bytes 3244040 | tf_op jit(solution)/shard_map/ppermute | solution.py:158
  124.0 12.3 %all-to-all-start.4 = ((bf16[16,2,768]{2,1,0:T(2,128)(2,1)}), bf16[16,2,768]{2,1,0:T(2,128)(2,1)S(1)}, u32[]{:S(2)}, u32[]{:S(2)}) async-start(bf16[16,2,768]{2,1,0:T(2,128)(2,1)} %broadcast_in_dim.15), calls=%async_computation.4 | async-start | bytes 98304 | tf_op jit(solution)/shard_map/all_to_all | solution.py:103

commit v3 on v2

--- a/solution.py
+++ b/solution.py
@@ -24,13 +24,19 @@
     return lax.dot_general(a, b, (contract, ((), ())), preferred_element_type=F32)
 
 
+def specs(args):
+    return [
+        pl.BlockSpec(memory_space=pltpu.SMEM if a.ndim == 1 else pltpu.VMEM) for a in args
+    ]
+
+
 def call(kernel, out, args, macs):
     return pl.pallas_call(
         kernel,
         out_shape=out,
-        in_specs=[pl.BlockSpec(memory_space=pltpu.VMEM)] * len(args),
+        in_specs=specs(args),
         out_specs=jax.tree.map(lambda _: pl.BlockSpec(memory_space=pltpu.VMEM), out),
-        compiler_params=pltpu.CompilerParams(vmem_limit_bytes=40 * 2**20),
+        compiler_params=pltpu.CompilerParams(vmem_limit_bytes=16 * 2**20),
         cost_estimate=pl.CostEstimate(
             flops=2 * macs,
             bytes_accessed=sum(a.size * a.dtype.itemsize for a in list(args) + list(out)),
@@ -39,7 +45,50 @@
     )(*args)
 
 
-def hidden_kernel(x_ref, g_ref, w0, w1, w2, w3, back_ref, act_ref, slope_ref):
+def softmax(values, axis):
+    top = jnp.exp(values - jnp.max(values, axis=axis, keepdims=True))
+    return top / jnp.sum(top, axis=axis, keepdims=True)
+
+
+def route_kernel(low, tok, cot, par, kept_ref, away_ref, dispatch_ref, combine_ref):
+    logits = dot(par[...], tok[...], ((1,), (1,)))
+    dispatch_ref[...] = softmax(logits, 1)
+    combine_ref[...] = softmax(logits, 0)
+    row = lax.broadcasted_iota(jnp.int32, (16, 16), 0)
+    column = lax.broadcasted_iota(jnp.int32, (16, 16), 1)
+    mine = 1 - low[0]
+    wanted = jnp.where(row < 8, 2 * row + mine, 2 * (row - 8) + 1 - mine)
+    order = jnp.where(column == wanted, 1.0, 0.0).astype(BF16)
+    for k, (weights, rows) in enumerate(((dispatch_ref, tok), (combine_ref, cot))):
+        both = dot(order, weights[...].astype(BF16), ((1,), (0,))).astype(BF16)
+        sums = dot(both, rows[...], ((1,), (0,))).astype(BF16)
+        kept_ref[:, k, :] = sums[:8, :]
+        away_ref[:, k, :] = sums[8:, :]
+
+
+def spread_kernel(low, kept, met, out, rows, sems):
+    @pl.when(low[0] == 1)
+    def _():
+        rows[:, 0] = kept[...]
+        rows[:, 1] = met[...]
+
+    @pl.when(low[0] != 1)
+    def _():
+        rows[:, 0] = met[...]
+        rows[:, 1] = kept[...]
+
+    copies = [pltpu.make_async_copy(rows, out.at[y], sems.at[y]) for y in range(8)]
+    for copy in copies:
+        copy.start()
+    for copy in copies:
+        copy.wait()
+
+
+def hidden_kernel(
+    routed, w0, w1, w2, w3, back_ref, act_ref, slope_ref, x_ref, g_ref
+):
+    x_ref[...] = routed[:, 0, :]
+    g_ref[...] = routed[:, 1, :]
     total = None
     for k, w in enumerate((w0, w1, w2, w3)):
         lift = w[:192, :]
@@ -52,7 +101,10 @@
         slope_ref[pl.ds(192 * k, 192), :] = preact_grad
         part = dot(preact_grad, lift, ((0,), (0,)))
         total = part if total is None else total + part
-    back_ref[...] = total.astype(BF16)
+    back = total.astype(BF16)
+    back_ref[:, 0, :] = back[:, :768]
+    back_ref[:, 1, :640] = back[:, 768:]
+    back_ref[:, 1, 640:] = jnp.zeros((128, 128), BF16)
 
 
 def block_grads(k, x_ref, g_ref, act_ref, slope_ref):
@@ -116,39 +168,49 @@
     over_x = pl.pallas_call(
         copy_kernel,
         out_shape=jax.ShapeDtypeStruct((384, 1408), BF16),
+        compiler_params=pltpu.CompilerParams(vmem_limit_bytes=16 * 2**20),
         cost_estimate=pl.CostEstimate(flops=2 * 10**10, bytes_accessed=4, transcendentals=0),
     )(over_x)
     over_both = lax.ppermute(over_x, "core", SWAP)
 
     params_t = slot_params.T
-    logits = mm("sd,pd->sp", params_t, tokens)
-    dispatch = jax.nn.softmax(logits, axis=1)
-    combine = jax.nn.softmax(logits, axis=0)
+    low = (lax.axis_index("xlo") == 0).astype(jnp.int32).reshape(1)
+    shape = jax.ShapeDtypeStruct
+    rows = shape((8, 2, 1408), BF16)
+    weights = shape((16, 256), F32)
+    kept, away, dispatch, combine = call(
+        route_kernel,
+        (rows, rows, weights, weights),
+        (low, tokens, cotangent, params_t),
+        3 * 16 * 256 * 1408,
+    )
+    met = lax.ppermute(away, "xlo", SWAP)
+    sent = pl.pallas_call(
+        spread_kernel,
+        out_shape=shape((8, 8, 2, 2, 1408), BF16),
+        in_specs=specs((low, kept, met)),
+        out_specs=pl.BlockSpec(memory_space=pltpu.HBM),
+        scratch_shapes=[pltpu.VMEM((8, 2, 2, 1408), BF16), pltpu.SemaphoreType.DMA((8,))],
+        compiler_params=pltpu.CompilerParams(vmem_limit_bytes=16 * 2**20),
+        cost_estimate=pl.CostEstimate(flops=0, bytes_accessed=10**6, transcendentals=0),
+    )(low, kept, met)
+    routed = exchange(sent.reshape(128, 2, 1408), ("y", "z"))
     dispatch_half = dispatch.astype(BF16)
-    slot_inputs = mm("sp,pd->sd", dispatch_half, tokens).astype(BF16)
-    slot_upstream = mm("sp,pd->sd", combine.astype(BF16), cotangent).astype(BF16)
-    sent = jnp.stack([slot_inputs, slot_upstream], axis=1)
-    sent = jnp.broadcast_to(sent[None], (8, 16, 2, 1408)).reshape(128, 2, 1408)
-    routed = exchange(sent, HIDDEN)
-    inputs, upstream = routed[:, 0, :], routed[:, 1, :]
 
     combine_grad = mm("sd,pd->sp", slot_outputs, cotangent)
     combine_part = combine * (
         combine_grad - jnp.sum(combine_grad * combine, axis=0, keepdims=True)
     )
 
-    shape = jax.ShapeDtypeStruct
     units = shape((768, 128), BF16)
-    backward, activated, slopes = call(
+    images = shape((128, 1408), BF16)
+    backward, activated, slopes, inputs, upstream = call(
         hidden_kernel,
-        (shape((128, 1408), BF16), units, units),
-        (inputs, upstream, own, over_x, over_core, over_both),
+        (shape((128, 2, 768), BF16), units, units, images, images),
+        (routed, own, over_x, over_core, over_both),
         3 * 128 * 768 * 1408,
     )
-    returned = exchange(fold(backward), HIDDEN)
-    slot_grad = jnp.sum(returned.astype(F32).reshape(8, 16, 2, 768), axis=0)
-    slot_grad = unfold(slot_grad.astype(BF16))
-
+    returned = exchange(backward, HIDDEN)
     rows = (inputs, upstream, activated, slopes)
     to_core = call(core_kernel, (shape((768, 1408), BF16),), rows, 4 * 192 * 128 * 1408)[0]
     from_core = lax.ppermute(to_core, "core", SWAP)
@@ -156,6 +218,10 @@
         x_kernel, (shape((384, 1408), BF16),), rows + (from_core,), 2 * 192 * 128 * 1408
     )[0]
     from_x = lax.ppermute(to_x, "xhi", SWAP)
+    returned, to_x = lax.optimization_barrier((returned, to_x))
+    slot_grad = jnp.sum(returned.astype(F32).reshape(8, 16, 2, 768), axis=0)
+    slot_grad = unfold(slot_grad.astype(BF16))
+
     half = shape((192, 1408), BF16)
     lift_grad, drop_grad = call(
         own_kernel, (half, half), rows + (from_core, from_x), 2 * 192 * 128 * 1408
@@ -173,6 +239,7 @@
     by_group = exchange(jnp.broadcast_to(by_slot[None], (32, 2, 768)), FAR)
     total = jnp.sum(by_group.astype(F32), axis=0).astype(BF16)
     columns = exchange(jnp.broadcast_to(total[None], (16, 2, 768)), NEAR)
+    columns, lift_grad, drop_grad = lax.optimization_barrier((columns, lift_grad, drop_grad))
     param_grad = unfold(columns).astype(F32).T
 
     token_grad = mm(

time: 141 us -> 155 us (1.099)
  blocking collectives: 48.1 us -> 25.8 us
  waiting for transfers between devices: 22.2 us -> 38.6 us
  starting transfers between devices: 43.7 us -> 55.4 us
  Pallas kernels: 14.2 us -> 16.6 us
  matrix products: 2.93 us -> 5.25 us
  other arithmetic: 3.01 us -> 5.05 us
  local copies, waits for them, and re-layouts: 4.9 us -> 6.56 us
    all_to_all x3 -> x2, blocking collectives: 48.1 us -> 25.8 us  [exchange(): return lax.all_to_all(blocks, axes, split_axis=0, concat_axis=0, tiled=True)]
    ppermute x0 -> x1, waiting for transfers between devices: none -> 15.5 us  [shards(): met = lax.ppermute(away, 'xlo', SWAP)]
    all_to_all x2 -> x3, starting transfers between devices: 20.4 us -> 30.4 us  [exchange(): return lax.all_to_all(blocks, axes, split_axis=0, concat_axis=0, tiled=True)]
    unnamed x16 -> x32, local copies, waits for them, and re-layouts: 1.2 us -> 4.96 us
    pallas_call x4 -> x6, Pallas kernels: 11.9 us -> 14.3 us  [the longest x5 13.2 us: call(): pl.pallas_call(kernel, out_shape=out, in_specs=specs(args), out_specs=jax...]
    dot_general x7 -> x4, matrix products: 2.93 us -> 5.25 us  [mm(): return jnp.einsum(spec, a, b, preferred_element_type=F32)]
    ppermute x0 -> x1, starting transfers between devices: none -> 2.21 us  [shards(): met = lax.ppermute(away, 'xlo', SWAP)]
    ppermute x1, starting transfers between devices: 4.13 us -> 6.04 us  [shards(): from_core = lax.ppermute(to_core, 'core', SWAP)]
  transfers between devices with their start and end apart: 7 -> 9, of which waited for: 2 -> 4; matrix products, arithmetic and copies ran while one was open for 6% -> 7% of each run, Pallas kernels for 2% -> 6%
where the time goes in v3:
time: 155 us; the launch traced here: 154 us
  starting transfers between devices  55.4 us (36%)
  waiting for transfers between devices  38.6 us (25%)
  blocking collectives  25.8 us (17%)
  Pallas kernels  16.6 us (11%)
  local copies, waits for them, and re-layouts  6.56 us (4%)
  matrix products  5.25 us (3%)
  other arithmetic  5.05 us (3%)
    all_to_all x3, starting transfers between devices, exchange(): return lax.all_to_all(blocks, axes, split_axis=0, concat_axis=0, tiled=True)  30.4 us
    all_to_all x2, blocking collectives, exchange(): return lax.all_to_all(blocks, axes, split_axis=0, concat_axis=0, tiled=True)  25.8 us
    all_to_all x3, waiting for transfers between devices, exchange(): return lax.all_to_all(blocks, axes, split_axis=0, concat_axis=0, tiled=True)  23.1 us
    ppermute x1, waiting for transfers between devices, shards(): met = lax.ppermute(away, 'xlo', SWAP)  15.5 us
    pallas_call x5, Pallas kernels, call(): pl.pallas_call(kernel, out_shape=out, in_specs=specs(args), out_specs=jax...  13.2 us
    ppermute x1, starting transfers between devices, shards(): from_core = lax.ppermute(to_core, 'core', SWAP)  6.04 us
    ppermute x1, starting transfers between devices, shards(): over_x = lax.ppermute(own, 'xhi', SWAP)  5.48 us
    dot_general x4, matrix products, mm(): return jnp.einsum(spec, a, b, preferred_element_type=F32)  5.25 us
  transfers between devices with their start and end apart: 9, of which 4 were waited for; matrix products, arithmetic and copies ran while one was open for 7% of the time, Pallas kernels for 6%

profile of v3, /device:TPU:1, one launch (start us, length us, event | category | flops | bytes accessed | tf_op | source)
XLA Modules:
  0.0 154.2 jit_solution(17425461123476218130)
XLA Ops:
  0.7 1.4 pad_maximum_fusion.w0
  2.1 5.5 %collective-permute-start.1 = (bf16[384,1408]{1,0:T(8,128)(2,1)S(1)}, bf16[384,1408]{1,0:T(8,128)(2,1)}, u32[]{:S(2)}, u32[]{:S(2)}) collective-permute-start(bf16[384,1408]{1,0:T(8,128)(2,1)S(1)} %pad_maximum_fusion.w0), channel_id=1, source_target_pairs={{0,256},{256,0},{1,257},{257,1},{2,258},{258,2},{3,259},{259,3},{4... | collective-permute-start | bytes 3244040 | tf_op jit(solution)/shard_map/ppermute | solution.py:166
  7.6 1.3 shard_map.93
  9.5 2.2 %collective-permute-start = (bf16[8,2,1408]{2,1,0:T(2,128)(2,1)S(1)}, bf16[8,2,1408]{2,1,0:T(2,128)(2,1)S(1)}, u32[]{:S(2)}, u32[]{:S(2)}) collective-permute-start(bf16[8,2,1408]{2,1,0:T(2,128)(2,1)S(1)} %get-tuple-element.22), channel_id=1, source_target_pairs={{0,1},{1,0},{2,3},{3,2},{4,5},{5,4},{6,7},{7,6},{8,9},{9,8},{10,11... | collective-permute-start | bytes 135176 | tf_op jit(solution)/shard_map/ppermute | solution.py:187
  11.8 4.9 %collective-permute-start.2 = (bf16[384,1408]{1,0:T(8,128)(2,1)S(1)}, bf16[384,1408]{1,0:T(8,128)(2,1)}, u32[]{:S(2)}, u32[]{:S(2)}) collective-permute-start(bf16[384,1408]{1,0:T(8,128)(2,1)S(1)} %pad_maximum_fusion.w0), channel_id=1, source_target_pairs={{0,16},{16,0},{1,17},{17,1},{2,18},{18,2},{3,19},{19,3},{4,20},{20... | collective-permute-start | bytes 3244040 | tf_op jit(solution)/shard_map/ppermute | solution.py:167
  16.7 15.5 %collective-permute-done.met = bf16[8,2,1408]{2,1,0:T(2,128)(2,1)S(1)} collective-permute-done((bf16[8,2,1408]{2,1,0:T(2,128)(2,1)S(1)}, bf16[8,2,1408]{2,1,0:T(2,128)(2,1)S(1)}, u32[]{:S(2)}, u32[]{:S(2)}) %collective-permute-start) | collective-permute-done | bytes 45088 | tf_op jit(solution)/shard_map/ppermute | solution.py:187
  32.2 1.0 shard_map.94
  33.2 0.8 copy-done.6
  34.1 16.3 %all-to-all-start = ((bf16[128,2,1408]{2,1,0:T(2,128)(2,1)}), bf16[128,2,1408]{2,1,0:T(2,128)(2,1)S(1)}, u32[]{:S(2)}, u32[]{:S(2)}) async-start(bf16[128,2,1408]{2,1,0:T(2,128)(2,1)} %bitcast.46), calls=%async_computation | async-start | bytes 1441792 | tf_op jit(solution)/shard_map/all_to_all | solution.py:155
  50.4 2.3 %shard_map.95.w1 = bf16[384,1408]{1,0:T(8,128)(2,1)} custom-call(bf16[384,1408]{1,0:T(8,128)(2,1)} %collective-permute-done.1.src_ref), custom_call_target="tpu_custom_call" | custom-call | flops 20000000000 | bytes 4 | tf_op jit(solution)/shard_map/pallas_call | solution.py:168
  52.7 3.6 %collective-permute-start.3 = (bf16[384,1408]{1,0:T(8,128)(2,1)}, bf16[384,1408]{1,0:T(8,128)(2,1)}, u32[]{:S(2)}, u32[]{:S(2)}) collective-permute-start(bf16[384,1408]{1,0:T(8,128)(2,1)} %shard_map.95.w1), channel_id=1, source_target_pairs={{0,16},{16,0},{1,17},{17,1},{2,18},{18,2},{3,19},{19,3},{4,20},{20... | collective-permute-start | bytes 3244040 | tf_op jit(solution)/shard_map/ppermute | solution.py:174
  56.4 13.6 %all-to-all-done.routed = bf16[128,2,1408]{2,1,0:T(2,128)(2,1)S(1)} async-done(((bf16[128,2,1408]{2,1,0:T(2,128)(2,1)}), bf16[128,2,1408]{2,1,0:T(2,128)(2,1)S(1)}, u32[]{:S(2)}, u32[]{:S(2)}) %all-to-all-start) | async-done | bytes 720928 | tf_op jit(solution)/shard_map/all_to_all | solution.py:155
  70.0 5.8 %shard_map.96 = (bf16[128,2,768]{2,1,0:T(2,128)(2,1)S(1)}, bf16[768,128]{1,0:T(8,128)(2,1)S(1)}, bf16[768,128]{1,0:T(8,128)(2,1)S(1)}, bf16[128,1408]{1,0:T(8,128)(2,1)S(1)}, bf16[128,1408]{1,0:T(8,128)(2,1)S(1)}) custom-call(bf16[128,2,1408]{2,1,0:T(2,128)(2,1)S(1)} %all-to-all-done.routed, bf16[384,1408]{1,0:T(8,128)(2,1)S(1)} %pad_maximum_fusion.w0, ...), custom_call_target="tpu_custom_call" | custom-call | flops 830472192 | bytes 6553600 | tf_op jit(solution)/shard_map/pallas_call | solution.py:34
  75.8 2.1 %shard_map.97 = bf16[768,1408]{1,0:T(8,128)(2,1)} custom-call(bf16[128,1408]{1,0:T(8,128)(2,1)S(1)} %get-tuple-element.24.x_ref, bf16[128,1408]{1,0:T(8,128)(2,1)S(1)} %get-tuple-element.25.g_ref, bf16[768,128]{1,0:T(8,128)(2,1)S(1)} %get-tuple-element.26.act_ref, bf16[768,128]{1,0:T(8,128)(2,1)S(1)} %get-tuple-element.27.slope_ref), custom_call_target="tpu_custom_call" | custom-call | flops 276824064 | bytes 3276800 | tf_op jit(solution)/shard_map/pallas_call | solution.py:34
  78.6 6.0 %collective-permute-start.4 = (bf16[768,1408]{1,0:T(8,128)(2,1)}, bf16[768,1408]{1,0:T(8,128)(2,1)S(1)}, u32[]{:S(2)}, u32[]{:S(2)}) collective-permute-start(bf16[768,1408]{1,0:T(8,128)(2,1)} %shard_map.97), channel_id=1, source_target_pairs={{0,16},{16,0},{1,17},{17,1},{2,18},{18,2},{3,19},{19,3},{4,20},{20... | collective-permute-start | bytes 6488072 | tf_op jit(solution)/shard_map/ppermute | solution.py:216
  84.7 8.5 %all-to-all-start.1 = ((bf16[128,2,768]{2,1,0:T(2,128)(2,1)}), bf16[128,2,768]{2,1,0:T(2,128)(2,1)}, u32[]{:S(2)}, u32[]{:S(2)}) async-start(bf16[128,2,768]{2,1,0:T(2,128)(2,1)} %copy-done.10), calls=%async_computation.1 | async-start | bytes 786432 | tf_op jit(solution)/shard_map/all_to_all | solution.py:155
  93.2 2.6 %multiply_reduce_fusion.1 = (f32[256]{0:T(256)}, f32[16,256]{1,0:T(8,128)}) fusion(f32[16,256]{1,0:T(8,128)} %copy-done.12, bf16[1,256,1408]{2,1,0:T(8,128)(2,1)} %param.7, bf16[1,16,1408]{2,1,0:T(8,128)(2,1)S(1)} %copy-done), kind=kOutput, calls=%fused_computation.38 | convolution fusion | flops 11542272 | bytes 799744 | tf_op jit(solution)/shard_map/sd,pd->sp/dot_general | solution.py:20
  95.9 1.0 copy-done.3
  96.8 0.9 copy-done.8
  97.8 1.4 shard_map.98
  99.2 2.8 %collective-permute-start.5 = (bf16[384,1408]{1,0:T(8,128)(2,1)}, bf16[384,1408]{1,0:T(8,128)(2,1)}, u32[]{:S(2)}, u32[]{:S(2)}) collective-permute-start(bf16[384,1408]{1,0:T(8,128)(2,1)} %shard_map.98), channel_id=1, source_target_pairs={{0,256},{256,0},{1,257},{257,1},{2,258},{258,2},{3,259},{259,3},{4... | collective-permute-start | bytes 3244040 | tf_op jit(solution)/shard_map/ppermute | solution.py:220
  102.0 7.0 %all-to-all-done.1 = bf16[128,2,768]{2,1,0:T(2,128)(2,1)} async-done(((bf16[128,2,768]{2,1,0:T(2,128)(2,1)}), bf16[128,2,768]{2,1,0:T(2,128)(2,1)}, u32[]{:S(2)}, u32[]{:S(2)}) %all-to-all-start.1) | async-done | bytes 393248 | tf_op jit(solution)/shard_map/all_to_all | solution.py:155
  109.0 2.0 %reduce.2 = bf16[16,2,768]{2,1,0:T(2,128)(2,1)} reduce(bf16[8,16,2,768]{3,2,1,0:T(2,128)(2,1)} %bitcast.8, bf16[]{:T(256)} %constant.11.clone.1), dimensions={0}, to_apply=%region_1.0.clone | reduce | flops 172032 | bytes 442370 | tf_op jit(solution)/shard_map/reduce_sum | solution.py:222
  111.0 0.8 slice.33
  111.8 0.8 copy.34
  113.1 0.8 fusion.30
  114.3 12.7 %all_to_all.25 = bf16[16,2,768]{2,1,0:T(2,128)(2,1)S(1)} all-to-all(bf16[16,2,768]{2,1,0:T(2,128)(2,1)S(1)} %copy.25), channel_id=1, replica_groups=mesh['xhi'=2,'y'=8,'core'=2,'z'=8,'xlo'=2] {'core','z'}, dimensions={0} | all-to-all | bytes 98304 | tf_op jit(solution)/shard_map/all_to_all | solution.py:155
  127.1 13.1 %all_to_all.26 = bf16[32,2,768]{2,1,0:T(2,128)(2,1)S(1)} all-to-all(bf16[32,2,768]{2,1,0:T(2,128)(2,1)S(1)} %broadcast_in_dim.11), channel_id=1, replica_groups=mesh['xhi'=2,'y'=8,'core'=2,'z'=8,'xlo'=2] {'xhi','y','xlo'}, dimensions={0} | all-to-all | bytes 196608 | tf_op jit(solution)/shard_map/all_to_all | solution.py:155
  140.9 5.5 %all-to-all-start.4 = ((bf16[16,2,768]{2,1,0:T(2,128)(2,1)}), bf16[16,2,768]{2,1,0:T(2,128)(2,1)S(1)}, u32[]{:S(2)}, u32[]{:S(2)}) async-start(bf16[16,2,768]{2,1,0:T(2,128)(2,1)} %broadcast_in_dim.12), calls=%async_computation.4 | async-start | bytes 98304 | tf_op jit(solution)/shard_map/all_to_all | solution.py:155
  146.5 2.0 %fusion = bf16[1,256,1408]{2,1,0:T(8,128)(2,1)} fusion(bf16[16,1408]{1,0:T(8,128)(2,1)S(1)} %bitcast.48, bf16[16,640]{1,0:T(8,128)(2,1)} %bitcast.55, bf16[16,768]{1,0:T(8,128)(2,1)} %bitcast.53, bf16[16,256]{1,0:T(8,128)(2,1)S(1)} %get-tuple-element.34, bf16[16,256]{1,0:T(8,128)(2,1)S(1)} %get-tuple-element.35, bf16[16,256]{1,0:T(8,128)(2,1)S(1)} %get-tuple-element.36), kind=kOutput, calls=%fused_computation.1 | convolution fusion | flops 35577856 | bytes 835584 | tf_op jit(solution)/shard_map/kp,kd->pd/dot_general | solution.py:20
  148.5 2.6 %shard_map.99 = (bf16[192,1408]{1,0:T(8,128)(2,1)}, bf16[192,1408]{1,0:T(8,128)(2,1)}) custom-call(bf16[128,1408]{1,0:T(8,128)(2,1)S(1)} %get-tuple-element.24.x_ref, bf16[128,1408]{1,0:T(8,128)(2,1)S(1)} %copy-done.4, bf16[768,128]{1,0:T(8,128)(2,1)S(1)} %get-tuple-element.26.act_ref, bf16[768,128]{1,0:T(8,128)(2,1)S(1)} %copy-done.9, ...), custom_call_target="tpu_custom_call" | custom-call | flops 138412032 | bytes 5439488 | tf_op jit(solution)/shard_map/pallas_call | solution.py:34
  151.1 2.4 %all-to-all-done.4 = bf16[16,2,768]{2,1,0:T(2,128)(2,1)S(1)} async-done(((bf16[16,2,768]{2,1,0:T(2,128)(2,1)}), bf16[16,2,768]{2,1,0:T(2,128)(2,1)S(1)}, u32[]{:S(2)}, u32[]{:S(2)}) %all-to-all-start.4) | async-done | bytes 49184 | tf_op jit(solution)/shard_map/all_to_all | solution.py:155
  (49 shorter events, 3.7 us)
Async XLA Ops:
  0.6 92.6 %copy-start = (bf16[1,16,1408]{2,1,0:T(8,128)(2,1)S(1)}, bf16[1,16,1408]{2,1,0:T(8,128)(2,1)}, u32[]{:S(2)}) copy-start(bf16[1,16,1408]{2,1,0:T(8,128)(2,1)} %param.8) | copy-start | bytes 135172
  0.6 6.9 %copy-start.1 = (bf16[1,256,1408]{2,1,0:T(8,128)(2,1)S(1)}, bf16[1,256,1408]{2,1,0:T(8,128)(2,1)}, u32[]{:S(2)}) copy-start(bf16[1,256,1408]{2,1,0:T(8,128)(2,1)} %param.6) | copy-start | bytes 2162692
  0.7 6.9 %copy-start.5 = (bf16[1,256,1408]{2,1,0:T(8,128)(2,1)S(1)}, bf16[1,256,1408]{2,1,0:T(8,128)(2,1)}, u32[]{:S(2)}) copy-start(bf16[1,256,1408]{2,1,0:T(8,128)(2,1)} %param.7) | copy-start | bytes 2162692
  0.7 6.9 %copy-start.11 = (bf16[1408,16]{0,1:T(8,128)(2,1)S(1)}, bf16[1408,16]{0,1:T(8,128)(2,1)}, u32[]{:S(2)}) copy-start(bf16[1408,16]{0,1:T(8,128)(2,1)} %param.9) | copy-start | bytes 135172
  2.1 48.3 %collective-permute-start.1 = (bf16[384,1408]{1,0:T(8,128)(2,1)S(1)}, bf16[384,1408]{1,0:T(8,128)(2,1)}, u32[]{:S(2)}, u32[]{:S(2)}) collective-permute-start(bf16[384,1408]{1,0:T(8,128)(2,1)S(1)} %pad_maximum_fusion.w0), channel_id=1, source_target_pairs={{0,256},{256,0},{1,257},{257,1},{2,258},{258,2},{3,259},{259,3},{4... | collective-permute-start | bytes 3244040 | tf_op jit(solution)/shard_map/ppermute | solution.py:166
  8.9 0.6 copy-start.12
  9.5 22.7 %collective-permute-start = (bf16[8,2,1408]{2,1,0:T(2,128)(2,1)S(1)}, bf16[8,2,1408]{2,1,0:T(2,128)(2,1)S(1)}, u32[]{:S(2)}, u32[]{:S(2)}) collective-permute-start(bf16[8,2,1408]{2,1,0:T(2,128)(2,1)S(1)} %get-tuple-element.22), channel_id=1, source_target_pairs={{0,1},{1,0},{2,3},{3,2},{4,5},{5,4},{6,7},{7,6},{8,9},{9,8},{10,11... | collective-permute-start | bytes 135176 | tf_op jit(solution)/shard_map/ppermute | solution.py:187
  11.8 44.6 %collective-permute-start.2 = (bf16[384,1408]{1,0:T(8,128)(2,1)S(1)}, bf16[384,1408]{1,0:T(8,128)(2,1)}, u32[]{:S(2)}, u32[]{:S(2)}) collective-permute-start(bf16[384,1408]{1,0:T(8,128)(2,1)S(1)} %pad_maximum_fusion.w0), channel_id=1, source_target_pairs={{0,16},{16,0},{1,17},{17,1},{2,18},{18,2},{3,19},{19,3},{4,20},{20... | collective-permute-start | bytes 3244040 | tf_op jit(solution)/shard_map/ppermute | solution.py:167
  33.2 0.9 copy-start.6
  34.1 35.9 %all-to-all-start = ((bf16[128,2,1408]{2,1,0:T(2,128)(2,1)}), bf16[128,2,1408]{2,1,0:T(2,128)(2,1)S(1)}, u32[]{:S(2)}, u32[]{:S(2)}) async-start(bf16[128,2,1408]{2,1,0:T(2,128)(2,1)} %bitcast.46), calls=%async_computation | async-start | bytes 1441792 | tf_op jit(solution)/shard_map/all_to_all | solution.py:155
  52.7 17.3 %collective-permute-start.3 = (bf16[384,1408]{1,0:T(8,128)(2,1)}, bf16[384,1408]{1,0:T(8,128)(2,1)}, u32[]{:S(2)}, u32[]{:S(2)}) collective-permute-start(bf16[384,1408]{1,0:T(8,128)(2,1)} %shard_map.95.w1), channel_id=1, source_target_pairs={{0,16},{16,0},{1,17},{17,1},{2,18},{18,2},{3,19},{19,3},{4,20},{20... | collective-permute-start | bytes 3244040 | tf_op jit(solution)/shard_map/ppermute | solution.py:174
  75.8 2.1 %copy-start.7 = (bf16[768,128]{1,0:T(8,128)(2,1)}, bf16[768,128]{1,0:T(8,128)(2,1)S(1)}, u32[]{:S(2)}) copy-start(bf16[768,128]{1,0:T(8,128)(2,1)S(1)} %get-tuple-element.27.slope_ref) | copy-start | bytes 589828
  75.8 2.1 %copy-start.10 = (bf16[128,2,768]{2,1,0:T(2,128)(2,1)}, bf16[128,2,768]{2,1,0:T(2,128)(2,1)S(1)}, u32[]{:S(2)}) copy-start(bf16[128,2,768]{2,1,0:T(2,128)(2,1)S(1)} %get-tuple-element.23) | copy-start | bytes 1179652
  77.9 0.7 copy-start.2
  78.6 17.2 %collective-permute-start.4 = (bf16[768,1408]{1,0:T(8,128)(2,1)}, bf16[768,1408]{1,0:T(8,128)(2,1)S(1)}, u32[]{:S(2)}, u32[]{:S(2)}) collective-permute-start(bf16[768,1408]{1,0:T(8,128)(2,1)} %shard_map.97), channel_id=1, source_target_pairs={{0,16},{16,0},{1,17},{17,1},{2,18},{18,2},{3,19},{19,3},{4,20},{20... | collective-permute-start | bytes 6488072 | tf_op jit(solution)/shard_map/ppermute | solution.py:216
  84.7 24.3 %all-to-all-start.1 = ((bf16[128,2,768]{2,1,0:T(2,128)(2,1)}), bf16[128,2,768]{2,1,0:T(2,128)(2,1)}, u32[]{:S(2)}, u32[]{:S(2)}) async-start(bf16[128,2,768]{2,1,0:T(2,128)(2,1)} %copy-done.10), calls=%async_computation.1 | async-start | bytes 786432 | tf_op jit(solution)/shard_map/all_to_all | solution.py:155
  95.9 1.0 copy-start.3
  96.8 0.9 copy-start.8
  99.2 49.3 %collective-permute-start.5 = (bf16[384,1408]{1,0:T(8,128)(2,1)}, bf16[384,1408]{1,0:T(8,128)(2,1)}, u32[]{:S(2)}, u32[]{:S(2)}) collective-permute-start(bf16[384,1408]{1,0:T(8,128)(2,1)} %shard_map.98), channel_id=1, source_target_pairs={{0,256},{256,0},{1,257},{257,1},{2,258},{258,2},{3,259},{259,3},{4... | collective-permute-start | bytes 3244040 | tf_op jit(solution)/shard_map/ppermute | solution.py:220
  111.8 2.4 %copy-start.14 = (bf16[16,1,640]{2,0,1:T(8,128)(2,1)}, bf16[16,1,640]{2,0,1:T(8,128)(2,1)S(1)}, u32[]{:S(2)}) copy-start(bf16[16,1,640]{2,0,1:T(8,128)(2,1)S(1)} %copy.35) | copy-start | bytes 61444
  112.6 1.6 %copy-start.13 = (bf16[16,1,768]{2,0,1:T(8,128)(2,1)}, bf16[16,1,768]{2,0,1:T(8,128)(2,1)S(1)}, u32[]{:S(2)}) copy-start(bf16[16,1,768]{2,0,1:T(8,128)(2,1)S(1)} %copy.34) | copy-start | bytes 73732
  114.1 34.3 %copy-start.4 = (bf16[128,1408]{1,0:T(8,128)(2,1)S(1)}, bf16[128,1408]{1,0:T(8,128)(2,1)}, u32[]{:S(2)}) copy-start(bf16[128,1408]{1,0:T(8,128)(2,1)} %copy-done.2) | copy-start | bytes 1081348
  114.1 34.3 %copy-start.9 = (bf16[768,128]{1,0:T(8,128)(2,1)S(1)}, bf16[768,128]{1,0:T(8,128)(2,1)}, u32[]{:S(2)}) copy-start(bf16[768,128]{1,0:T(8,128)(2,1)} %copy-done.7) | copy-start | bytes 589828
  140.9 12.6 %all-to-all-start.4 = ((bf16[16,2,768]{2,1,0:T(2,128)(2,1)}), bf16[16,2,768]{2,1,0:T(2,128)(2,1)S(1)}, u32[]{:S(2)}, u32[]{:S(2)}) async-start(bf16[16,2,768]{2,1,0:T(2,128)(2,1)} %broadcast_in_dim.12), calls=%async_computation.4 | async-start | bytes 98304 | tf_op jit(solution)/shard_map/all_to_all | solution.py:155

commit v4 on v2

v4 whole, which is shorter than its diff:
```python
import jax
import jax.numpy as jnp
from jax import lax
from jax.experimental import pallas as pl
from jax.experimental.pallas import tpu as pltpu
from jax.sharding import Mesh, PartitionSpec as P

AXES = ("xhi", "y", "core", "z", "xlo")
DP = ("xhi", "y", "core")
NEAR = ("core", "z")
FAR = ("xhi", "y", "xlo")
EXPERT = ("z", "xlo")
HIDDEN = ("y", "z", "xlo")
SWAP = [(0, 1), (1, 0)]
BF16 = jnp.bfloat16
F32 = jnp.float32
LIMIT = 56 * 2**20
shape = jax.ShapeDtypeStruct


def dot(a, b, contract):
    return lax.dot_general(a, b, (contract, ((), ())), preferred_element_type=F32)


def call(kernel, out, args, macs, hbm=False, scratch=(), aliases={}):
    place = pl.ANY if hbm else pltpu.VMEM
    return pl.pallas_call(
        kernel,
        out_shape=out,
        in_specs=[pl.BlockSpec(memory_space=place)] * len(args),
        out_specs=jax.tree.map(lambda _: pl.BlockSpec(memory_space=place), out),
        scratch_shapes=scratch,
        input_output_aliases=aliases,
        compiler_params=pltpu.CompilerParams(vmem_limit_bytes=LIMIT),
        cost_estimate=pl.CostEstimate(
            flops=2 * macs,
            bytes_accessed=sum(a.size * a.dtype.itemsize for a in list(args) + list(out)),
            transcendentals=0,
        ),
    )(*args)


def hold_kernel(src_ref, dst_ref):
    pass


def hold(value):
    return call(hold_kernel, (value,), (value,), 10**10, hbm=True, aliases={0: 0})[0]


def exchange(blocks, axes):
    return lax.all_to_all(blocks, axes, split_axis=0, concat_axis=0, tiled=True)


def softmax(values, axis):
    top = jnp.exp(values - jnp.max(values, axis=axis, keepdims=True))
    return top / jnp.sum(top, axis=axis, keepdims=True)


def route_kernel(tok, cot, par, out, dispatch_ref, combine_ref, tok_v, cot_v, pairs, sems):
    loads = [
        pltpu.make_async_copy(tok, tok_v, sems.at[0]),
        pltpu.make_async_copy(cot, cot_v, sems.at[1]),
    ]
    for load in loads:
        load.start()
    loads[0].wait()
    logits = dot(par[...], tok_v[...], ((1,), (1,)))
    dispatch = softmax(logits, 1)
    combine = softmax(logits, 0)
    dispatch_ref[...] = dispatch
    combine_ref[...] = combine
    pairs[:, 0, :] = dot(dispatch.astype(BF16), tok_v[...], ((1,), (0,))).astype(BF16)
    loads[1].wait()
    pairs[:, 1, :] = dot(combine.astype(BF16), cot_v[...], ((1,), (0,))).astype(BF16)
    copies = [pltpu.make_async_copy(pairs, out.at[y], sems.at[2 + y]) for y in range(8)]
    for copy in copies:
        copy.start()
    for copy in copies:
        copy.wait()


def route(tokens, cotangent, params_t):
    hbm = pl.BlockSpec(memory_space=pl.ANY)
    vmem = pl.BlockSpec(memory_space=pltpu.VMEM)
    return pl.pallas_call(
        route_kernel,
        out_shape=(shape((8, 16, 2, 1408), BF16), shape((16, 256), F32), shape((16, 256), F32)),
        in_specs=[hbm, hbm, vmem],
        out_specs=(hbm, vmem, vmem),
        scratch_shapes=[
            pltpu.VMEM((256, 1408), BF16),
            pltpu.VMEM((256, 1408), BF16),
            pltpu.VMEM((16, 2, 1408), BF16),
            pltpu.SemaphoreType.DMA((10,)),
        ],
        compiler_params=pltpu.CompilerParams(vmem_limit_bytes=LIMIT),
        cost_estimate=pl.CostEstimate(flops=4 * 10**7, bytes_accessed=3 * 10**6, transcendentals=0),
    )(tokens, cotangent, params_t)


def hidden_kernel(*refs):
    routed, weights, outs, scratch = refs[0], refs[1:9], refs[9:15], refs[15:]
    back_out, core_out, act_out, slope_out, x_out, g_out = outs
    rows, lifts, drops, x, g, act, slope, back, core, sems = scratch
    unpack = pltpu.make_async_copy(routed, rows, sems.at[0])
    unpack.start()
    order = (2, 3, 0, 1)
    loads = {}
    for k in order:
        part = pl.ds(192 * k, 192)
        loads[k] = (
            pltpu.make_async_copy(weights[2 * k], lifts.at[part], sems.at[1 + 2 * k]),
            pltpu.make_async_copy(weights[2 * k + 1], drops.at[part], sems.at[2 + 2 * k]),
        )
        for load in loads[k]:
            load.start()
    stores = []

    def store(src, dst):
        copy = pltpu.make_async_copy(src, dst, sems.at[9 + len(stores)])
        copy.start()
        stores.append(copy)

    unpack.wait()
    x[...] = rows[:, 0, :]
    g[...] = rows[:, 1, :]
    store(x, x_out)
    store(g, g_out)
    for k in order:
        part = pl.ds(192 * k, 192)
        for load in loads[k]:
            load.wait()
        preact = dot(lifts[part, :], x[...], ((1,), (1,)))
        activated_grad = dot(drops[part, :], g[...], ((1,), (1,)))
        rise = 0.5 * (1.0 + lax.erf(preact * 0.7071067811865476))
        bell = preact * jnp.exp(-0.5 * preact * preact) * 0.3989422804014327
        activated = (preact * rise).astype(BF16)
        preact_grad = (activated_grad * (rise + bell)).astype(BF16)
        act[part, :] = activated
        slope[part, :] = preact_grad
        if k >= 2:
            half = pl.ds(384 * (k - 2), 384)
            core[pl.ds(384 * (k - 2), 192), :] = dot(preact_grad, x[...], ((1,), (0,))).astype(BF16)
            core[pl.ds(384 * (k - 2) + 192, 192), :] = dot(
                activated, g[...], ((1,), (0,))
            ).astype(BF16)
            store(core.at[half], core_out.at[half])
    store(act, act_out)
    store(slope, slope_out)
    total = dot(slope[...], lifts[...], ((0,), (0,))).astype(BF16)
    back[:, 0, :] = total[:, :768]
    back[:, 1, :640] = total[:, 768:]
    back[:, 1, 640:] = jnp.zeros((128, 128), BF16)
    store(back, back_out)
    for copy in stores:
        copy.wait()


def block_grads(k, x_ref, g_ref, act_ref, slope_ref):
    rows = pl.ds(192 * k, 192)
    lift = dot(slope_ref[rows, :], x_ref[...], ((1,), (0,)))
    drop = dot(act_ref[rows, :], g_ref[...], ((1,), (0,)))
    return lift, drop


def x_kernel(x_ref, g_ref, act_ref, slope_ref, core_ref, out_ref):
    lift, drop = block_grads(1, x_ref, g_ref, act_ref, slope_ref)
    out_ref[:192, :] = (lift + core_ref[384:576, :].astype(F32)).astype(BF16)
    out_ref[192:, :] = (drop + core_ref[576:, :].astype(F32)).astype(BF16)


def own_kernel(x_ref, g_ref, act_ref, slope_ref, core_ref, over_ref, lift_ref, drop_ref):
    lift, drop = block_grads(0, x_ref, g_ref, act_ref, slope_ref)
    lift_ref[...] = (
        lift + core_ref[:192, :].astype(F32) + over_ref[:192, :].astype(F32)
    ).astype(BF16)
    drop_ref[...] = (
        drop + core_ref[192:384, :].astype(F32) + over_ref[192:, :].astype(F32)
    ).astype(BF16)


def combine_kernel(out_ref, cot, combine, grad_ref):
    grad = dot(out_ref[...], cot[...], ((1,), (1,)))
    weighted = jnp.sum(grad * combine[...], axis=0, keepdims=True)
    grad_ref[...] = combine[...] * (grad - weighted)


def image_kernel(
    returned, tok, par, dispatch, part, out, left_ref, right_ref, parts, tok_v, sems
):
    loads = [
        pltpu.make_async_copy(returned, parts, sems.at[0]),
        pltpu.make_async_copy(tok, tok_v, sems.at[1]),
    ]
    for load in loads:
        load.start()
    left_ref[:16, :] = dispatch[...].astype(BF16)
    right_ref[16:32, :] = par[...]
    right_ref[32:, :] = par[...]
    loads[0].wait()
    head = tail = None
    for y in range(8):
        rows = pl.ds(16 * y, 16)
        one = parts[rows, 0, :].astype(F32)
        two = parts[rows, 1, :].astype(F32)
        head = one if head is None else head + one
        tail = two if tail is None else tail + two
    slot_grad = jnp.concatenate([head, tail[:, :640]], axis=1).astype(BF16)
    right_ref[:16, :] = slot_grad
    loads[1].wait()
    grad = dot(slot_grad, tok_v[...], ((1,), (1,)))
    weighted = jnp.sum(grad * dispatch[...], axis=1, keepdims=True)
    logit = part[...] + dispatch[...] * (grad - weighted)
    high = logit.astype(BF16)
    low = (logit - high.astype(F32)).astype(BF16)
    left_ref[16:32, :] = high
    left_ref[32:, :] = low
    local = dot(high, tok_v[...], ((1,), (0,))) + dot(low, tok_v[...], ((1,), (0,)))
    local = local.astype(BF16)
    out[:, 0, :] = local[:, :768]
    out[:, 1, :640] = local[:, 768:]
    out[:, 1, 640:] = jnp.zeros((16, 128), BF16)


def shards(tokens, cotangent, slot_outputs, slot_params, lift_weight, drop_weight):
    tokens, cotangent, slot_outputs = tokens[0], cotangent[0], slot_outputs[0]
    lift, drop = lift_weight[0], drop_weight[0]
    x_lift = hold(lax.ppermute(lift, "xhi", SWAP))
    x_lift, lift_later, drop_later = lax.optimization_barrier((x_lift, lift, drop))
    x_drop = lax.ppermute(drop_later, "xhi", SWAP)
    c_lift = lax.ppermute(lift_later, "core", SWAP)
    c_drop = lax.ppermute(drop_later, "core", SWAP)
    b_lift = lax.ppermute(x_lift, "core", SWAP)
    b_drop = lax.ppermute(x_drop, "core", SWAP)

    params_t = slot_params.T
    sent, dispatch, combine = route(tokens, cotangent, params_t)
    routed = exchange(sent.reshape(128, 2, 1408), HIDDEN)
    combine_part = call(
        combine_kernel,
        (shape((16, 256), F32),),
        (slot_outputs, cotangent, combine),
        16 * 256 * 1408,
    )[0]

    units = shape((768, 128), BF16)
    images = shape((128, 1408), BF16)
    core_half = shape((768, 1408), BF16)
    folded = shape((128, 2, 768), BF16)
    backward, to_core, activated, slopes, inputs, upstream = call(
        hidden_kernel,
        (folded, core_half, units, units, images, images),
        (routed, lift, drop, x_lift, x_drop, c_lift, c_drop, b_lift, b_drop),
        5 * 128 * 768 * 1408,
        hbm=True,
        scratch=[
            pltpu.VMEM(a.shape, BF16)
            for a in (
                routed, core_half, core_half, images, images, units, units, folded, core_half
            )
        ]
        + [pltpu.SemaphoreType.DMA((16,))],
    )
    returned = exchange(backward, HIDDEN)
    rows = (inputs, upstream, activated, slopes)
    from_core = lax.ppermute(to_core, "core", SWAP)
    to_x = call(
        x_kernel, (shape((384, 1408), BF16),), rows + (from_core,), 2 * 192 * 128 * 1408
    )[0]
    from_x = lax.ppermute(to_x, "xhi", SWAP)
    returned, to_x = lax.optimization_barrier((returned, to_x))
    half = shape((192, 1408), BF16)
    lift_grad, drop_grad = call(
        own_kernel, (half, half), rows + (from_core, from_x), 2 * 192 * 128 * 1408
    )

    vmem = pl.BlockSpec(memory_space=pltpu.VMEM)
    hbm = pl.BlockSpec(memory_space=pl.ANY)
    local, left, right = pl.pallas_call(
        image_kernel,
        out_shape=(shape((16, 2, 768), BF16), shape((48, 256), BF16), shape((48, 1408), BF16)),
        in_specs=[hbm, hbm, vmem, vmem, vmem],
        out_specs=(vmem, vmem, vmem),
        scratch_shapes=[
            pltpu.VMEM((128, 2, 768), BF16),
            pltpu.VMEM((256, 1408), BF16),
            pltpu.SemaphoreType.DMA((2,)),
        ],
        compiler_params=pltpu.CompilerParams(vmem_limit_bytes=LIMIT),
        cost_estimate=pl.CostEstimate(flops=4 * 10**7, bytes_accessed=2 * 10**6, transcendentals=0),
    )(returned, tokens, params_t, dispatch, combine_part)
    by_slot = exchange(local, NEAR)
    by_slot = jnp.sum(by_slot.astype(F32), axis=0).astype(BF16)
    by_group = exchange(jnp.broadcast_to(by_slot[None], (32, 2, 768)), FAR)
    total = jnp.sum(by_group.astype(F32), axis=0).astype(BF16)
    columns = exchange(jnp.broadcast_to(total[None], (16, 2, 768)), NEAR)
    columns, lift_grad, drop_grad = lax.optimization_barrier((columns, lift_grad, drop_grad))
    param_grad = jnp.concatenate([columns[:, 0, :], columns[:, 1, :640]], axis=1).astype(F32).T

    token_grad = jnp.einsum("kp,kd->pd", left, right, preferred_element_type=F32).astype(BF16)
    return (token_grad[None], param_grad, lift_grad[None], drop_grad[None])


def solution(mesh):
    split = Mesh(mesh.devices.reshape(2, 8, 2, 8, 2), AXES)
    images = P(AXES, None, None)
    hidden = P(EXPERT, DP, None)
    return jax.shard_map(
        shards,
        mesh=split,
        in_specs=(images, images, images, P(), hidden, hidden),
        out_specs=(images, P(), hidden, hidden),
        check_vma=False,
    )
```

time: 141 us -> 142 us (level)
  blocking collectives: 48.1 us -> 27.2 us
  starting transfers between devices: 43.7 us -> 62.1 us
  Pallas kernels: 14.2 us -> 24.3 us
  waiting for transfers between devices: 22.2 us -> 18.3 us
  other arithmetic: 3.01 us -> 0.81 us
    all_to_all x3 -> x2, blocking collectives: 48.1 us -> 27.2 us  [exchange(): return lax.all_to_all(blocks, axes, split_axis=0, concat_axis=0, tiled=True)]
    all_to_all x2 -> x3, waiting for transfers between devices: 22.2 us -> 5.36 us  [exchange(): return lax.all_to_all(blocks, axes, split_axis=0, concat_axis=0, tiled=True)]
    all_to_all x2 -> x3, starting transfers between devices: 20.4 us -> 35.5 us  [exchange(): return lax.all_to_all(blocks, axes, split_axis=0, concat_axis=0, tiled=True)]
    ppermute x3 -> x6, waiting for transfers between devices: 0.01 us -> 12.9 us  [the longest x1 11.3 us: shards(): x_drop = lax.ppermute(drop_later, 'xhi', SWAP)]
    pallas_call x1 -> x2, Pallas kernels: 2.31 us -> 8.41 us  [the longest x1 4.7 us: route(): pl.pallas_call(route_kernel, out_shape=(shape((8, 16, 2, 1408), BF16), sh...]
    ppermute x3 -> x6, starting transfers between devices: 14.7 us -> 20.3 us  [the longest x1 5.48 us: shards(): x_lift = hold(lax.ppermute(lift, 'xhi', SWAP))]
    pallas_call x4 -> x5, Pallas kernels: 11.9 us -> 15.9 us  [call(): pl.pallas_call(kernel, out_shape=out, in_specs=[pl.BlockSpec(memory_space...]
    unnamed x16 -> x20, local copies, waits for them, and re-layouts: 1.2 us -> 4.32 us
  transfers between devices with their start and end apart: 7 -> 11, of which waited for: 2 -> 4; matrix products, arithmetic and copies ran while one was open for 6% -> 2% of each run, Pallas kernels for 2% -> 12%
where the time goes in v4:
time: 142 us; the launch traced here: 141 us
  starting transfers between devices  62.1 us (44%)
  blocking collectives  27.2 us (19%)
  Pallas kernels  24.3 us (17%)
  waiting for transfers between devices  18.3 us (13%)
  local copies, waits for them, and re-layouts  5.04 us (4%)
  matrix products  2.16 us (2%)
    all_to_all x3, starting transfers between devices, exchange(): return lax.all_to_all(blocks, axes, split_axis=0, concat_axis=0, tiled=True)  35.5 us
    all_to_all x2, blocking collectives, exchange(): return lax.all_to_all(blocks, axes, split_axis=0, concat_axis=0, tiled=True)  27.2 us
    pallas_call x5, Pallas kernels, call(): pl.pallas_call(kernel, out_shape=out, in_specs=[pl.BlockSpec(memory_space...  15.9 us
    ppermute x1, waiting for transfers between devices, shards(): x_drop = lax.ppermute(drop_later, 'xhi', SWAP)  11.3 us
    ppermute x1, starting transfers between devices, shards(): x_lift = hold(lax.ppermute(lift, 'xhi', SWAP))  5.48 us
    all_to_all x3, waiting for transfers between devices, exchange(): return lax.all_to_all(blocks, axes, split_axis=0, concat_axis=0, tiled=True)  5.36 us
    pallas_call x1, Pallas kernels, route(): pl.pallas_call(route_kernel, out_shape=(shape((8, 16, 2, 1408), BF16), sh...  4.7 us
    unnamed x20, local copies, waits for them, and re-layouts  4.32 us
  transfers between devices with their start and end apart: 11, of which 4 were waited for; matrix products, arithmetic and copies ran while one was open for 2% of the time, Pallas kernels for 12%

profile of v4, /device:TPU:1, one launch (start us, length us, event | category | flops | bytes accessed | tf_op | source)
XLA Modules:
  0.0 140.7 jit_solution(8045558825304289765)
XLA Ops:
  0.6 5.5 %collective-permute-start = (bf16[192,1408]{1,0:T(8,128)(2,1)}, bf16[192,1408]{1,0:T(8,128)(2,1)S(1)}, u32[]{:S(2)}, u32[]{:S(2)}) collective-permute-start(bf16[192,1408]{1,0:T(8,128)(2,1)} %bitcast.27), channel_id=1, source_target_pairs={{0,256},{256,0},{1,257},{257,1},{2,258},{258,2},{3,259},{259,3},{4... | collective-permute-start | bytes 1622024 | tf_op jit(solution)/shard_map/ppermute | solution.py:229
  6.1 4.7 %shard_map.93 = (bf16[8,16,2,1408]{3,2,1,0:T(2,128)(2,1)}, f32[16,256]{1,0:T(8,128)}, f32[16,256]{1,0:T(8,128)}) custom-call(bf16[256,1408]{1,0:T(8,128)(2,1)} %bitcast.21, bf16[256,1408]{1,0:T(8,128)(2,1)} %bitcast.19, bf16[16,1408]{1,0:T(8,128)(2,1)} %bitcast.24), custom_call_target="tpu_custom_call" | custom-call | flops 40000000 | bytes 3000000 | tf_op jit(solution)/shard_map/pallas_call | solution.py:86
  10.8 17.6 %all-to-all-start = ((bf16[128,2,1408]{2,1,0:T(2,128)(2,1)}), bf16[128,2,1408]{2,1,0:T(2,128)(2,1)S(1)}, u32[]{:S(2)}, u32[]{:S(2)}) async-start(bf16[128,2,1408]{2,1,0:T(2,128)(2,1)} %bitcast.23), calls=%async_computation | async-start | bytes 1441792 | tf_op jit(solution)/shard_map/all_to_all | solution.py:52
  28.4 0.8 copy-done.9
  29.2 0.4 copy-done.5
  29.6 3.6 %collective-permute-start.1 = (bf16[192,1408]{1,0:T(8,128)(2,1)S(1)}, bf16[192,1408]{1,0:T(8,128)(2,1)S(1)}, u32[]{:S(2)}, u32[]{:S(2)}) collective-permute-start(bf16[192,1408]{1,0:T(8,128)(2,1)S(1)} %bitcast.31), channel_id=1, source_target_pairs={{0,256},{256,0},{1,257},{257,1},{2,258},{258,2},{3,259},{259,3},{4... | collective-permute-start | bytes 1622024 | tf_op jit(solution)/shard_map/ppermute | solution.py:231
  33.3 3.4 %collective-permute-start.2 = (bf16[192,1408]{1,0:T(8,128)(2,1)S(1)}, bf16[192,1408]{1,0:T(8,128)(2,1)S(1)}, u32[]{:S(2)}, u32[]{:S(2)}) collective-permute-start(bf16[192,1408]{1,0:T(8,128)(2,1)S(1)} %bitcast.29), channel_id=1, source_target_pairs={{0,16},{16,0},{1,17},{17,1},{2,18},{18,2},{3,19},{19,3},{4,20},{20... | collective-permute-start | bytes 1622024 | tf_op jit(solution)/shard_map/ppermute | solution.py:232
  36.7 1.9 %collective-permute-start.4 = (bf16[192,1408]{1,0:T(8,128)(2,1)}, bf16[192,1408]{1,0:T(8,128)(2,1)S(1)}, u32[]{:S(2)}, u32[]{:S(2)}) collective-permute-start(bf16[192,1408]{1,0:T(8,128)(2,1)} %shard_map.94.refs_3_), channel_id=1, source_target_pairs={{0,16},{16,0},{1,17},{17,1},{2,18},{18,2},{3,19},{19,3},{4,20},{20... | collective-permute-start | bytes 1622024 | tf_op jit(solution)/shard_map/ppermute | solution.py:234
  38.7 2.4 %collective-permute-start.3 = (bf16[192,1408]{1,0:T(8,128)(2,1)S(1)}, bf16[192,1408]{1,0:T(8,128)(2,1)}, u32[]{:S(2)}, u32[]{:S(2)}) collective-permute-start(bf16[192,1408]{1,0:T(8,128)(2,1)S(1)} %bitcast.32), channel_id=1, source_target_pairs={{0,16},{16,0},{1,17},{17,1},{2,18},{18,2},{3,19},{19,3},{4,20},{20... | collective-permute-start | bytes 1622024 | tf_op jit(solution)/shard_map/ppermute | solution.py:233
  41.1 11.3 %collective-permute-done.1.refs_4_ = bf16[192,1408]{1,0:T(8,128)(2,1)S(1)} collective-permute-done((bf16[192,1408]{1,0:T(8,128)(2,1)S(1)}, bf16[192,1408]{1,0:T(8,128)(2,1)S(1)}, u32[]{:S(2)}, u32[]{:S(2)}) %collective-permute-start.1) | collective-permute-done | bytes 540704 | tf_op jit(solution)/shard_map/ppermute | solution.py:231
  52.4 3.5 %collective-permute-start.5 = (bf16[192,1408]{1,0:T(8,128)(2,1)S(1)}, bf16[192,1408]{1,0:T(8,128)(2,1)}, u32[]{:S(2)}, u32[]{:S(2)}) collective-permute-start(bf16[192,1408]{1,0:T(8,128)(2,1)S(1)} %collective-permute-done.1.refs_4_), channel_id=1, source_target_pairs={{0,16},{16,0},{1,17},{17,1},{2,18},{18,2},{3,19},{19,3},{4,20},{20... | collective-permute-start | bytes 1622024 | tf_op jit(solution)/shard_map/ppermute | solution.py:235
  55.9 1.6 %collective-permute-done.5.refs_8_ = bf16[192,1408]{1,0:T(8,128)(2,1)} collective-permute-done((bf16[192,1408]{1,0:T(8,128)(2,1)S(1)}, bf16[192,1408]{1,0:T(8,128)(2,1)}, u32[]{:S(2)}, u32[]{:S(2)}) %collective-permute-start.5) | collective-permute-done | bytes 540704 | tf_op jit(solution)/shard_map/ppermute | solution.py:235
  57.5 6.8 %shard_map.95 = (bf16[128,2,768]{2,1,0:T(2,128)(2,1)}, bf16[768,1408]{1,0:T(8,128)(2,1)}, bf16[768,128]{1,0:T(8,128)(2,1)}, bf16[768,128]{1,0:T(8,128)(2,1)}, bf...) custom-call(bf16[128,2,1408]{2,1,0:T(2,128)(2,1)} %copy-done.3, bf16[192,1408]{1,0:T(8,128)(2,1)} %bitcast.28, ...), custom_call_target="tpu_custom_call" | custom-call | flops 1384120320 | bytes 8716288 | tf_op jit(solution)/shard_map/pallas_call | solution.py:27
  64.3 2.3 %collective-permute-start.6 = (bf16[768,1408]{1,0:T(8,128)(2,1)}, bf16[768,1408]{1,0:T(8,128)(2,1)S(1)}, u32[]{:S(2)}, u32[]{:S(2)}) collective-permute-start(bf16[768,1408]{1,0:T(8,128)(2,1)} %get-tuple-element.34), channel_id=1, source_target_pairs={{0,16},{16,0},{1,17},{17,1},{2,18},{18,2},{3,19},{19,3},{4,20},{20... | collective-permute-start | bytes 6488072 | tf_op jit(solution)/shard_map/ppermute | solution.py:267
  66.6 12.3 %all-to-all-start.1 = ((bf16[128,2,768]{2,1,0:T(2,128)(2,1)}), bf16[128,2,768]{2,1,0:T(2,128)(2,1)S(1)}, u32[]{:S(2)}, u32[]{:S(2)}) async-start(bf16[128,2,768]{2,1,0:T(2,128)(2,1)} %get-tuple-element.29), calls=%async_computation.1 | async-start | bytes 786432 | tf_op jit(solution)/shard_map/all_to_all | solution.py:52
  79.0 1.3 copy-done
  80.3 3.4 %shard_map.96 = bf16[384,1408]{1,0:T(8,128)(2,1)} custom-call(bf16[128,1408]{1,0:T(8,128)(2,1)} %get-tuple-element.30.x_ref, bf16[128,1408]{1,0:T(8,128)(2,1)} %get-tuple-element.31.g_ref, bf16[768,128]{1,0:T(8,128)(2,1)} %get-tuple-element.32.act_ref, bf16[768,128]{1,0:T(8,128)(2,1)} %get-tuple-element.33.slope_ref, bf16[768,1408]{1,0:T(8,128)(2,1)} %copy-done), custom_call_target="tpu_custom_call" | custom-call | flops 138412032 | bytes 4358144 | tf_op jit(solution)/shard_map/pallas_call | solution.py:27
  83.7 4.0 %collective-permute-start.7 = (bf16[384,1408]{1,0:T(8,128)(2,1)}, bf16[384,1408]{1,0:T(8,128)(2,1)S(1)}, u32[]{:S(2)}, u32[]{:S(2)}) collective-permute-start(bf16[384,1408]{1,0:T(8,128)(2,1)} %shard_map.96), channel_id=1, source_target_pairs={{0,256},{256,0},{1,257},{257,1},{2,258},{258,2},{3,259},{259,3},{4... | collective-permute-start | bytes 3244040 | tf_op jit(solution)/shard_map/ppermute | solution.py:271
  87.8 2.0 %shard_map.97.part = f32[16,256]{1,0:T(8,128)} custom-call(bf16[16,1408]{1,0:T(8,128)(2,1)} %bitcast.26, bf16[256,1408]{1,0:T(8,128)(2,1)} %bitcast.20, f32[16,256]{1,0:T(8,128)} %get-tuple-element.37.combine), custom_call_target="tpu_custom_call" | custom-call | flops 11534336 | bytes 798720 | tf_op jit(solution)/shard_map/pallas_call | solution.py:27
  89.8 5.1 %all-to-all-done.1.returned = bf16[128,2,768]{2,1,0:T(2,128)(2,1)S(1)} async-done(((bf16[128,2,768]{2,1,0:T(2,128)(2,1)}), bf16[128,2,768]{2,1,0:T(2,128)(2,1)S(1)}, u32[]{:S(2)}, u32[]{:S(2)}) %all-to-all-start.1) | async-done | bytes 393248 | tf_op jit(solution)/shard_map/all_to_all | solution.py:52
  94.9 0.7 copy-done.1
  95.7 3.7 %shard_map.98 = (bf16[16,2,768]{2,1,0:T(2,128)(2,1)}, bf16[48,256]{1,0:T(8,128)(2,1)}, bf16[48,1408]{1,0:T(8,128)(2,1)}) custom-call(bf16[128,2,768]{2,1,0:T(2,128)(2,1)} %copy-done.1, bf16[256,1408]{1,0:T(8,128)(2,1)} %bitcast.22, bf16[16,1408]{1,0:T(8,128)(2,1)} %bitcast.25, f32[16,256]{1,0:T(8,128)} %get-tuple-element.36.dispatch, f32[16,256]{1,0:T(8,128)} %shard_map.97.part), custom_call_target="tpu_custom_call" | custom-call | flops 40000000 | bytes 2000000 | tf_op jit(solution)/shard_map/pallas_call | solution.py:280
  99.4 12.9 %all_to_all.25 = bf16[16,2,768]{2,1,0:T(2,128)(2,1)S(1)} all-to-all(bf16[16,2,768]{2,1,0:T(2,128)(2,1)} %get-tuple-element.40), channel_id=1, replica_groups=mesh['xhi'=2,'y'=8,'core'=2,'z'=8,'xlo'=2] {'core','z'}, dimensions={0} | all-to-all | bytes 98304 | tf_op jit(solution)/shard_map/all_to_all | solution.py:52
  112.4 14.3 %all_to_all.26 = bf16[32,2,768]{2,1,0:T(2,128)(2,1)S(1)} all-to-all(bf16[32,2,768]{2,1,0:T(2,128)(2,1)S(1)} %broadcast_in_dim.22), channel_id=1, replica_groups=mesh['xhi'=2,'y'=8,'core'=2,'z'=8,'xlo'=2] {'xhi','y','xlo'}, dimensions={0} | all-to-all | bytes 196608 | tf_op jit(solution)/shard_map/all_to_all | solution.py:52
  126.7 0.1 reduce_sum.25
  126.8 0.7 broadcast_in_dim.23
  127.4 5.5 %all-to-all-start.4 = ((bf16[16,2,768]{2,1,0:T(2,128)(2,1)}), bf16[16,2,768]{2,1,0:T(2,128)(2,1)S(1)}, u32[]{:S(2)}, u32[]{:S(2)}) async-start(bf16[16,2,768]{2,1,0:T(2,128)(2,1)} %broadcast_in_dim.23), calls=%async_computation.4 | async-start | bytes 98304 | tf_op jit(solution)/shard_map/all_to_all | solution.py:52
  133.0 2.2 %fusion = bf16[1,256,1408]{2,1,0:T(8,128)(2,1)} fusion(bf16[48,256]{1,0:T(8,128)(2,1)} %get-tuple-element.38, bf16[48,1408]{1,0:T(8,128)(2,1)} %get-tuple-element.39), kind=kOutput, calls=%fused_computation.1 | convolution fusion | flops 34963456 | bytes 880640 | tf_op jit(solution)/shard_map/kp,kd->pd/dot_general | solution.py:301
  135.1 1.0 copy-done.2
  136.1 3.6 %shard_map.99 = (bf16[192,1408]{1,0:T(8,128)(2,1)}, bf16[192,1408]{1,0:T(8,128)(2,1)}) custom-call(bf16[128,1408]{1,0:T(8,128)(2,1)} %get-tuple-element.30.x_ref, bf16[128,1408]{1,0:T(8,128)(2,1)} %get-tuple-element.31.g_ref, bf16[768,128]{1,0:T(8,128)(2,1)} %get-tuple-element.32.act_ref, bf16[768,128]{1,0:T(8,128)(2,1)} %get-tuple-element.33.slope_ref, ...), custom_call_target="tpu_custom_call" | custom-call | flops 138412032 | bytes 5439488 | tf_op jit(solution)/shard_map/pallas_call | solution.py:27
  139.7 0.3 all-to-all-done.4
  140.0 0.6 convert_bitcast_fusion
  (28 shorter events, 0.2 us)
Async XLA Ops:
  0.6 27.8 %collective-permute-start = (bf16[192,1408]{1,0:T(8,128)(2,1)}, bf16[192,1408]{1,0:T(8,128)(2,1)S(1)}, u32[]{:S(2)}, u32[]{:S(2)}) collective-permute-start(bf16[192,1408]{1,0:T(8,128)(2,1)} %bitcast.27), channel_id=1, source_target_pairs={{0,256},{256,0},{1,257},{257,1},{2,258},{258,2},{3,259},{259,3},{4... | collective-permute-start | bytes 1622024 | tf_op jit(solution)/shard_map/ppermute | solution.py:229
  10.8 45.0 %all-to-all-start = ((bf16[128,2,1408]{2,1,0:T(2,128)(2,1)}), bf16[128,2,1408]{2,1,0:T(2,128)(2,1)S(1)}, u32[]{:S(2)}, u32[]{:S(2)}) async-start(bf16[128,2,1408]{2,1,0:T(2,128)(2,1)} %bitcast.23), calls=%async_computation | async-start | bytes 1441792 | tf_op jit(solution)/shard_map/all_to_all | solution.py:52
  28.4 1.2 copy-start.5
  28.4 4.9 %copy-start.4 = (bf16[1,192,1408]{2,1,0:T(8,128)(2,1)S(1)}, bf16[1,192,1408]{2,1,0:T(8,128)(2,1)}, u32[]{:S(2)}) copy-start(bf16[1,192,1408]{2,1,0:T(8,128)(2,1)} %param.10) | copy-start | bytes 1622020
  28.4 0.8 copy-start.9
  29.6 22.7 %collective-permute-start.1 = (bf16[192,1408]{1,0:T(8,128)(2,1)S(1)}, bf16[192,1408]{1,0:T(8,128)(2,1)S(1)}, u32[]{:S(2)}, u32[]{:S(2)}) collective-permute-start(bf16[192,1408]{1,0:T(8,128)(2,1)S(1)} %bitcast.31), channel_id=1, source_target_pairs={{0,256},{256,0},{1,257},{257,1},{2,258},{258,2},{3,259},{259,3},{4... | collective-permute-start | bytes 1622024 | tf_op jit(solution)/shard_map/ppermute | solution.py:231
  33.3 22.5 %collective-permute-start.2 = (bf16[192,1408]{1,0:T(8,128)(2,1)S(1)}, bf16[192,1408]{1,0:T(8,128)(2,1)S(1)}, u32[]{:S(2)}, u32[]{:S(2)}) collective-permute-start(bf16[192,1408]{1,0:T(8,128)(2,1)S(1)} %bitcast.29), channel_id=1, source_target_pairs={{0,16},{16,0},{1,17},{17,1},{2,18},{18,2},{3,19},{19,3},{4,20},{20... | collective-permute-start | bytes 1622024 | tf_op jit(solution)/shard_map/ppermute | solution.py:232
  36.7 19.1 %collective-permute-start.4 = (bf16[192,1408]{1,0:T(8,128)(2,1)}, bf16[192,1408]{1,0:T(8,128)(2,1)S(1)}, u32[]{:S(2)}, u32[]{:S(2)}) collective-permute-start(bf16[192,1408]{1,0:T(8,128)(2,1)} %shard_map.94.refs_3_), channel_id=1, source_target_pairs={{0,16},{16,0},{1,17},{17,1},{2,18},{18,2},{3,19},{19,3},{4,20},{20... | collective-permute-start | bytes 1622024 | tf_op jit(solution)/shard_map/ppermute | solution.py:234
  38.7 17.2 %collective-permute-start.3 = (bf16[192,1408]{1,0:T(8,128)(2,1)S(1)}, bf16[192,1408]{1,0:T(8,128)(2,1)}, u32[]{:S(2)}, u32[]{:S(2)}) collective-permute-start(bf16[192,1408]{1,0:T(8,128)(2,1)S(1)} %bitcast.32), channel_id=1, source_target_pairs={{0,16},{16,0},{1,17},{17,1},{2,18},{18,2},{3,19},{19,3},{4,20},{20... | collective-permute-start | bytes 1622024 | tf_op jit(solution)/shard_map/ppermute | solution.py:233
  52.3 5.1 %copy-start.6 = (bf16[192,1408]{1,0:T(8,128)(2,1)}, bf16[192,1408]{1,0:T(8,128)(2,1)S(1)}, u32[]{:S(2)}) copy-start(bf16[192,1408]{1,0:T(8,128)(2,1)S(1)} %collective-permute-done.1.refs_4_) | copy-start | bytes 1622020
  52.4 5.1 %collective-permute-start.5 = (bf16[192,1408]{1,0:T(8,128)(2,1)S(1)}, bf16[192,1408]{1,0:T(8,128)(2,1)}, u32[]{:S(2)}, u32[]{:S(2)}) collective-permute-start(bf16[192,1408]{1,0:T(8,128)(2,1)S(1)} %collective-permute-done.1.refs_4_), channel_id=1, source_target_pairs={{0,16},{16,0},{1,17},{17,1},{2,18},{18,2},{3,19},{19,3},{4,20},{20... | collective-permute-start | bytes 1622024 | tf_op jit(solution)/shard_map/ppermute | solution.py:235
  55.8 1.7 %copy-start.7 = (bf16[192,1408]{1,0:T(8,128)(2,1)}, bf16[192,1408]{1,0:T(8,128)(2,1)S(1)}, u32[]{:S(2)}) copy-start(bf16[192,1408]{1,0:T(8,128)(2,1)S(1)} %collective-permute-done.2.refs_5_) | copy-start | bytes 1622020
  55.8 1.6 %copy-start.8 = (bf16[192,1408]{1,0:T(8,128)(2,1)}, bf16[192,1408]{1,0:T(8,128)(2,1)S(1)}, u32[]{:S(2)}) copy-start(bf16[192,1408]{1,0:T(8,128)(2,1)S(1)} %collective-permute-done.4.refs_7_) | copy-start | bytes 1622020
  55.9 1.6 %copy-start.3 = (bf16[128,2,1408]{2,1,0:T(2,128)(2,1)}, bf16[128,2,1408]{2,1,0:T(2,128)(2,1)S(1)}, u32[]{:S(2)}) copy-start(bf16[128,2,1408]{2,1,0:T(2,128)(2,1)S(1)} %all-to-all-done.refs_0_) | copy-start | bytes 2162692
  64.3 14.6 %collective-permute-start.6 = (bf16[768,1408]{1,0:T(8,128)(2,1)}, bf16[768,1408]{1,0:T(8,128)(2,1)S(1)}, u32[]{:S(2)}, u32[]{:S(2)}) collective-permute-start(bf16[768,1408]{1,0:T(8,128)(2,1)} %get-tuple-element.34), channel_id=1, source_target_pairs={{0,16},{16,0},{1,17},{17,1},{2,18},{18,2},{3,19},{19,3},{4,20},{20... | collective-permute-start | bytes 6488072 | tf_op jit(solution)/shard_map/ppermute | solution.py:267
  66.6 28.3 %all-to-all-start.1 = ((bf16[128,2,768]{2,1,0:T(2,128)(2,1)}), bf16[128,2,768]{2,1,0:T(2,128)(2,1)S(1)}, u32[]{:S(2)}, u32[]{:S(2)}) async-start(bf16[128,2,768]{2,1,0:T(2,128)(2,1)} %get-tuple-element.29), calls=%async_computation.1 | async-start | bytes 786432 | tf_op jit(solution)/shard_map/all_to_all | solution.py:52
  79.0 1.3 copy-start
  83.7 51.4 %collective-permute-start.7 = (bf16[384,1408]{1,0:T(8,128)(2,1)}, bf16[384,1408]{1,0:T(8,128)(2,1)S(1)}, u32[]{:S(2)}, u32[]{:S(2)}) collective-permute-start(bf16[384,1408]{1,0:T(8,128)(2,1)} %shard_map.96), channel_id=1, source_target_pairs={{0,256},{256,0},{1,257},{257,1},{2,258},{258,2},{3,259},{259,3},{4... | collective-permute-start | bytes 3244040 | tf_op jit(solution)/shard_map/ppermute | solution.py:271
  94.9 0.7 copy-start.1
  127.4 12.6 %all-to-all-start.4 = ((bf16[16,2,768]{2,1,0:T(2,128)(2,1)}), bf16[16,2,768]{2,1,0:T(2,128)(2,1)S(1)}, u32[]{:S(2)}, u32[]{:S(2)}) async-start(bf16[16,2,768]{2,1,0:T(2,128)(2,1)} %broadcast_in_dim.23), calls=%async_computation.4 | async-start | bytes 98304 | tf_op jit(solution)/shard_map/all_to_all | solution.py:52
  135.1 1.0 copy-start.2

commit v5 on v4

--- a/solution.py
+++ b/solution.py
@@ -15,6 +15,7 @@
 BF16 = jnp.bfloat16
 F32 = jnp.float32
 LIMIT = 56 * 2**20
+SMALL = 24 * 2**20
 shape = jax.ShapeDtypeStruct
 
 
@@ -22,16 +23,16 @@
     return lax.dot_general(a, b, (contract, ((), ())), preferred_element_type=F32)
 
 
-def call(kernel, out, args, macs, hbm=False, scratch=(), aliases={}):
+def call(kernel, out, args, macs, hbm=False, scratch=(), aliases={}, limit=LIMIT):
     place = pl.ANY if hbm else pltpu.VMEM
     return pl.pallas_call(
         kernel,
         out_shape=out,
-        in_specs=[pl.BlockSpec(memory_space=place)] * len(args),
+        in_specs=[pl.BlockSpec(memory_space=place) for a in args],
         out_specs=jax.tree.map(lambda _: pl.BlockSpec(memory_space=place), out),
         scratch_shapes=scratch,
         input_output_aliases=aliases,
-        compiler_params=pltpu.CompilerParams(vmem_limit_bytes=LIMIT),
+        compiler_params=pltpu.CompilerParams(vmem_limit_bytes=limit),
         cost_estimate=pl.CostEstimate(
             flops=2 * macs,
             bytes_accessed=sum(a.size * a.dtype.itemsize for a in list(args) + list(out)),
@@ -57,25 +58,17 @@
     return top / jnp.sum(top, axis=axis, keepdims=True)
 
 
-def route_kernel(tok, cot, par, out, dispatch_ref, combine_ref, tok_v, cot_v, pairs, sems):
-    loads = [
-        pltpu.make_async_copy(tok, tok_v, sems.at[0]),
-        pltpu.make_async_copy(cot, cot_v, sems.at[1]),
-    ]
-    for load in loads:
-        load.start()
-    loads[0].wait()
-    logits = dot(par[...], tok_v[...], ((1,), (1,)))
+def route_kernel(tok, cot, par, out, dispatch_ref, combine_ref, pairs, sems):
+    logits = dot(par[...], tok[...], ((1,), (1,)))
     dispatch = softmax(logits, 1)
     combine = softmax(logits, 0)
+    pairs[:, 0, :] = dot(dispatch.astype(BF16), tok[...], ((1,), (0,))).astype(BF16)
+    pairs[:, 1, :] = dot(combine.astype(BF16), cot[...], ((1,), (0,))).astype(BF16)
+    copies = [pltpu.make_async_copy(pairs, out.at[y], sems.at[y]) for y in range(8)]
+    for copy in copies:
+        copy.start()
     dispatch_ref[...] = dispatch
     combine_ref[...] = combine
-    pairs[:, 0, :] = dot(dispatch.astype(BF16), tok_v[...], ((1,), (0,))).astype(BF16)
-    loads[1].wait()
-    pairs[:, 1, :] = dot(combine.astype(BF16), cot_v[...], ((1,), (0,))).astype(BF16)
-    copies = [pltpu.make_async_copy(pairs, out.at[y], sems.at[2 + y]) for y in range(8)]
-    for copy in copies:
-        copy.start()
     for copy in copies:
         copy.wait()
 
@@ -86,15 +79,10 @@
     return pl.pallas_call(
         route_kernel,
         out_shape=(shape((8, 16, 2, 1408), BF16), shape((16, 256), F32), shape((16, 256), F32)),
-        in_specs=[hbm, hbm, vmem],
+        in_specs=[vmem, vmem, vmem],
         out_specs=(hbm, vmem, vmem),
-        scratch_shapes=[
-            pltpu.VMEM((256, 1408), BF16),
-            pltpu.VMEM((256, 1408), BF16),
-            pltpu.VMEM((16, 2, 1408), BF16),
-            pltpu.SemaphoreType.DMA((10,)),
-        ],
-        compiler_params=pltpu.CompilerParams(vmem_limit_bytes=LIMIT),
+        scratch_shapes=[pltpu.VMEM((16, 2, 1408), BF16), pltpu.SemaphoreType.DMA((8,))],
+        compiler_params=pltpu.CompilerParams(vmem_limit_bytes=SMALL),
         cost_estimate=pl.CostEstimate(flops=4 * 10**7, bytes_accessed=3 * 10**6, transcendentals=0),
     )(tokens, cotangent, params_t)
 
@@ -186,37 +174,27 @@
     grad_ref[...] = combine[...] * (grad - weighted)
 
 
-def image_kernel(
-    returned, tok, par, dispatch, part, out, left_ref, right_ref, parts, tok_v, sems
-):
-    loads = [
-        pltpu.make_async_copy(returned, parts, sems.at[0]),
-        pltpu.make_async_copy(tok, tok_v, sems.at[1]),
-    ]
-    for load in loads:
-        load.start()
-    left_ref[:16, :] = dispatch[...].astype(BF16)
-    right_ref[16:32, :] = par[...]
-    right_ref[32:, :] = par[...]
-    loads[0].wait()
+def image_kernel(returned, tok, par, dispatch, part, out, left_ref, right_ref):
     head = tail = None
     for y in range(8):
         rows = pl.ds(16 * y, 16)
-        one = parts[rows, 0, :].astype(F32)
-        two = parts[rows, 1, :].astype(F32)
+        one = returned[rows, 0, :].astype(F32)
+        two = returned[rows, 1, :].astype(F32)
         head = one if head is None else head + one
         tail = two if tail is None else tail + two
     slot_grad = jnp.concatenate([head, tail[:, :640]], axis=1).astype(BF16)
     right_ref[:16, :] = slot_grad
-    loads[1].wait()
-    grad = dot(slot_grad, tok_v[...], ((1,), (1,)))
+    right_ref[16:32, :] = par[...]
+    right_ref[32:, :] = par[...]
+    grad = dot(slot_grad, tok[...], ((1,), (1,)))
     weighted = jnp.sum(grad * dispatch[...], axis=1, keepdims=True)
     logit = part[...] + dispatch[...] * (grad - weighted)
     high = logit.astype(BF16)
     low = (logit - high.astype(F32)).astype(BF16)
+    left_ref[:16, :] = dispatch[...].astype(BF16)
     left_ref[16:32, :] = high
     left_ref[32:, :] = low
-    local = dot(high, tok_v[...], ((1,), (0,))) + dot(low, tok_v[...], ((1,), (0,)))
+    local = dot(high, tok[...], ((1,), (0,))) + dot(low, tok[...], ((1,), (0,)))
     local = local.astype(BF16)
     out[:, 0, :] = local[:, :768]
     out[:, 1, :640] = local[:, 768:]
@@ -227,8 +205,8 @@
     tokens, cotangent, slot_outputs = tokens[0], cotangent[0], slot_outputs[0]
     lift, drop = lift_weight[0], drop_weight[0]
     x_lift = hold(lax.ppermute(lift, "xhi", SWAP))
+    x_drop = hold(lax.ppermute(drop, "xhi", SWAP))
     x_lift, lift_later, drop_later = lax.optimization_barrier((x_lift, lift, drop))
-    x_drop = lax.ppermute(drop_later, "xhi", SWAP)
     c_lift = lax.ppermute(lift_later, "core", SWAP)
     c_drop = lax.ppermute(drop_later, "core", SWAP)
     b_lift = lax.ppermute(x_lift, "core", SWAP)
@@ -275,21 +253,13 @@
         own_kernel, (half, half), rows + (from_core, from_x), 2 * 192 * 128 * 1408
     )
 
-    vmem = pl.BlockSpec(memory_space=pltpu.VMEM)
-    hbm = pl.BlockSpec(memory_space=pl.ANY)
-    local, left, right = pl.pallas_call(
+    local, left, right = call(
         image_kernel,
-        out_shape=(shape((16, 2, 768), BF16), shape((48, 256), BF16), shape((48, 1408), BF16)),
-        in_specs=[hbm, hbm, vmem, vmem, vmem],
-        out_specs=(vmem, vmem, vmem),
-        scratch_shapes=[
-            pltpu.VMEM((128, 2, 768), BF16),
-            pltpu.VMEM((256, 1408), BF16),
-            pltpu.SemaphoreType.DMA((2,)),
-        ],
-        compiler_params=pltpu.CompilerParams(vmem_limit_bytes=LIMIT),
-        cost_estimate=pl.CostEstimate(flops=4 * 10**7, bytes_accessed=2 * 10**6, transcendentals=0),
-    )(returned, tokens, params_t, dispatch, combine_part)
+        (shape((16, 2, 768), BF16), shape((48, 256), BF16), shape((48, 1408), BF16)),
+        (returned, tokens, params_t, dispatch, combine_part),
+        3 * 16 * 256 * 1408,
+        limit=SMALL,
+    )
     by_slot = exchange(local, NEAR)
     by_slot = jnp.sum(by_slot.astype(F32), axis=0).astype(BF16)
     by_group = exchange(jnp.broadcast_to(by_slot[None], (32, 2, 768)), FAR)

time: 142 us -> 133 us (0.937)
  Pallas kernels: 24.3 us -> 19 us
  local copies, waits for them, and re-layouts: 5.04 us -> 9.51 us
  starting transfers between devices: 62.1 us -> 57.7 us
  waiting for transfers between devices: 18.3 us -> 16 us
    ppermute x1, waiting for transfers between devices: 11.3 us -> 0.01 us  [shards(): x_drop = hold(lax.ppermute(drop, 'xhi', SWAP))]
    all_to_all x3, waiting for transfers between devices: 5.36 us -> 13.8 us  [exchange(): return lax.all_to_all(blocks, axes, split_axis=0, concat_axis=0, tiled=True)]
    all_to_all x3, starting transfers between devices: 35.5 us -> 30.6 us  [exchange(): return lax.all_to_all(blocks, axes, split_axis=0, concat_axis=0, tiled=True)]
    unnamed x20 -> x32, local copies, waits for them, and re-layouts: 4.32 us -> 8.79 us
    pallas_call x1 -> x0, Pallas kernels: 3.72 us -> none  [shards(): pl.pallas_call(image_kernel, out_shape=(shape((16, 2, 768), BF16), shape(...]
    ppermute x1, starting transfers between devices: 2.28 us -> 5.72 us  [shards(): from_core = lax.ppermute(to_core, 'core', SWAP)]
    pallas_call x1, Pallas kernels: 4.7 us -> 2.04 us  [route(): pl.pallas_call(route_kernel, out_shape=(shape((8, 16, 2, 1408), BF16), sh...]
    ppermute x1, starting transfers between devices: 3.63 us -> 1.92 us  [shards(): x_drop = hold(lax.ppermute(drop, 'xhi', SWAP))]
  transfers between devices with their start and end apart: 11 -> 11, of which waited for: 4 -> 4; matrix products, arithmetic and copies ran while one was open for 2% -> 2% of each run, Pallas kernels for 12% -> 9%
where the time goes in v5:
time: 133 us; the launch traced here: 132 us
  starting transfers between devices  57.7 us (43%)
  blocking collectives  26.5 us (20%)
  Pallas kernels  19 us (14%)
  waiting for transfers between devices  16 us (12%)
  local copies, waits for them, and re-layouts  9.51 us (7%)
    all_to_all x3, starting transfers between devices, exchange(): return lax.all_to_all(blocks, axes, split_axis=0, concat_axis=0, tiled=True)  30.6 us
    all_to_all x2, blocking collectives, exchange(): return lax.all_to_all(blocks, axes, split_axis=0, concat_axis=0, tiled=True)  26.5 us
    pallas_call x7, Pallas kernels, call(): pl.pallas_call(kernel, out_shape=out, in_specs=[pl.BlockSpec(memory_space...  17 us
    all_to_all x3, waiting for transfers between devices, exchange(): return lax.all_to_all(blocks, axes, split_axis=0, concat_axis=0, tiled=True)  13.8 us
    unnamed x32, local copies, waits for them, and re-layouts  8.79 us
    ppermute x1, starting transfers between devices, shards(): from_core = lax.ppermute(to_core, 'core', SWAP)  5.72 us
    ppermute x1, starting transfers between devices, shards(): x_lift = hold(lax.ppermute(lift, 'xhi', SWAP))  5.48 us
    ppermute x1, starting transfers between devices, shards(): from_x = lax.ppermute(to_x, 'xhi', SWAP)  4.34 us
  transfers between devices with their start and end apart: 11, of which 4 were waited for; matrix products, arithmetic and copies ran while one was open for 2% of the time, Pallas kernels for 9%

profile of v5, /device:TPU:1, one launch (start us, length us, event | category | flops | bytes accessed | tf_op | source)
XLA Modules:
  0.0 131.7 jit_solution(15828209074201331982)
XLA Ops:
  0.6 5.5 %collective-permute-start = (bf16[192,1408]{1,0:T(8,128)(2,1)}, bf16[192,1408]{1,0:T(8,128)(2,1)S(1)}, u32[]{:S(2)}, u32[]{:S(2)}) collective-permute-start(bf16[192,1408]{1,0:T(8,128)(2,1)} %bitcast.26), channel_id=1, source_target_pairs={{0,256},{256,0},{1,257},{257,1},{2,258},{258,2},{3,259},{259,3},{4... | collective-permute-start | bytes 1622024 | tf_op jit(solution)/shard_map/ppermute | solution.py:207
  6.1 1.9 %collective-permute-start.1 = (bf16[192,1408]{1,0:T(8,128)(2,1)}, bf16[192,1408]{1,0:T(8,128)(2,1)}, u32[]{:S(2)}, u32[]{:S(2)}) collective-permute-start(bf16[192,1408]{1,0:T(8,128)(2,1)} %bitcast.29), channel_id=1, source_target_pairs={{0,256},{256,0},{1,257},{257,1},{2,258},{258,2},{3,259},{259,3},{4... | collective-permute-start | bytes 1622024 | tf_op jit(solution)/shard_map/ppermute | solution.py:208
  8.1 1.1 copy-done
  9.2 1.1 copy-done.1
  10.3 0.8 copy-done.3
  11.1 2.0 %shard_map.93 = (bf16[8,16,2,1408]{3,2,1,0:T(2,128)(2,1)}, f32[16,256]{1,0:T(8,128)S(1)}, f32[16,256]{1,0:T(8,128)S(1)}) custom-call(bf16[256,1408]{1,0:T(8,128)(2,1)S(1)} %bitcast.21, bf16[256,1408]{1,0:T(8,128)(2,1)S(1)} %bitcast.20, bf16[16,1408]{1,0:T(8,128)(2,1)S(1)} %bitcast.23), custom_call_target="tpu_custom_call" | custom-call | flops 40000000 | bytes 3000000 | tf_op jit(solution)/shard_map/pallas_call | solution.py:79
  13.7 18.7 %all-to-all-start = ((bf16[128,2,1408]{2,1,0:T(2,128)(2,1)}), bf16[128,2,1408]{2,1,0:T(2,128)(2,1)S(1)}, u32[]{:S(2)}, u32[]{:S(2)}) async-start(bf16[128,2,1408]{2,1,0:T(2,128)(2,1)} %bitcast.3), calls=%async_computation | async-start | bytes 1441792 | tf_op jit(solution)/shard_map/all_to_all | solution.py:53
  32.4 0.8 copy-done.15
  33.6 3.4 %collective-permute-start.2 = (bf16[192,1408]{1,0:T(8,128)(2,1)S(1)}, bf16[192,1408]{1,0:T(8,128)(2,1)S(1)}, u32[]{:S(2)}, u32[]{:S(2)}) collective-permute-start(bf16[192,1408]{1,0:T(8,128)(2,1)S(1)} %bitcast.28), channel_id=1, source_target_pairs={{0,16},{16,0},{1,17},{17,1},{2,18},{18,2},{3,19},{19,3},{4,20},{20... | collective-permute-start | bytes 1622024 | tf_op jit(solution)/shard_map/ppermute | solution.py:210
  37.1 1.9 %collective-permute-start.3 = (bf16[192,1408]{1,0:T(8,128)(2,1)S(1)}, bf16[192,1408]{1,0:T(8,128)(2,1)S(1)}, u32[]{:S(2)}, u32[]{:S(2)}) collective-permute-start(bf16[192,1408]{1,0:T(8,128)(2,1)S(1)} %bitcast.31), channel_id=1, source_target_pairs={{0,16},{16,0},{1,17},{17,1},{2,18},{18,2},{3,19},{19,3},{4,20},{20... | collective-permute-start | bytes 1622024 | tf_op jit(solution)/shard_map/ppermute | solution.py:211
  39.0 2.4 %collective-permute-start.4 = (bf16[192,1408]{1,0:T(8,128)(2,1)}, bf16[192,1408]{1,0:T(8,128)(2,1)S(1)}, u32[]{:S(2)}, u32[]{:S(2)}) collective-permute-start(bf16[192,1408]{1,0:T(8,128)(2,1)} %shard_map.94.refs_3_), channel_id=1, source_target_pairs={{0,16},{16,0},{1,17},{17,1},{2,18},{18,2},{3,19},{19,3},{4,20},{20... | collective-permute-start | bytes 1622024 | tf_op jit(solution)/shard_map/ppermute | solution.py:212
  41.4 1.9 %collective-permute-start.5 = (bf16[192,1408]{1,0:T(8,128)(2,1)}, bf16[192,1408]{1,0:T(8,128)(2,1)}, u32[]{:S(2)}, u32[]{:S(2)}) collective-permute-start(bf16[192,1408]{1,0:T(8,128)(2,1)} %shard_map.95.refs_4_), channel_id=1, source_target_pairs={{0,16},{16,0},{1,17},{17,1},{2,18},{18,2},{3,19},{19,3},{4,20},{20... | collective-permute-start | bytes 1622024 | tf_op jit(solution)/shard_map/ppermute | solution.py:213
  43.4 2.2 %collective-permute-done.5.refs_8_ = bf16[192,1408]{1,0:T(8,128)(2,1)} collective-permute-done((bf16[192,1408]{1,0:T(8,128)(2,1)}, bf16[192,1408]{1,0:T(8,128)(2,1)}, u32[]{:S(2)}, u32[]{:S(2)}) %collective-permute-start.5) | collective-permute-done | bytes 540704 | tf_op jit(solution)/shard_map/ppermute | solution.py:213
  45.6 7.7 %all-to-all-done.refs_0_ = bf16[128,2,1408]{2,1,0:T(2,128)(2,1)S(1)} async-done(((bf16[128,2,1408]{2,1,0:T(2,128)(2,1)}), bf16[128,2,1408]{2,1,0:T(2,128)(2,1)S(1)}, u32[]{:S(2)}, u32[]{:S(2)}) %all-to-all-start) | async-done | bytes 720928 | tf_op jit(solution)/shard_map/all_to_all | solution.py:53
  53.4 0.8 copy-done.9
  54.2 6.8 %shard_map.96 = (bf16[128,2,768]{2,1,0:T(2,128)(2,1)}, bf16[768,1408]{1,0:T(8,128)(2,1)}, bf16[768,128]{1,0:T(8,128)(2,1)}, bf16[768,128]{1,0:T(8,128)(2,1)}, bf...) custom-call(bf16[128,2,1408]{2,1,0:T(2,128)(2,1)} %copy-done.9, bf16[192,1408]{1,0:T(8,128)(2,1)} %bitcast.27, ...), custom_call_target="tpu_custom_call" | custom-call | flops 1384120320 | bytes 8716288 | tf_op jit(solution)/shard_map/pallas_call | solution.py:28
  61.0 5.7 %collective-permute-start.6 = (bf16[768,1408]{1,0:T(8,128)(2,1)}, bf16[768,1408]{1,0:T(8,128)(2,1)S(1)}, u32[]{:S(2)}, u32[]{:S(2)}) collective-permute-start(bf16[768,1408]{1,0:T(8,128)(2,1)} %get-tuple-element.34), channel_id=1, source_target_pairs={{0,16},{16,0},{1,17},{17,1},{2,18},{18,2},{3,19},{19,3},{4,20},{20... | collective-permute-start | bytes 6488072 | tf_op jit(solution)/shard_map/ppermute | solution.py:245
  66.8 6.4 %all-to-all-start.1 = ((bf16[128,2,768]{2,1,0:T(2,128)(2,1)}), bf16[128,2,768]{2,1,0:T(2,128)(2,1)S(1)}, u32[]{:S(2)}, u32[]{:S(2)}) async-start(bf16[128,2,768]{2,1,0:T(2,128)(2,1)} %get-tuple-element.29), calls=%async_computation.1 | async-start | bytes 786432 | tf_op jit(solution)/shard_map/all_to_all | solution.py:53
  73.2 1.4 %copy-done.7 = bf16[768,1408]{1,0:T(8,128)(2,1)} copy-done((bf16[768,1408]{1,0:T(8,128)(2,1)}, bf16[768,1408]{1,0:T(8,128)(2,1)S(1)}, u32[]{:S(2)}) %copy-start.7) | copy-done | bytes 2162712
  74.6 3.5 %shard_map.97 = bf16[384,1408]{1,0:T(8,128)(2,1)} custom-call(bf16[128,1408]{1,0:T(8,128)(2,1)} %get-tuple-element.30.x_ref, bf16[128,1408]{1,0:T(8,128)(2,1)} %get-tuple-element.31.g_ref, bf16[768,128]{1,0:T(8,128)(2,1)} %get-tuple-element.32.act_ref, bf16[768,128]{1,0:T(8,128)(2,1)} %get-tuple-element.33.slope_ref, bf16[768,1408]{1,0:T(8,128)(2,1)} %copy-done.7), custom_call_target="tpu_custom_call" | custom-call | flops 138412032 | bytes 4358144 | tf_op jit(solution)/shard_map/pallas_call | solution.py:28
  78.0 4.3 %collective-permute-start.7 = (bf16[384,1408]{1,0:T(8,128)(2,1)}, bf16[384,1408]{1,0:T(8,128)(2,1)S(1)}, u32[]{:S(2)}, u32[]{:S(2)}) collective-permute-start(bf16[384,1408]{1,0:T(8,128)(2,1)} %shard_map.97), channel_id=1, source_target_pairs={{0,256},{256,0},{1,257},{257,1},{2,258},{258,2},{3,259},{259,3},{4... | collective-permute-start | bytes 3244040 | tf_op jit(solution)/shard_map/ppermute | solution.py:249
  82.4 2.0 %shard_map.98.part = f32[16,256]{1,0:T(8,128)} custom-call(bf16[16,1408]{1,0:T(8,128)(2,1)} %bitcast.25, bf16[256,1408]{1,0:T(8,128)(2,1)} %bitcast.19, f32[16,256]{1,0:T(8,128)} %copy-done.6), custom_call_target="tpu_custom_call" | custom-call | flops 11534336 | bytes 798720 | tf_op jit(solution)/shard_map/pallas_call | solution.py:28
  84.4 4.8 %all-to-all-done.1.returned = bf16[128,2,768]{2,1,0:T(2,128)(2,1)S(1)} async-done(((bf16[128,2,768]{2,1,0:T(2,128)(2,1)}), bf16[128,2,768]{2,1,0:T(2,128)(2,1)S(1)}, u32[]{:S(2)}, u32[]{:S(2)}) %all-to-all-start.1) | async-done | bytes 393248 | tf_op jit(solution)/shard_map/all_to_all | solution.py:53
  89.3 0.7 copy-done.5
  90.0 1.0 shard_map.99
  91.1 12.5 %all_to_all.25 = bf16[16,2,768]{2,1,0:T(2,128)(2,1)S(1)} all-to-all(bf16[16,2,768]{2,1,0:T(2,128)(2,1)S(1)} %get-tuple-element.40), channel_id=1, replica_groups=mesh['xhi'=2,'y'=8,'core'=2,'z'=8,'xlo'=2] {'core','z'}, dimensions={0} | all-to-all | bytes 98304 | tf_op jit(solution)/shard_map/all_to_all | solution.py:53
  103.7 13.9 %all_to_all.26 = bf16[32,2,768]{2,1,0:T(2,128)(2,1)S(1)} all-to-all(bf16[32,2,768]{2,1,0:T(2,128)(2,1)S(1)} %broadcast_in_dim.22), channel_id=1, replica_groups=mesh['xhi'=2,'y'=8,'core'=2,'z'=8,'xlo'=2] {'xhi','y','xlo'}, dimensions={0} | all-to-all | bytes 196608 | tf_op jit(solution)/shard_map/all_to_all | solution.py:53
  118.4 5.5 %all-to-all-start.4 = ((bf16[16,2,768]{2,1,0:T(2,128)(2,1)}), bf16[16,2,768]{2,1,0:T(2,128)(2,1)S(1)}, u32[]{:S(2)}, u32[]{:S(2)}) async-start(bf16[16,2,768]{2,1,0:T(2,128)(2,1)} %broadcast_in_dim.23), calls=%async_computation.4 | async-start | bytes 98304 | tf_op jit(solution)/shard_map/all_to_all | solution.py:53
  124.0 1.2 fusion
  125.2 1.0 copy-done.8
  126.2 3.6 %shard_map.100 = (bf16[192,1408]{1,0:T(8,128)(2,1)}, bf16[192,1408]{1,0:T(8,128)(2,1)}) custom-call(bf16[128,1408]{1,0:T(8,128)(2,1)} %get-tuple-element.30.x_ref, bf16[128,1408]{1,0:T(8,128)(2,1)} %get-tuple-element.31.g_ref, bf16[768,128]{1,0:T(8,128)(2,1)} %get-tuple-element.32.act_ref, bf16[768,128]{1,0:T(8,128)(2,1)} %get-tuple-element.33.slope_ref, ...), custom_call_target="tpu_custom_call" | custom-call | flops 138412032 | bytes 5439488 | tf_op jit(solution)/shard_map/pallas_call | solution.py:28
  129.8 1.2 all-to-all-done.4
  (41 shorter events, 2.6 us)
Async XLA Ops:
  0.6 31.8 %collective-permute-start = (bf16[192,1408]{1,0:T(8,128)(2,1)}, bf16[192,1408]{1,0:T(8,128)(2,1)S(1)}, u32[]{:S(2)}, u32[]{:S(2)}) collective-permute-start(bf16[192,1408]{1,0:T(8,128)(2,1)} %bitcast.26), channel_id=1, source_target_pairs={{0,256},{256,0},{1,257},{257,1},{2,258},{258,2},{3,259},{259,3},{4... | collective-permute-start | bytes 1622024 | tf_op jit(solution)/shard_map/ppermute | solution.py:207
  6.1 35.3 %collective-permute-start.1 = (bf16[192,1408]{1,0:T(8,128)(2,1)}, bf16[192,1408]{1,0:T(8,128)(2,1)}, u32[]{:S(2)}, u32[]{:S(2)}) collective-permute-start(bf16[192,1408]{1,0:T(8,128)(2,1)} %bitcast.29), channel_id=1, source_target_pairs={{0,256},{256,0},{1,257},{257,1},{2,258},{258,2},{3,259},{259,3},{4... | collective-permute-start | bytes 1622024 | tf_op jit(solution)/shard_map/ppermute | solution.py:208
  8.1 1.1 copy-start
  9.2 1.1 copy-start.1
  10.3 0.8 copy-start.3
  13.1 0.6 copy-start.6
  13.7 39.6 %all-to-all-start = ((bf16[128,2,1408]{2,1,0:T(2,128)(2,1)}), bf16[128,2,1408]{2,1,0:T(2,128)(2,1)S(1)}, u32[]{:S(2)}, u32[]{:S(2)}) async-start(bf16[128,2,1408]{2,1,0:T(2,128)(2,1)} %bitcast.3), calls=%async_computation | async-start | bytes 1441792 | tf_op jit(solution)/shard_map/all_to_all | solution.py:53
  32.4 1.2 copy-start.10
  32.4 4.7 %copy-start.11 = (bf16[1,192,1408]{2,1,0:T(8,128)(2,1)S(1)}, bf16[1,192,1408]{2,1,0:T(8,128)(2,1)}, u32[]{:S(2)}) copy-start(bf16[1,192,1408]{2,1,0:T(8,128)(2,1)} %param.11) | copy-start | bytes 1622020
  32.4 0.8 copy-start.15
  33.6 9.7 %collective-permute-start.2 = (bf16[192,1408]{1,0:T(8,128)(2,1)S(1)}, bf16[192,1408]{1,0:T(8,128)(2,1)S(1)}, u32[]{:S(2)}, u32[]{:S(2)}) collective-permute-start(bf16[192,1408]{1,0:T(8,128)(2,1)S(1)} %bitcast.28), channel_id=1, source_target_pairs={{0,16},{16,0},{1,17},{17,1},{2,18},{18,2},{3,19},{19,3},{4,20},{20... | collective-permute-start | bytes 1622024 | tf_op jit(solution)/shard_map/ppermute | solution.py:210
  37.1 6.3 %collective-permute-start.3 = (bf16[192,1408]{1,0:T(8,128)(2,1)S(1)}, bf16[192,1408]{1,0:T(8,128)(2,1)S(1)}, u32[]{:S(2)}, u32[]{:S(2)}) collective-permute-start(bf16[192,1408]{1,0:T(8,128)(2,1)S(1)} %bitcast.31), channel_id=1, source_target_pairs={{0,16},{16,0},{1,17},{17,1},{2,18},{18,2},{3,19},{19,3},{4,20},{20... | collective-permute-start | bytes 1622024 | tf_op jit(solution)/shard_map/ppermute | solution.py:211
  39.0 4.4 %collective-permute-start.4 = (bf16[192,1408]{1,0:T(8,128)(2,1)}, bf16[192,1408]{1,0:T(8,128)(2,1)S(1)}, u32[]{:S(2)}, u32[]{:S(2)}) collective-permute-start(bf16[192,1408]{1,0:T(8,128)(2,1)} %shard_map.94.refs_3_), channel_id=1, source_target_pairs={{0,16},{16,0},{1,17},{17,1},{2,18},{18,2},{3,19},{19,3},{4,20},{20... | collective-permute-start | bytes 1622024 | tf_op jit(solution)/shard_map/ppermute | solution.py:212
  41.4 4.2 %collective-permute-start.5 = (bf16[192,1408]{1,0:T(8,128)(2,1)}, bf16[192,1408]{1,0:T(8,128)(2,1)}, u32[]{:S(2)}, u32[]{:S(2)}) collective-permute-start(bf16[192,1408]{1,0:T(8,128)(2,1)} %shard_map.95.refs_4_), channel_id=1, source_target_pairs={{0,16},{16,0},{1,17},{17,1},{2,18},{18,2},{3,19},{19,3},{4,20},{20... | collective-permute-start | bytes 1622024 | tf_op jit(solution)/shard_map/ppermute | solution.py:213
  43.4 10.0 %copy-start.12 = (bf16[192,1408]{1,0:T(8,128)(2,1)}, bf16[192,1408]{1,0:T(8,128)(2,1)S(1)}, u32[]{:S(2)}) copy-start(bf16[192,1408]{1,0:T(8,128)(2,1)S(1)} %collective-permute-done.2.refs_5_) | copy-start | bytes 1622020
  43.4 9.9 %copy-start.13 = (bf16[192,1408]{1,0:T(8,128)(2,1)}, bf16[192,1408]{1,0:T(8,128)(2,1)S(1)}, u32[]{:S(2)}) copy-start(bf16[192,1408]{1,0:T(8,128)(2,1)S(1)} %collective-permute-done.3.refs_6_) | copy-start | bytes 1622020
  43.4 9.9 %copy-start.14 = (bf16[192,1408]{1,0:T(8,128)(2,1)}, bf16[192,1408]{1,0:T(8,128)(2,1)S(1)}, u32[]{:S(2)}) copy-start(bf16[192,1408]{1,0:T(8,128)(2,1)S(1)} %collective-permute-done.4.refs_7_) | copy-start | bytes 1622020
  53.4 0.9 copy-start.9
  61.0 12.1 %collective-permute-start.6 = (bf16[768,1408]{1,0:T(8,128)(2,1)}, bf16[768,1408]{1,0:T(8,128)(2,1)S(1)}, u32[]{:S(2)}, u32[]{:S(2)}) collective-permute-start(bf16[768,1408]{1,0:T(8,128)(2,1)} %get-tuple-element.34), channel_id=1, source_target_pairs={{0,16},{16,0},{1,17},{17,1},{2,18},{18,2},{3,19},{19,3},{4,20},{20... | collective-permute-start | bytes 6488072 | tf_op jit(solution)/shard_map/ppermute | solution.py:245
  66.8 22.5 %all-to-all-start.1 = ((bf16[128,2,768]{2,1,0:T(2,128)(2,1)}), bf16[128,2,768]{2,1,0:T(2,128)(2,1)S(1)}, u32[]{:S(2)}, u32[]{:S(2)}) async-start(bf16[128,2,768]{2,1,0:T(2,128)(2,1)} %get-tuple-element.29), calls=%async_computation.1 | async-start | bytes 786432 | tf_op jit(solution)/shard_map/all_to_all | solution.py:53
  73.2 1.4 %copy-start.7 = (bf16[768,1408]{1,0:T(8,128)(2,1)}, bf16[768,1408]{1,0:T(8,128)(2,1)S(1)}, u32[]{:S(2)}) copy-start(bf16[768,1408]{1,0:T(8,128)(2,1)S(1)} %collective-permute-done.6.core_ref) | copy-start | bytes 6488068
  74.5 14.7 %copy-start.2 = (bf16[1,256,1408]{2,1,0:T(8,128)(2,1)S(1)}, bf16[1,256,1408]{2,1,0:T(8,128)(2,1)}, u32[]{:S(2)}) copy-start(bf16[1,256,1408]{2,1,0:T(8,128)(2,1)} %param.6) | copy-start | bytes 2162692
  74.6 14.7 %copy-start.4 = (bf16[1408,16]{0,1:T(8,128)(2,1)S(1)}, bf16[1408,16]{0,1:T(8,128)(2,1)}, u32[]{:S(2)}) copy-start(bf16[1408,16]{0,1:T(8,128)(2,1)} %param.9) | copy-start | bytes 135172
  78.0 47.1 %collective-permute-start.7 = (bf16[384,1408]{1,0:T(8,128)(2,1)}, bf16[384,1408]{1,0:T(8,128)(2,1)S(1)}, u32[]{:S(2)}, u32[]{:S(2)}) collective-permute-start(bf16[384,1408]{1,0:T(8,128)(2,1)} %shard_map.97), channel_id=1, source_target_pairs={{0,256},{256,0},{1,257},{257,1},{2,258},{258,2},{3,259},{259,3},{4... | collective-permute-start | bytes 3244040 | tf_op jit(solution)/shard_map/ppermute | solution.py:249
  89.3 0.7 copy-start.5
  118.4 12.6 %all-to-all-start.4 = ((bf16[16,2,768]{2,1,0:T(2,128)(2,1)}), bf16[16,2,768]{2,1,0:T(2,128)(2,1)S(1)}, u32[]{:S(2)}, u32[]{:S(2)}) async-start(bf16[16,2,768]{2,1,0:T(2,128)(2,1)} %broadcast_in_dim.23), calls=%async_computation.4 | async-start | bytes 98304 | tf_op jit(solution)/shard_map/all_to_all | solution.py:53
  125.2 1.0 copy-start.8

commit v6 on v5

--- a/solution.py
+++ b/solution.py
@@ -46,7 +46,9 @@
 
 
 def hold(value):
-    return call(hold_kernel, (value,), (value,), 10**10, hbm=True, aliases={0: 0})[0]
+    return call(
+        hold_kernel, (value,), (value,), 10**10, hbm=True, aliases={0: 0}, limit=SMALL
+    )[0]
 
 
 def exchange(blocks, axes):
@@ -88,7 +90,7 @@
 
 
 def hidden_kernel(*refs):
-    routed, weights, outs, scratch = refs[0], refs[1:9], refs[9:15], refs[15:]
+    routed, weights, outs, scratch = refs[0], refs[1:5], refs[5:11], refs[11:]
     back_out, core_out, act_out, slope_out, x_out, g_out = outs
     rows, lifts, drops, x, g, act, slope, back, core, sems = scratch
     unpack = pltpu.make_async_copy(routed, rows, sems.at[0])
@@ -98,8 +100,8 @@
     for k in order:
         part = pl.ds(192 * k, 192)
         loads[k] = (
-            pltpu.make_async_copy(weights[2 * k], lifts.at[part], sems.at[1 + 2 * k]),
-            pltpu.make_async_copy(weights[2 * k + 1], drops.at[part], sems.at[2 + 2 * k]),
+            pltpu.make_async_copy(weights[k].at[pl.ds(0, 192)], lifts.at[part], sems.at[1 + 2 * k]),
+            pltpu.make_async_copy(weights[k].at[pl.ds(192, 192)], drops.at[part], sems.at[2 + 2 * k]),
         )
         for load in loads[k]:
             load.start()
@@ -111,8 +113,11 @@
         stores.append(copy)
 
     unpack.wait()
-    x[...] = rows[:, 0, :]
-    g[...] = rows[:, 1, :]
+    for column in range(0, 1408, 128):
+        lanes = pl.ds(column, 128)
+        both = rows[:, :, lanes].astype(F32)
+        x[:, lanes] = both[:, 0, :].astype(BF16)
+        g[:, lanes] = both[:, 1, :].astype(BF16)
     store(x, x_out)
     store(g, g_out)
     for k in order:
@@ -204,13 +209,11 @@
 def shards(tokens, cotangent, slot_outputs, slot_params, lift_weight, drop_weight):
     tokens, cotangent, slot_outputs = tokens[0], cotangent[0], slot_outputs[0]
     lift, drop = lift_weight[0], drop_weight[0]
-    x_lift = hold(lax.ppermute(lift, "xhi", SWAP))
-    x_drop = hold(lax.ppermute(drop, "xhi", SWAP))
-    x_lift, lift_later, drop_later = lax.optimization_barrier((x_lift, lift, drop))
-    c_lift = lax.ppermute(lift_later, "core", SWAP)
-    c_drop = lax.ppermute(drop_later, "core", SWAP)
-    b_lift = lax.ppermute(x_lift, "core", SWAP)
-    b_drop = lax.ppermute(x_drop, "core", SWAP)
+    own = jnp.concatenate([lift, drop], axis=0)
+    over_x = hold(lax.ppermute(own, "xhi", SWAP))
+    over_x, own_later = lax.optimization_barrier((over_x, own))
+    over_core = lax.ppermute(own_later, "core", SWAP)
+    over_both = lax.ppermute(over_x, "core", SWAP)
 
     params_t = slot_params.T
     sent, dispatch, combine = route(tokens, cotangent, params_t)
@@ -229,7 +232,7 @@
     backward, to_core, activated, slopes, inputs, upstream = call(
         hidden_kernel,
         (folded, core_half, units, units, images, images),
-        (routed, lift, drop, x_lift, x_drop, c_lift, c_drop, b_lift, b_drop),
+        (routed, own, over_x, over_core, over_both),
         5 * 128 * 768 * 1408,
         hbm=True,
         scratch=[
@@ -244,13 +247,21 @@
     rows = (inputs, upstream, activated, slopes)
     from_core = lax.ppermute(to_core, "core", SWAP)
     to_x = call(
-        x_kernel, (shape((384, 1408), BF16),), rows + (from_core,), 2 * 192 * 128 * 1408
+        x_kernel,
+        (shape((384, 1408), BF16),),
+        rows + (from_core,),
+        2 * 192 * 128 * 1408,
+        limit=SMALL,
     )[0]
     from_x = lax.ppermute(to_x, "xhi", SWAP)
     returned, to_x = lax.optimization_barrier((returned, to_x))
     half = shape((192, 1408), BF16)
     lift_grad, drop_grad = call(
-        own_kernel, (half, half), rows + (from_core, from_x), 2 * 192 * 128 * 1408
+        own_kernel,
+        (half, half),
+        rows + (from_core, from_x),
+        2 * 192 * 128 * 1408,
+        limit=SMALL,
     )
 
     local, left, right = call(

time: 133 us -> 135 us (1.015)
  Pallas kernels: 19 us -> 15.3 us
  local copies, waits for them, and re-layouts: 9.51 us -> 6.15 us
  starting transfers between devices: 57.7 us -> 61 us
  waiting for transfers between devices: 16 us -> 18.4 us
  other arithmetic: 0.81 us -> 3.1 us
  blocking collectives: 26.5 us -> 28 us
    all_to_all x3, starting transfers between devices: 30.6 us -> 35.7 us  [exchange(): return lax.all_to_all(blocks, axes, split_axis=0, concat_axis=0, tiled=True)]
    all_to_all x3, waiting for transfers between devices: 13.8 us -> 17.9 us  [exchange(): return lax.all_to_all(blocks, axes, split_axis=0, concat_axis=0, tiled=True)]
    pallas_call x7 -> x6, Pallas kernels: 17 us -> 13.3 us  [call(): pl.pallas_call(kernel, out_shape=out, in_specs=[pl.BlockSpec(memory_space...]
    unnamed x32 -> x34, local copies, waits for them, and re-layouts: 8.79 us -> 5.43 us
    ppermute x6 -> x3, starting transfers between devices: 17.1 us -> 15.1 us  [the longest x1 7.65 us: shards(): over_core = lax.ppermute(own_later, 'core', SWAP)]
    ppermute x6 -> x3, waiting for transfers between devices: 2.19 us -> 0.43 us  [the longest x1 0.43 us: shards(): over_x = hold(lax.ppermute(own, 'xhi', SWAP))]
    all_to_all x2, blocking collectives: 26.5 us -> 28 us  [exchange(): return lax.all_to_all(blocks, axes, split_axis=0, concat_axis=0, tiled=True)]
    concatenate x0 -> x1, other arithmetic: none -> 1.4 us  [shards(): own = jnp.concatenate([lift, drop], axis=0)]
  transfers between devices with their start and end apart: 11 -> 8, of which waited for: 4 -> 4; matrix products, arithmetic and copies ran while one was open for 2% -> 2% of each run, Pallas kernels for 9% -> 7%
where the time goes in v6:
time: 135 us; the launch traced here: 134 us
  starting transfers between devices  61 us (45%)
  blocking collectives  28 us (21%)
  waiting for transfers between devices  18.4 us (14%)
  Pallas kernels  15.3 us (11%)
  local copies, waits for them, and re-layouts  6.15 us (5%)
  other arithmetic  3.1 us (2%)
    all_to_all x3, starting transfers between devices, exchange(): return lax.all_to_all(blocks, axes, split_axis=0, concat_axis=0, tiled=True)  35.7 us
    all_to_all x2, blocking collectives, exchange(): return lax.all_to_all(blocks, axes, split_axis=0, concat_axis=0, tiled=True)  28 us
    all_to_all x3, waiting for transfers between devices, exchange(): return lax.all_to_all(blocks, axes, split_axis=0, concat_axis=0, tiled=True)  17.9 us
    pallas_call x6, Pallas kernels, call(): pl.pallas_call(kernel, out_shape=out, in_specs=[pl.BlockSpec(memory_space...  13.3 us
    ppermute x1, starting transfers between devices, shards(): over_core = lax.ppermute(own_later, 'core', SWAP)  7.65 us
    ppermute x1, starting transfers between devices, shards(): from_core = lax.ppermute(to_core, 'core', SWAP)  5.71 us
    ppermute x1, starting transfers between devices, shards(): over_x = hold(lax.ppermute(own, 'xhi', SWAP))  5.48 us
    unnamed x34, local copies, waits for them, and re-layouts  5.43 us
  transfers between devices with their start and end apart: 8, of which 4 were waited for; matrix products, arithmetic and copies ran while one was open for 2% of the time, Pallas kernels for 7%

profile of v6, /device:TPU:1, one launch (start us, length us, event | category | flops | bytes accessed | tf_op | source)
XLA Modules:
  0.0 134.0 jit_solution(2494003042717693720)
XLA Ops:
  0.7 1.4 %pad_maximum_fusion.refs_1_ = bf16[384,1408]{1,0:T(8,128)(2,1)S(1)} fusion(bf16[192,1408]{1,0:T(8,128)(2,1)} %bitcast.25, bf16[192,1408]{1,0:T(8,128)(2,1)} %bitcast.26), kind=kLoop, calls=%fused_computation.2 | loop fusion | flops 2162688 | bytes 2162688 | tf_op jit(solution)/shard_map/concatenate | solution.py:212
  2.1 5.5 %collective-permute-start = (bf16[384,1408]{1,0:T(8,128)(2,1)S(1)}, bf16[384,1408]{1,0:T(8,128)(2,1)S(1)}, u32[]{:S(2)}, u32[]{:S(2)}) collective-permute-start(bf16[384,1408]{1,0:T(8,128)(2,1)S(1)} %pad_maximum_fusion.refs_1_), channel_id=1, source_target_pairs={{0,256},{256,0},{1,257},{257,1},{2,258},{258,2},{3,259},{259,3},{4... | collective-permute-start | bytes 3244040 | tf_op jit(solution)/shard_map/ppermute | solution.py:213
  7.6 2.0 %shard_map.93 = (bf16[8,16,2,1408]{3,2,1,0:T(2,128)(2,1)}, f32[16,256]{1,0:T(8,128)S(1)}, f32[16,256]{1,0:T(8,128)S(1)}) custom-call(bf16[256,1408]{1,0:T(8,128)(2,1)S(1)} %bitcast.21, bf16[256,1408]{1,0:T(8,128)(2,1)S(1)} %bitcast.20, bf16[16,1408]{1,0:T(8,128)(2,1)S(1)} %bitcast.23), custom_call_target="tpu_custom_call" | custom-call | flops 40000000 | bytes 3000000 | tf_op jit(solution)/shard_map/pallas_call | solution.py:81
  9.7 17.6 %all-to-all-start = ((bf16[128,2,1408]{2,1,0:T(2,128)(2,1)}), bf16[128,2,1408]{2,1,0:T(2,128)(2,1)S(1)}, u32[]{:S(2)}, u32[]{:S(2)}) async-start(bf16[128,2,1408]{2,1,0:T(2,128)(2,1)} %bitcast.3), calls=%async_computation | async-start | bytes 1441792 | tf_op jit(solution)/shard_map/all_to_all | solution.py:55
  27.2 0.4 collective-permute-done.src_ref
  27.7 7.6 %collective-permute-start.1 = (bf16[384,1408]{1,0:T(8,128)(2,1)S(1)}, bf16[384,1408]{1,0:T(8,128)(2,1)}, u32[]{:S(2)}, u32[]{:S(2)}) collective-permute-start(bf16[384,1408]{1,0:T(8,128)(2,1)S(1)} %pad_maximum_fusion.refs_1_), channel_id=1, source_target_pairs={{0,16},{16,0},{1,17},{17,1},{2,18},{18,2},{3,19},{19,3},{4,20},{20... | collective-permute-start | bytes 3244040 | tf_op jit(solution)/shard_map/ppermute | solution.py:215
  35.3 1.9 %collective-permute-start.2 = (bf16[384,1408]{1,0:T(8,128)(2,1)S(1)}, bf16[384,1408]{1,0:T(8,128)(2,1)}, u32[]{:S(2)}, u32[]{:S(2)}) collective-permute-start(bf16[384,1408]{1,0:T(8,128)(2,1)S(1)} %shard_map.94.refs_2_), channel_id=1, source_target_pairs={{0,16},{16,0},{1,17},{17,1},{2,18},{18,2},{3,19},{19,3},{4,20},{20... | collective-permute-start | bytes 3244040 | tf_op jit(solution)/shard_map/ppermute | solution.py:216
  37.3 11.0 %all-to-all-done.refs_0_ = bf16[128,2,1408]{2,1,0:T(2,128)(2,1)S(1)} async-done(((bf16[128,2,1408]{2,1,0:T(2,128)(2,1)}), bf16[128,2,1408]{2,1,0:T(2,128)(2,1)S(1)}, u32[]{:S(2)}, u32[]{:S(2)}) %all-to-all-start) | async-done | bytes 720928 | tf_op jit(solution)/shard_map/all_to_all | solution.py:55
  48.2 0.8 copy-done.16
  49.1 6.2 %shard_map.95 = (bf16[128,2,768]{2,1,0:T(2,128)(2,1)}, bf16[768,1408]{1,0:T(8,128)(2,1)}, bf16[768,128]{1,0:T(8,128)(2,1)}, bf16[768,128]{1,0:T(8,128)(2,1)}, bf...) custom-call(bf16[128,2,1408]{2,1,0:T(2,128)(2,1)} %copy-done.16, bf16[384,1408]{1,0:T(8,128)(2,1)} %copy-done.15, ...), custom_call_target="tpu_custom_call" | custom-call | flops 1384120320 | bytes 8716288 | tf_op jit(solution)/shard_map/pallas_call | solution.py:28
  55.3 5.7 %collective-permute-start.3 = (bf16[768,1408]{1,0:T(8,128)(2,1)}, bf16[768,1408]{1,0:T(8,128)(2,1)S(1)}, u32[]{:S(2)}, u32[]{:S(2)}) collective-permute-start(bf16[768,1408]{1,0:T(8,128)(2,1)} %get-tuple-element.32), channel_id=1, source_target_pairs={{0,16},{16,0},{1,17},{17,1},{2,18},{18,2},{3,19},{19,3},{4,20},{20... | collective-permute-start | bytes 6488072 | tf_op jit(solution)/shard_map/ppermute | solution.py:248
  61.0 12.6 %all-to-all-start.1 = ((bf16[128,2,768]{2,1,0:T(2,128)(2,1)}), bf16[128,2,768]{2,1,0:T(2,128)(2,1)S(1)}, u32[]{:S(2)}, u32[]{:S(2)}) async-start(bf16[128,2,768]{2,1,0:T(2,128)(2,1)} %get-tuple-element.27), calls=%async_computation.1 | async-start | bytes 786432 | tf_op jit(solution)/shard_map/all_to_all | solution.py:55
  73.7 1.0 copy-done.3
  74.6 1.0 copy-done.5
  75.6 0.9 copy-done.7
  76.6 0.9 copy-done.9
  77.5 1.4 %shard_map.96 = bf16[384,1408]{1,0:T(8,128)(2,1)} custom-call(bf16[128,1408]{1,0:T(8,128)(2,1)S(1)} %copy-done.3, bf16[128,1408]{1,0:T(8,128)(2,1)S(1)} %copy-done.5, bf16[768,128]{1,0:T(8,128)(2,1)S(1)} %copy-done.7, bf16[768,128]{1,0:T(8,128)(2,1)S(1)} %copy-done.9, bf16[768,1408]{1,0:T(8,128)(2,1)S(1)} %collective-permute-done.3.core_ref), custom_call_target="tpu_custom_call" | custom-call | flops 138412032 | bytes 4358144 | tf_op jit(solution)/shard_map/pallas_call | solution.py:28
  78.9 4.5 %collective-permute-start.4 = (bf16[384,1408]{1,0:T(8,128)(2,1)}, bf16[384,1408]{1,0:T(8,128)(2,1)}, u32[]{:S(2)}, u32[]{:S(2)}) collective-permute-start(bf16[384,1408]{1,0:T(8,128)(2,1)} %shard_map.96), channel_id=1, source_target_pairs={{0,256},{256,0},{1,257},{257,1},{2,258},{258,2},{3,259},{259,3},{4... | collective-permute-start | bytes 3244040 | tf_op jit(solution)/shard_map/ppermute | solution.py:256
  83.4 2.0 %shard_map.97.part = f32[16,256]{1,0:T(8,128)} custom-call(bf16[16,1408]{1,0:T(8,128)(2,1)} %bitcast.27, bf16[256,1408]{1,0:T(8,128)(2,1)} %bitcast.19, f32[16,256]{1,0:T(8,128)} %copy-done.13), custom_call_target="tpu_custom_call" | custom-call | flops 11534336 | bytes 798720 | tf_op jit(solution)/shard_map/pallas_call | solution.py:28
  85.4 3.8 %all-to-all-done.1.returned = bf16[128,2,768]{2,1,0:T(2,128)(2,1)S(1)} async-done(((bf16[128,2,768]{2,1,0:T(2,128)(2,1)}), bf16[128,2,768]{2,1,0:T(2,128)(2,1)S(1)}, u32[]{:S(2)}, u32[]{:S(2)}) %all-to-all-start.1) | async-done | bytes 393248 | tf_op jit(solution)/shard_map/all_to_all | solution.py:55
  89.2 0.7 copy-done.12
  89.9 1.0 shard_map.98
  91.0 13.2 %all_to_all.25 = bf16[16,2,768]{2,1,0:T(2,128)(2,1)S(1)} all-to-all(bf16[16,2,768]{2,1,0:T(2,128)(2,1)S(1)} %get-tuple-element.38), channel_id=1, replica_groups=mesh['xhi'=2,'y'=8,'core'=2,'z'=8,'xlo'=2] {'core','z'}, dimensions={0} | all-to-all | bytes 98304 | tf_op jit(solution)/shard_map/all_to_all | solution.py:55
  104.3 0.1 reduce_sum.24
  104.4 14.7 %all_to_all.26 = bf16[32,2,768]{2,1,0:T(2,128)(2,1)} all-to-all(bf16[32,2,768]{2,1,0:T(2,128)(2,1)S(1)} %broadcast_in_dim.22), channel_id=1, replica_groups=mesh['xhi'=2,'y'=8,'core'=2,'z'=8,'xlo'=2] {'xhi','y','xlo'}, dimensions={0} | all-to-all | bytes 196608 | tf_op jit(solution)/shard_map/all_to_all | solution.py:55
  119.1 1.0 reduce_sum.25
  120.1 0.7 broadcast_in_dim.23
  120.8 5.5 %all-to-all-start.4 = ((bf16[16,2,768]{2,1,0:T(2,128)(2,1)}), bf16[16,2,768]{2,1,0:T(2,128)(2,1)S(1)}, u32[]{:S(2)}, u32[]{:S(2)}) async-start(bf16[16,2,768]{2,1,0:T(2,128)(2,1)} %broadcast_in_dim.23), calls=%async_computation.4 | async-start | bytes 98304 | tf_op jit(solution)/shard_map/all_to_all | solution.py:55
  126.3 1.2 fusion
  127.6 2.6 %shard_map.99 = (bf16[192,1408]{1,0:T(8,128)(2,1)}, bf16[192,1408]{1,0:T(8,128)(2,1)}) custom-call(bf16[128,1408]{1,0:T(8,128)(2,1)S(1)} %copy-done.4, bf16[128,1408]{1,0:T(8,128)(2,1)S(1)} %copy-done.6, bf16[768,128]{1,0:T(8,128)(2,1)S(1)} %copy-done.8, bf16[768,128]{1,0:T(8,128)(2,1)S(1)} %copy-done.10, ...), custom_call_target="tpu_custom_call" | custom-call | flops 138412032 | bytes 5439488 | tf_op jit(solution)/shard_map/pallas_call | solution.py:28
  130.1 3.2 %all-to-all-done.4 = bf16[16,2,768]{2,1,0:T(2,128)(2,1)S(1)} async-done(((bf16[16,2,768]{2,1,0:T(2,128)(2,1)}), bf16[16,2,768]{2,1,0:T(2,128)(2,1)S(1)}, u32[]{:S(2)}, u32[]{:S(2)}) %all-to-all-start.4) | async-done | bytes 49184 | tf_op jit(solution)/shard_map/all_to_all | solution.py:55
  133.4 0.6 convert_bitcast_fusion
  (37 shorter events, 0.1 us)
Async XLA Ops:
  0.6 6.9 %copy-start = (bf16[1,256,1408]{2,1,0:T(8,128)(2,1)S(1)}, bf16[1,256,1408]{2,1,0:T(8,128)(2,1)}, u32[]{:S(2)}) copy-start(bf16[1,256,1408]{2,1,0:T(8,128)(2,1)} %param.7) | copy-start | bytes 2162692
  0.6 6.9 %copy-start.1 = (bf16[1,256,1408]{2,1,0:T(8,128)(2,1)S(1)}, bf16[1,256,1408]{2,1,0:T(8,128)(2,1)}, u32[]{:S(2)}) copy-start(bf16[1,256,1408]{2,1,0:T(8,128)(2,1)} %param.6) | copy-start | bytes 2162692
  0.7 6.9 %copy-start.11 = (bf16[1408,16]{0,1:T(8,128)(2,1)S(1)}, bf16[1408,16]{0,1:T(8,128)(2,1)}, u32[]{:S(2)}) copy-start(bf16[1408,16]{0,1:T(8,128)(2,1)} %param.9) | copy-start | bytes 135172
  2.1 25.6 %copy-start.15 = (bf16[384,1408]{1,0:T(8,128)(2,1)}, bf16[384,1408]{1,0:T(8,128)(2,1)S(1)}, u32[]{:S(2)}) copy-start(bf16[384,1408]{1,0:T(8,128)(2,1)S(1)} %pad_maximum_fusion.refs_1_) | copy-start | bytes 3244036
  2.1 25.6 %collective-permute-start = (bf16[384,1408]{1,0:T(8,128)(2,1)S(1)}, bf16[384,1408]{1,0:T(8,128)(2,1)S(1)}, u32[]{:S(2)}, u32[]{:S(2)}) collective-permute-start(bf16[384,1408]{1,0:T(8,128)(2,1)S(1)} %pad_maximum_fusion.refs_1_), channel_id=1, source_target_pairs={{0,256},{256,0},{1,257},{257,1},{2,258},{258,2},{3,259},{259,3},{4... | collective-permute-start | bytes 3244040 | tf_op jit(solution)/shard_map/ppermute | solution.py:213
  9.6 18.0 %copy-start.13 = (f32[16,256]{1,0:T(8,128)}, f32[16,256]{1,0:T(8,128)S(1)}, u32[]{:S(2)}) copy-start(f32[16,256]{1,0:T(8,128)S(1)} %get-tuple-element.35.combine) | copy-start | bytes 49156
  9.7 38.6 %all-to-all-start = ((bf16[128,2,1408]{2,1,0:T(2,128)(2,1)}), bf16[128,2,1408]{2,1,0:T(2,128)(2,1)S(1)}, u32[]{:S(2)}, u32[]{:S(2)}) async-start(bf16[128,2,1408]{2,1,0:T(2,128)(2,1)} %bitcast.3), calls=%async_computation | async-start | bytes 1441792 | tf_op jit(solution)/shard_map/all_to_all | solution.py:55
  27.7 20.6 %copy-start.14 = (bf16[384,1408]{1,0:T(8,128)(2,1)}, bf16[384,1408]{1,0:T(8,128)(2,1)S(1)}, u32[]{:S(2)}) copy-start(bf16[384,1408]{1,0:T(8,128)(2,1)S(1)} %shard_map.94.refs_2_) | copy-start | bytes 3244036
  27.7 20.6 %collective-permute-start.1 = (bf16[384,1408]{1,0:T(8,128)(2,1)S(1)}, bf16[384,1408]{1,0:T(8,128)(2,1)}, u32[]{:S(2)}, u32[]{:S(2)}) collective-permute-start(bf16[384,1408]{1,0:T(8,128)(2,1)S(1)} %pad_maximum_fusion.refs_1_), channel_id=1, source_target_pairs={{0,16},{16,0},{1,17},{17,1},{2,18},{18,2},{3,19},{19,3},{4,20},{20... | collective-permute-start | bytes 3244040 | tf_op jit(solution)/shard_map/ppermute | solution.py:215
  35.3 12.9 %collective-permute-start.2 = (bf16[384,1408]{1,0:T(8,128)(2,1)S(1)}, bf16[384,1408]{1,0:T(8,128)(2,1)}, u32[]{:S(2)}, u32[]{:S(2)}) collective-permute-start(bf16[384,1408]{1,0:T(8,128)(2,1)S(1)} %shard_map.94.refs_2_), channel_id=1, source_target_pairs={{0,16},{16,0},{1,17},{17,1},{2,18},{18,2},{3,19},{19,3},{4,20},{20... | collective-permute-start | bytes 3244040 | tf_op jit(solution)/shard_map/ppermute | solution.py:216
  48.2 0.9 copy-start.16
  55.3 18.4 %collective-permute-start.3 = (bf16[768,1408]{1,0:T(8,128)(2,1)}, bf16[768,1408]{1,0:T(8,128)(2,1)S(1)}, u32[]{:S(2)}, u32[]{:S(2)}) collective-permute-start(bf16[768,1408]{1,0:T(8,128)(2,1)} %get-tuple-element.32), channel_id=1, source_target_pairs={{0,16},{16,0},{1,17},{17,1},{2,18},{18,2},{3,19},{19,3},{4,20},{20... | collective-permute-start | bytes 6488072 | tf_op jit(solution)/shard_map/ppermute | solution.py:248
  61.0 28.2 %all-to-all-start.1 = ((bf16[128,2,768]{2,1,0:T(2,128)(2,1)}), bf16[128,2,768]{2,1,0:T(2,128)(2,1)S(1)}, u32[]{:S(2)}, u32[]{:S(2)}) async-start(bf16[128,2,768]{2,1,0:T(2,128)(2,1)} %get-tuple-element.27), calls=%async_computation.1 | async-start | bytes 786432 | tf_op jit(solution)/shard_map/all_to_all | solution.py:55
  73.7 1.0 copy-start.3
  74.6 1.0 copy-start.5
  75.6 0.9 copy-start.7
  76.6 0.9 copy-start.9
  78.9 10.3 %copy-start.2 = (bf16[1,256,1408]{2,1,0:T(8,128)(2,1)S(1)}, bf16[1,256,1408]{2,1,0:T(8,128)(2,1)}, u32[]{:S(2)}) copy-start(bf16[1,256,1408]{2,1,0:T(8,128)(2,1)} %param.6) | copy-start | bytes 2162692
  78.9 48.6 %collective-permute-start.4 = (bf16[384,1408]{1,0:T(8,128)(2,1)}, bf16[384,1408]{1,0:T(8,128)(2,1)}, u32[]{:S(2)}, u32[]{:S(2)}) collective-permute-start(bf16[384,1408]{1,0:T(8,128)(2,1)} %shard_map.96), channel_id=1, source_target_pairs={{0,256},{256,0},{1,257},{257,1},{2,258},{258,2},{3,259},{259,3},{4... | collective-permute-start | bytes 3244040 | tf_op jit(solution)/shard_map/ppermute | solution.py:256
  89.2 0.7 copy-start.12
  91.0 36.6 %copy-start.4 = (bf16[128,1408]{1,0:T(8,128)(2,1)S(1)}, bf16[128,1408]{1,0:T(8,128)(2,1)}, u32[]{:S(2)}) copy-start(bf16[128,1408]{1,0:T(8,128)(2,1)} %get-tuple-element.28.x_ref) | copy-start | bytes 1081348
  91.0 36.6 %copy-start.6 = (bf16[128,1408]{1,0:T(8,128)(2,1)S(1)}, bf16[128,1408]{1,0:T(8,128)(2,1)}, u32[]{:S(2)}) copy-start(bf16[128,1408]{1,0:T(8,128)(2,1)} %get-tuple-element.29.g_ref) | copy-start | bytes 1081348
  91.0 36.5 %copy-start.8 = (bf16[768,128]{1,0:T(8,128)(2,1)S(1)}, bf16[768,128]{1,0:T(8,128)(2,1)}, u32[]{:S(2)}) copy-start(bf16[768,128]{1,0:T(8,128)(2,1)} %get-tuple-element.30.act_ref) | copy-start | bytes 589828
  91.0 36.5 %copy-start.10 = (bf16[768,128]{1,0:T(8,128)(2,1)S(1)}, bf16[768,128]{1,0:T(8,128)(2,1)}, u32[]{:S(2)}) copy-start(bf16[768,128]{1,0:T(8,128)(2,1)} %get-tuple-element.31.slope_ref) | copy-start | bytes 589828
  120.8 12.6 %all-to-all-start.4 = ((bf16[16,2,768]{2,1,0:T(2,128)(2,1)}), bf16[16,2,768]{2,1,0:T(2,128)(2,1)S(1)}, u32[]{:S(2)}, u32[]{:S(2)}) async-start(bf16[16,2,768]{2,1,0:T(2,128)(2,1)} %broadcast_in_dim.23), calls=%async_computation.4 | async-start | bytes 98304 | tf_op jit(solution)/shard_map/all_to_all | solution.py:55

commit v7 on v6

--- a/solution.py
+++ b/solution.py
@@ -23,13 +23,13 @@
     return lax.dot_general(a, b, (contract, ((), ())), preferred_element_type=F32)
 
 
-def call(kernel, out, args, macs, hbm=False, scratch=(), aliases={}, limit=LIMIT):
+def call(kernel, out, args, macs, hbm=False, scratch=(), aliases={}, limit=LIMIT, out_place=None):
     place = pl.ANY if hbm else pltpu.VMEM
     return pl.pallas_call(
         kernel,
         out_shape=out,
         in_specs=[pl.BlockSpec(memory_space=place) for a in args],
-        out_specs=jax.tree.map(lambda _: pl.BlockSpec(memory_space=place), out),
+        out_specs=jax.tree.map(lambda _: out_place or pl.BlockSpec(memory_space=place), out),
         scratch_shapes=scratch,
         input_output_aliases=aliases,
         compiler_params=pltpu.CompilerParams(vmem_limit_bytes=limit),
@@ -150,27 +150,62 @@
         copy.wait()
 
 
-def block_grads(k, x_ref, g_ref, act_ref, slope_ref):
-    rows = pl.ds(192 * k, 192)
-    lift = dot(slope_ref[rows, :], x_ref[...], ((1,), (0,)))
-    drop = dot(act_ref[rows, :], g_ref[...], ((1,), (0,)))
-    return lift, drop
-
-
-def x_kernel(x_ref, g_ref, act_ref, slope_ref, core_ref, out_ref):
-    lift, drop = block_grads(1, x_ref, g_ref, act_ref, slope_ref)
-    out_ref[:192, :] = (lift + core_ref[384:576, :].astype(F32)).astype(BF16)
-    out_ref[192:, :] = (drop + core_ref[576:, :].astype(F32)).astype(BF16)
-
-
-def own_kernel(x_ref, g_ref, act_ref, slope_ref, core_ref, over_ref, lift_ref, drop_ref):
-    lift, drop = block_grads(0, x_ref, g_ref, act_ref, slope_ref)
-    lift_ref[...] = (
-        lift + core_ref[:192, :].astype(F32) + over_ref[:192, :].astype(F32)
-    ).astype(BF16)
-    drop_ref[...] = (
-        drop + core_ref[192:384, :].astype(F32) + over_ref[192:, :].astype(F32)
-    ).astype(BF16)
+def fetch(pairs, sems):
+    copies = [pltpu.make_async_copy(a, b, sems.at[k]) for k, (a, b) in enumerate(pairs)]
+    for copy in copies:
+        copy.start()
+    return copies
+
+
+def x_kernel(x_in, g_in, act_in, slope_in, core_in, out_ref, x, g, act, slope, core, sems):
+    rows = pl.ds(192, 192)
+    copies = fetch(
+        (
+            (slope_in.at[rows], slope),
+            (x_in, x),
+            (act_in.at[rows], act),
+            (g_in, g),
+            (core_in.at[pl.ds(384, 384)], core),
+        ),
+        sems,
+    )
+    copies[0].wait()
+    copies[1].wait()
+    lift = dot(slope[...], x[...], ((1,), (0,)))
+    copies[2].wait()
+    copies[3].wait()
+    drop = dot(act[...], g[...], ((1,), (0,)))
+    copies[4].wait()
+    out_ref[:192, :] = (lift + core[:192, :].astype(F32)).astype(BF16)
+    out_ref[192:, :] = (drop + core[192:, :].astype(F32)).astype(BF16)
+
+
+def own_kernel(
+    x_in, g_in, act_in, slope_in, core_in, over_in, lift_ref, drop_ref,
+    x, g, act, slope, core, over, sems,
+):
+    rows = pl.ds(0, 192)
+    copies = fetch(
+        (
+            (slope_in.at[rows], slope),
+            (x_in, x),
+            (act_in.at[rows], act),
+            (g_in, g),
+            (core_in.at[pl.ds(0, 384)], core),
+            (over_in, over),
+        ),
+        sems,
+    )
+    copies[0].wait()
+    copies[1].wait()
+    lift = dot(slope[...], x[...], ((1,), (0,)))
+    copies[2].wait()
+    copies[3].wait()
+    drop = dot(act[...], g[...], ((1,), (0,)))
+    copies[4].wait()
+    copies[5].wait()
+    lift_ref[...] = (lift + core[:192, :].astype(F32) + over[:192, :].astype(F32)).astype(BF16)
+    drop_ref[...] = (drop + core[192:, :].astype(F32) + over[192:, :].astype(F32)).astype(BF16)
 
 
 def combine_kernel(out_ref, cot, combine, grad_ref):
@@ -179,7 +214,10 @@
     grad_ref[...] = combine[...] * (grad - weighted)
 
 
-def image_kernel(returned, tok, par, dispatch, part, out, left_ref, right_ref):
+def image_kernel(
+    returned, tok, par, dispatch_in, part_in, out, left_ref, right_ref, dispatch, part, sems
+):
+    loads = fetch(((dispatch_in, dispatch), (part_in, part)), sems)
     head = tail = None
     for y in range(8):
         rows = pl.ds(16 * y, 16)
@@ -192,6 +230,8 @@
     right_ref[16:32, :] = par[...]
     right_ref[32:, :] = par[...]
     grad = dot(slot_grad, tok[...], ((1,), (1,)))
+    for load in loads:
+        load.wait()
     weighted = jnp.sum(grad * dispatch[...], axis=1, keepdims=True)
     logit = part[...] + dispatch[...] * (grad - weighted)
     high = logit.astype(BF16)
@@ -211,12 +251,12 @@
     lift, drop = lift_weight[0], drop_weight[0]
     own = jnp.concatenate([lift, drop], axis=0)
     over_x = hold(lax.ppermute(own, "xhi", SWAP))
-    over_x, own_later = lax.optimization_barrier((over_x, own))
-    over_core = lax.ppermute(own_later, "core", SWAP)
     over_both = lax.ppermute(over_x, "core", SWAP)
 
     params_t = slot_params.T
     sent, dispatch, combine = route(tokens, cotangent, params_t)
+    combine, own_later = lax.optimization_barrier((combine, own))
+    over_core = lax.ppermute(own_later, "core", SWAP)
     routed = exchange(sent.reshape(128, 2, 1408), HIDDEN)
     combine_part = call(
         combine_kernel,
@@ -246,12 +286,18 @@
     returned = exchange(backward, HIDDEN)
     rows = (inputs, upstream, activated, slopes)
     from_core = lax.ppermute(to_core, "core", SWAP)
+    vmem = pl.BlockSpec(memory_space=pltpu.VMEM)
+    quarter = [
+        pltpu.VMEM(size, BF16) for size in ((128, 1408),) * 2 + ((192, 128),) * 2 + ((384, 1408),)
+    ]
     to_x = call(
         x_kernel,
         (shape((384, 1408), BF16),),
         rows + (from_core,),
         2 * 192 * 128 * 1408,
-        limit=SMALL,
+        hbm=True,
+        out_place=vmem,
+        scratch=quarter + [pltpu.SemaphoreType.DMA((5,))],
     )[0]
     from_x = lax.ppermute(to_x, "xhi", SWAP)
     returned, to_x = lax.optimization_barrier((returned, to_x))
@@ -261,16 +307,20 @@
         (half, half),
         rows + (from_core, from_x),
         2 * 192 * 128 * 1408,
-        limit=SMALL,
-    )
-
-    local, left, right = call(
+        hbm=True,
+        out_place=vmem,
+        scratch=quarter + quarter[4:] + [pltpu.SemaphoreType.DMA((6,))],
+    )
+
+    local, left, right = pl.pallas_call(
         image_kernel,
-        (shape((16, 2, 768), BF16), shape((48, 256), BF16), shape((48, 1408), BF16)),
-        (returned, tokens, params_t, dispatch, combine_part),
-        3 * 16 * 256 * 1408,
-        limit=SMALL,
-    )
+        out_shape=(shape((16, 2, 768), BF16), shape((48, 256), BF16), shape((48, 1408), BF16)),
+        in_specs=[vmem] * 3 + [pl.BlockSpec(memory_space=pl.ANY)] * 2,
+        out_specs=(vmem,) * 3,
+        scratch_shapes=[pltpu.VMEM((16, 256), F32)] * 2 + [pltpu.SemaphoreType.DMA((2,))],
+        compiler_params=pltpu.CompilerParams(vmem_limit_bytes=SMALL),
+        cost_estimate=pl.CostEstimate(flops=4 * 10**7, bytes_accessed=2 * 10**6, transcendentals=0),
+    )(returned, tokens, params_t, dispatch, combine_part)
     by_slot = exchange(local, NEAR)
     by_slot = jnp.sum(by_slot.astype(F32), axis=0).astype(BF16)
     by_group = exchange(jnp.broadcast_to(by_slot[None], (32, 2, 768)), FAR)

time: 135 us -> 132 us (0.978)
  starting transfers between devices: 61 us -> 56.3 us
  waiting for transfers between devices: 18.4 us -> 21.6 us
  Pallas kernels: 15.3 us -> 17.6 us
  local copies, waits for them, and re-layouts: 6.15 us -> 3.9 us
  blocking collectives: 28 us -> 26.6 us
    ppermute x1, starting transfers between devices: 7.65 us -> 3.14 us  [shards(): over_core = lax.ppermute(own_later, 'core', SWAP)]
    all_to_all x3, waiting for transfers between devices: 17.9 us -> 21.6 us  [exchange(): return lax.all_to_all(blocks, axes, split_axis=0, concat_axis=0, tiled=True)]
    ppermute x1, starting transfers between devices: 1.92 us -> 4.37 us  [shards(): over_both = lax.ppermute(over_x, 'core', SWAP)]
    all_to_all x3, starting transfers between devices: 35.7 us -> 33.3 us  [exchange(): return lax.all_to_all(blocks, axes, split_axis=0, concat_axis=0, tiled=True)]
    unnamed x34 -> x16, local copies, waits for them, and re-layouts: 5.43 us -> 3.17 us
    all_to_all x2, blocking collectives: 28 us -> 26.6 us  [exchange(): return lax.all_to_all(blocks, axes, split_axis=0, concat_axis=0, tiled=True)]
    pallas_call x6 -> x5, Pallas kernels: 13.3 us -> 14.4 us  [call(): pl.pallas_call(kernel, out_shape=out, in_specs=[pl.BlockSpec(memory_space...]
  transfers between devices with their start and end apart: 8 -> 8, of which waited for: 4 -> 3; matrix products, arithmetic and copies ran while one was open for 2% -> 2% of each run, Pallas kernels for 7% -> 9%
where the time goes in v7:
time: 132 us; the launch traced here: 131 us
  starting transfers between devices  56.3 us (43%)
  blocking collectives  26.6 us (20%)
  waiting for transfers between devices  21.6 us (16%)
  Pallas kernels  17.6 us (13%)
  local copies, waits for them, and re-layouts  3.9 us (3%)
  other arithmetic  3.19 us (2%)
    all_to_all x3, starting transfers between devices, exchange(): return lax.all_to_all(blocks, axes, split_axis=0, concat_axis=0, tiled=True)  33.3 us
    all_to_all x2, blocking collectives, exchange(): return lax.all_to_all(blocks, axes, split_axis=0, concat_axis=0, tiled=True)  26.6 us
    all_to_all x3, waiting for transfers between devices, exchange(): return lax.all_to_all(blocks, axes, split_axis=0, concat_axis=0, tiled=True)  21.6 us
    pallas_call x5, Pallas kernels, call(): pl.pallas_call(kernel, out_shape=out, in_specs=[pl.BlockSpec(memory_space...  14.4 us
    ppermute x1, starting transfers between devices, shards(): from_core = lax.ppermute(to_core, 'core', SWAP)  5.69 us
    ppermute x1, starting transfers between devices, shards(): over_x = hold(lax.ppermute(own, 'xhi', SWAP))  5.47 us
    ppermute x1, starting transfers between devices, shards(): over_both = lax.ppermute(over_x, 'core', SWAP)  4.37 us
    ppermute x1, starting transfers between devices, shards(): from_x = lax.ppermute(to_x, 'xhi', SWAP)  4.36 us
  transfers between devices with their start and end apart: 8, of which 3 were waited for; matrix products, arithmetic and copies ran while one was open for 2% of the time, Pallas kernels for 9%

profile of v7, /device:TPU:1, one launch (start us, length us, event | category | flops | bytes accessed | tf_op | source)
XLA Modules:
  0.0 131.3 jit_solution(9984534186145451354)
XLA Ops:
  0.6 0.0 copy-start
  0.7 2.4 %pad_maximum_fusion.refs_1_ = bf16[384,1408]{1,0:T(8,128)(2,1)} fusion(bf16[192,1408]{1,0:T(8,128)(2,1)} %bitcast.25, bf16[192,1408]{1,0:T(8,128)(2,1)} %bitcast.26), kind=kLoop, calls=%fused_computation.2 | loop fusion | flops 2162688 | bytes 2162688 | tf_op jit(solution)/shard_map/concatenate | solution.py:252
  3.0 5.5 %collective-permute-start = (bf16[384,1408]{1,0:T(8,128)(2,1)}, bf16[384,1408]{1,0:T(8,128)(2,1)S(1)}, u32[]{:S(2)}, u32[]{:S(2)}) collective-permute-start(bf16[384,1408]{1,0:T(8,128)(2,1)} %pad_maximum_fusion.refs_1_), channel_id=1, source_target_pairs={{0,256},{256,0},{1,257},{257,1},{2,258},{258,2},{3,259},{259,3},{4... | collective-permute-start | bytes 3244040 | tf_op jit(solution)/shard_map/ppermute | solution.py:253
  8.6 2.0 %shard_map.93 = (bf16[8,16,2,1408]{3,2,1,0:T(2,128)(2,1)}, f32[16,256]{1,0:T(8,128)S(1)}, f32[16,256]{1,0:T(8,128)S(1)}) custom-call(bf16[256,1408]{1,0:T(8,128)(2,1)S(1)} %bitcast.21, bf16[256,1408]{1,0:T(8,128)(2,1)S(1)} %bitcast.20, bf16[16,1408]{1,0:T(8,128)(2,1)S(1)} %bitcast.23), custom_call_target="tpu_custom_call" | custom-call | flops 40000000 | bytes 3000000 | tf_op jit(solution)/shard_map/pallas_call | solution.py:81
  10.6 0.0 copy-start.4
  10.6 0.6 copy-done.4
  11.2 17.6 %all-to-all-start = ((bf16[128,2,1408]{2,1,0:T(2,128)(2,1)}), bf16[128,2,1408]{2,1,0:T(2,128)(2,1)S(1)}, u32[]{:S(2)}, u32[]{:S(2)}) async-start(bf16[128,2,1408]{2,1,0:T(2,128)(2,1)} %bitcast.3), calls=%async_computation | async-start | bytes 1441792 | tf_op jit(solution)/shard_map/all_to_all | solution.py:55
  28.8 3.1 %collective-permute-start.1 = (bf16[384,1408]{1,0:T(8,128)(2,1)}, bf16[384,1408]{1,0:T(8,128)(2,1)}, u32[]{:S(2)}, u32[]{:S(2)}) collective-permute-start(bf16[384,1408]{1,0:T(8,128)(2,1)} %pad_maximum_fusion.refs_1_), channel_id=1, source_target_pairs={{0,16},{16,0},{1,17},{17,1},{2,18},{18,2},{3,19},{19,3},{4,20},{20... | collective-permute-start | bytes 3244040 | tf_op jit(solution)/shard_map/ppermute | solution.py:259
  32.0 4.4 %collective-permute-start.2 = (bf16[384,1408]{1,0:T(8,128)(2,1)S(1)}, bf16[384,1408]{1,0:T(8,128)(2,1)}, u32[]{:S(2)}, u32[]{:S(2)}) collective-permute-start(bf16[384,1408]{1,0:T(8,128)(2,1)S(1)} %shard_map.94.refs_2_), channel_id=1, source_target_pairs={{0,16},{16,0},{1,17},{17,1},{2,18},{18,2},{3,19},{19,3},{4,20},{20... | collective-permute-start | bytes 3244040 | tf_op jit(solution)/shard_map/ppermute | solution.py:254
  36.3 13.4 %all-to-all-done.refs_0_ = bf16[128,2,1408]{2,1,0:T(2,128)(2,1)S(1)} async-done(((bf16[128,2,1408]{2,1,0:T(2,128)(2,1)}), bf16[128,2,1408]{2,1,0:T(2,128)(2,1)S(1)}, u32[]{:S(2)}, u32[]{:S(2)}) %all-to-all-start) | async-done | bytes 720928 | tf_op jit(solution)/shard_map/all_to_all | solution.py:55
  49.8 0.8 copy-done.7
  50.6 6.2 %shard_map.95 = (bf16[128,2,768]{2,1,0:T(2,128)(2,1)}, bf16[768,1408]{1,0:T(8,128)(2,1)}, bf16[768,128]{1,0:T(8,128)(2,1)}, bf16[768,128]{1,0:T(8,128)(2,1)}, bf...) custom-call(bf16[128,2,1408]{2,1,0:T(2,128)(2,1)} %copy-done.7, bf16[384,1408]{1,0:T(8,128)(2,1)} %pad_maximum_fusion.refs_1_, ...), custom_call_target="tpu_custom_call" | custom-call | flops 1384120320 | bytes 8716288 | tf_op jit(solution)/shard_map/pallas_call | solution.py:28
  56.8 5.7 %collective-permute-start.3 = (bf16[768,1408]{1,0:T(8,128)(2,1)}, bf16[768,1408]{1,0:T(8,128)(2,1)}, u32[]{:S(2)}, u32[]{:S(2)}) collective-permute-start(bf16[768,1408]{1,0:T(8,128)(2,1)} %get-tuple-element.32), channel_id=1, source_target_pairs={{0,16},{16,0},{1,17},{17,1},{2,18},{18,2},{3,19},{19,3},{4,20},{20... | collective-permute-start | bytes 6488072 | tf_op jit(solution)/shard_map/ppermute | solution.py:288
  62.5 10.2 %all-to-all-start.1 = ((bf16[128,2,768]{2,1,0:T(2,128)(2,1)}), bf16[128,2,768]{2,1,0:T(2,128)(2,1)S(1)}, u32[]{:S(2)}, u32[]{:S(2)}) async-start(bf16[128,2,768]{2,1,0:T(2,128)(2,1)} %get-tuple-element.27), calls=%async_computation.1 | async-start | bytes 786432 | tf_op jit(solution)/shard_map/all_to_all | solution.py:55
  72.7 3.0 %shard_map.96 = bf16[384,1408]{1,0:T(8,128)(2,1)} custom-call(bf16[128,1408]{1,0:T(8,128)(2,1)} %get-tuple-element.28.x_in, bf16[128,1408]{1,0:T(8,128)(2,1)} %get-tuple-element.29.g_in, bf16[768,128]{1,0:T(8,128)(2,1)} %get-tuple-element.30.act_in, bf16[768,128]{1,0:T(8,128)(2,1)} %get-tuple-element.31.slope_in, ...), custom_call_target="tpu_custom_call" | custom-call | flops 138412032 | bytes 4358144 | tf_op jit(solution)/shard_map/pallas_call | solution.py:28
  75.7 4.4 %collective-permute-start.4 = (bf16[384,1408]{1,0:T(8,128)(2,1)}, bf16[384,1408]{1,0:T(8,128)(2,1)S(1)}, u32[]{:S(2)}, u32[]{:S(2)}) collective-permute-start(bf16[384,1408]{1,0:T(8,128)(2,1)} %shard_map.96), channel_id=1, source_target_pairs={{0,256},{256,0},{1,257},{257,1},{2,258},{258,2},{3,259},{259,3},{4... | collective-permute-start | bytes 3244040 | tf_op jit(solution)/shard_map/ppermute | solution.py:302
  80.1 2.0 %shard_map.97.part_in = f32[16,256]{1,0:T(8,128)} custom-call(bf16[16,1408]{1,0:T(8,128)(2,1)} %bitcast.27, bf16[256,1408]{1,0:T(8,128)(2,1)} %bitcast.19, f32[16,256]{1,0:T(8,128)} %copy-done.4), custom_call_target="tpu_custom_call" | custom-call | flops 11534336 | bytes 798720 | tf_op jit(solution)/shard_map/pallas_call | solution.py:28
  82.1 6.6 %all-to-all-done.1.returned = bf16[128,2,768]{2,1,0:T(2,128)(2,1)S(1)} async-done(((bf16[128,2,768]{2,1,0:T(2,128)(2,1)}), bf16[128,2,768]{2,1,0:T(2,128)(2,1)S(1)}, u32[]{:S(2)}, u32[]{:S(2)}) %all-to-all-start.1) | async-done | bytes 393248 | tf_op jit(solution)/shard_map/all_to_all | solution.py:55
  88.7 0.7 copy-done.3
  89.4 1.1 shard_map.98
  90.5 12.7 %all_to_all.25 = bf16[16,2,768]{2,1,0:T(2,128)(2,1)S(1)} all-to-all(bf16[16,2,768]{2,1,0:T(2,128)(2,1)S(1)} %get-tuple-element.38), channel_id=1, replica_groups=mesh['xhi'=2,'y'=8,'core'=2,'z'=8,'xlo'=2] {'core','z'}, dimensions={0} | all-to-all | bytes 98304 | tf_op jit(solution)/shard_map/all_to_all | solution.py:55
  103.2 0.1 reduce_sum.24
  103.3 0.1 broadcast_in_dim.22
  103.3 13.9 %all_to_all.26 = bf16[32,2,768]{2,1,0:T(2,128)(2,1)S(1)} all-to-all(bf16[32,2,768]{2,1,0:T(2,128)(2,1)S(1)} %broadcast_in_dim.22), channel_id=1, replica_groups=mesh['xhi'=2,'y'=8,'core'=2,'z'=8,'xlo'=2] {'xhi','y','xlo'}, dimensions={0} | all-to-all | bytes 196608 | tf_op jit(solution)/shard_map/all_to_all | solution.py:55
  117.2 0.1 reduce_sum.25
  117.3 0.7 broadcast_in_dim.23
  118.0 5.5 %all-to-all-start.4 = ((bf16[16,2,768]{2,1,0:T(2,128)(2,1)}), bf16[16,2,768]{2,1,0:T(2,128)(2,1)S(1)}, u32[]{:S(2)}, u32[]{:S(2)}) async-start(bf16[16,2,768]{2,1,0:T(2,128)(2,1)} %broadcast_in_dim.23), calls=%async_computation.4 | async-start | bytes 98304 | tf_op jit(solution)/shard_map/all_to_all | solution.py:55
  123.5 1.2 fusion
  124.8 1.0 copy-done.6
  125.8 3.2 %shard_map.99 = (bf16[192,1408]{1,0:T(8,128)(2,1)}, bf16[192,1408]{1,0:T(8,128)(2,1)}) custom-call(bf16[128,1408]{1,0:T(8,128)(2,1)} %get-tuple-element.28.x_in, bf16[128,1408]{1,0:T(8,128)(2,1)} %get-tuple-element.29.g_in, bf16[768,128]{1,0:T(8,128)(2,1)} %get-tuple-element.30.act_in, bf16[768,128]{1,0:T(8,128)(2,1)} %get-tuple-element.31.slope_in, ...), custom_call_target="tpu_custom_call" | custom-call | flops 138412032 | bytes 5439488 | tf_op jit(solution)/shard_map/pallas_call | solution.py:28
  129.0 1.6 %all-to-all-done.4 = bf16[16,2,768]{2,1,0:T(2,128)(2,1)S(1)} async-done(((bf16[16,2,768]{2,1,0:T(2,128)(2,1)}), bf16[16,2,768]{2,1,0:T(2,128)(2,1)S(1)}, u32[]{:S(2)}, u32[]{:S(2)}) %all-to-all-start.4) | async-done | bytes 49184 | tf_op jit(solution)/shard_map/all_to_all | solution.py:55
  130.6 0.6 convert_bitcast_fusion
  (19 shorter events, 0.1 us)
Async XLA Ops:
  0.6 7.9 %copy-start = (bf16[1,256,1408]{2,1,0:T(8,128)(2,1)S(1)}, bf16[1,256,1408]{2,1,0:T(8,128)(2,1)}, u32[]{:S(2)}) copy-start(bf16[1,256,1408]{2,1,0:T(8,128)(2,1)} %param.7) | copy-start | bytes 2162692
  0.6 7.9 %copy-start.1 = (bf16[1,256,1408]{2,1,0:T(8,128)(2,1)S(1)}, bf16[1,256,1408]{2,1,0:T(8,128)(2,1)}, u32[]{:S(2)}) copy-start(bf16[1,256,1408]{2,1,0:T(8,128)(2,1)} %param.6) | copy-start | bytes 2162692
  0.7 7.9 %copy-start.2 = (bf16[1408,16]{0,1:T(8,128)(2,1)S(1)}, bf16[1408,16]{0,1:T(8,128)(2,1)}, u32[]{:S(2)}) copy-start(bf16[1408,16]{0,1:T(8,128)(2,1)} %param.9) | copy-start | bytes 135172
  3.0 28.9 %collective-permute-start = (bf16[384,1408]{1,0:T(8,128)(2,1)}, bf16[384,1408]{1,0:T(8,128)(2,1)S(1)}, u32[]{:S(2)}, u32[]{:S(2)}) collective-permute-start(bf16[384,1408]{1,0:T(8,128)(2,1)} %pad_maximum_fusion.refs_1_), channel_id=1, source_target_pairs={{0,256},{256,0},{1,257},{257,1},{2,258},{258,2},{3,259},{259,3},{4... | collective-permute-start | bytes 3244040 | tf_op jit(solution)/shard_map/ppermute | solution.py:253
  10.6 0.6 copy-start.4
  11.2 38.6 %all-to-all-start = ((bf16[128,2,1408]{2,1,0:T(2,128)(2,1)}), bf16[128,2,1408]{2,1,0:T(2,128)(2,1)S(1)}, u32[]{:S(2)}, u32[]{:S(2)}) async-start(bf16[128,2,1408]{2,1,0:T(2,128)(2,1)} %bitcast.3), calls=%async_computation | async-start | bytes 1441792 | tf_op jit(solution)/shard_map/all_to_all | solution.py:55
  28.8 7.6 %collective-permute-start.1 = (bf16[384,1408]{1,0:T(8,128)(2,1)}, bf16[384,1408]{1,0:T(8,128)(2,1)}, u32[]{:S(2)}, u32[]{:S(2)}) collective-permute-start(bf16[384,1408]{1,0:T(8,128)(2,1)} %pad_maximum_fusion.refs_1_), channel_id=1, source_target_pairs={{0,16},{16,0},{1,17},{17,1},{2,18},{18,2},{3,19},{19,3},{4,20},{20... | collective-permute-start | bytes 3244040 | tf_op jit(solution)/shard_map/ppermute | solution.py:259
  31.9 17.8 %copy-start.5 = (bf16[384,1408]{1,0:T(8,128)(2,1)}, bf16[384,1408]{1,0:T(8,128)(2,1)S(1)}, u32[]{:S(2)}) copy-start(bf16[384,1408]{1,0:T(8,128)(2,1)S(1)} %shard_map.94.refs_2_) | copy-start | bytes 3244036
  32.0 17.8 %collective-permute-start.2 = (bf16[384,1408]{1,0:T(8,128)(2,1)S(1)}, bf16[384,1408]{1,0:T(8,128)(2,1)}, u32[]{:S(2)}, u32[]{:S(2)}) collective-permute-start(bf16[384,1408]{1,0:T(8,128)(2,1)S(1)} %shard_map.94.refs_2_), channel_id=1, source_target_pairs={{0,16},{16,0},{1,17},{17,1},{2,18},{18,2},{3,19},{19,3},{4,20},{20... | collective-permute-start | bytes 3244040 | tf_op jit(solution)/shard_map/ppermute | solution.py:254
  49.8 0.9 copy-start.7
  56.8 15.9 %collective-permute-start.3 = (bf16[768,1408]{1,0:T(8,128)(2,1)}, bf16[768,1408]{1,0:T(8,128)(2,1)}, u32[]{:S(2)}, u32[]{:S(2)}) collective-permute-start(bf16[768,1408]{1,0:T(8,128)(2,1)} %get-tuple-element.32), channel_id=1, source_target_pairs={{0,16},{16,0},{1,17},{17,1},{2,18},{18,2},{3,19},{19,3},{4,20},{20... | collective-permute-start | bytes 6488072 | tf_op jit(solution)/shard_map/ppermute | solution.py:288
  62.5 26.2 %all-to-all-start.1 = ((bf16[128,2,768]{2,1,0:T(2,128)(2,1)}), bf16[128,2,768]{2,1,0:T(2,128)(2,1)S(1)}, u32[]{:S(2)}, u32[]{:S(2)}) async-start(bf16[128,2,768]{2,1,0:T(2,128)(2,1)} %get-tuple-element.27), calls=%async_computation.1 | async-start | bytes 786432 | tf_op jit(solution)/shard_map/all_to_all | solution.py:55
  75.7 49.1 %collective-permute-start.4 = (bf16[384,1408]{1,0:T(8,128)(2,1)}, bf16[384,1408]{1,0:T(8,128)(2,1)S(1)}, u32[]{:S(2)}, u32[]{:S(2)}) collective-permute-start(bf16[384,1408]{1,0:T(8,128)(2,1)} %shard_map.96), channel_id=1, source_target_pairs={{0,256},{256,0},{1,257},{257,1},{2,258},{258,2},{3,259},{259,3},{4... | collective-permute-start | bytes 3244040 | tf_op jit(solution)/shard_map/ppermute | solution.py:302
  88.7 0.7 copy-start.3
  118.0 12.6 %all-to-all-start.4 = ((bf16[16,2,768]{2,1,0:T(2,128)(2,1)}), bf16[16,2,768]{2,1,0:T(2,128)(2,1)S(1)}, u32[]{:S(2)}, u32[]{:S(2)}) async-start(bf16[16,2,768]{2,1,0:T(2,128)(2,1)} %broadcast_in_dim.23), calls=%async_computation.4 | async-start | bytes 98304 | tf_op jit(solution)/shard_map/all_to_all | solution.py:55
  124.8 1.0 copy-start.6

commit v8 on v7

--- a/solution.py
+++ b/solution.py
@@ -255,8 +255,9 @@
 
     params_t = slot_params.T
     sent, dispatch, combine = route(tokens, cotangent, params_t)
-    combine, own_later = lax.optimization_barrier((combine, own))
-    over_core = lax.ppermute(own_later, "core", SWAP)
+    combine, lift, drop = lax.optimization_barrier((combine, lift, drop))
+    own = jnp.concatenate([lift, drop], axis=0)
+    over_core = lax.ppermute(own, "core", SWAP)
     routed = exchange(sent.reshape(128, 2, 1408), HIDDEN)
     combine_part = call(
         combine_kernel,
@@ -265,6 +266,7 @@
         16 * 256 * 1408,
     )[0]
 
+    routed, combine_part = lax.optimization_barrier((routed, combine_part))
     units = shape((768, 128), BF16)
     images = shape((128, 1408), BF16)
     core_half = shape((768, 1408), BF16)

time: 132 us -> 131 us (level)
  starting transfers between devices: 56.3 us -> 54.3 us
    ppermute x1, starting transfers between devices: 4.37 us -> 1.92 us  [shards(): over_both = lax.ppermute(over_x, 'core', SWAP)]
    unnamed x16 -> x21, local copies, waits for them, and re-layouts: 3.17 us -> 3.42 us
  transfers between devices with their start and end apart: 8 -> 8, of which waited for: 3 -> 3; matrix products, arithmetic and copies ran while one was open for 2% -> 3% of each run, Pallas kernels for 9% -> 9%
where the time goes in v8:
time: 131 us
  starting transfers between devices  54.3 us (41%)
  blocking collectives  27.1 us (21%)
  waiting for transfers between devices  21.4 us (16%)
  Pallas kernels  17.6 us (13%)
  local copies, waits for them, and re-layouts  4.99 us (4%)
  other arithmetic  3.2 us (2%)
    all_to_all x3, starting transfers between devices, exchange(): return lax.all_to_all(blocks, axes, split_axis=0, concat_axis=0, tiled=True)  33.7 us
    all_to_all x2, blocking collectives, exchange(): return lax.all_to_all(blocks, axes, split_axis=0, concat_axis=0, tiled=True)  27.1 us
    all_to_all x3, waiting for transfers between devices, exchange(): return lax.all_to_all(blocks, axes, split_axis=0, concat_axis=0, tiled=True)  21.4 us
    pallas_call x5, Pallas kernels, call(): pl.pallas_call(kernel, out_shape=out, in_specs=[pl.BlockSpec(memory_space...  14.4 us
    ppermute x1, starting transfers between devices, shards(): from_core = lax.ppermute(to_core, 'core', SWAP)  5.7 us
    ppermute x1, starting transfers between devices, shards(): over_x = hold(lax.ppermute(own, 'xhi', SWAP))  5.47 us
    ppermute x1, starting transfers between devices, shards(): from_x = lax.ppermute(to_x, 'xhi', SWAP)  4.36 us
    unnamed x21, local copies, waits for them, and re-layouts  3.42 us
  transfers between devices with their start and end apart: 8, of which 3 were waited for; matrix products, arithmetic and copies ran while one was open for 3% of the time, Pallas kernels for 9%

profile of v8, /device:TPU:1, one launch (start us, length us, event | category | flops | bytes accessed | tf_op | source)
XLA Modules:
  0.0 130.7 jit_solution(5594554824335141859)
XLA Ops:
  0.6 0.0 copy-start
  0.7 2.4 %pad_maximum_fusion = bf16[384,1408]{1,0:T(8,128)(2,1)} fusion(bf16[192,1408]{1,0:T(8,128)(2,1)} %bitcast.27, bf16[192,1408]{1,0:T(8,128)(2,1)} %bitcast.25), kind=kLoop, calls=%fused_computation.2 | loop fusion | flops 2162688 | bytes 2162688 | tf_op jit(solution)/shard_map/concatenate | solution.py:252
  3.1 5.5 %collective-permute-start = (bf16[384,1408]{1,0:T(8,128)(2,1)}, bf16[384,1408]{1,0:T(8,128)(2,1)S(1)}, u32[]{:S(2)}, u32[]{:S(2)}) collective-permute-start(bf16[384,1408]{1,0:T(8,128)(2,1)} %pad_maximum_fusion), channel_id=1, source_target_pairs={{0,256},{256,0},{1,257},{257,1},{2,258},{258,2},{3,259},{259,3},{4... | collective-permute-start | bytes 3244040 | tf_op jit(solution)/shard_map/ppermute | solution.py:253
  8.6 2.0 %shard_map.93 = (bf16[8,16,2,1408]{3,2,1,0:T(2,128)(2,1)}, f32[16,256]{1,0:T(8,128)S(1)}, f32[16,256]{1,0:T(8,128)S(1)}) custom-call(bf16[256,1408]{1,0:T(8,128)(2,1)S(1)} %bitcast.21, bf16[256,1408]{1,0:T(8,128)(2,1)S(1)} %bitcast.20, bf16[16,1408]{1,0:T(8,128)(2,1)S(1)} %bitcast.23), custom_call_target="tpu_custom_call" | custom-call | flops 40000000 | bytes 3000000 | tf_op jit(solution)/shard_map/pallas_call | solution.py:81
  10.6 0.6 copy-done.4
  11.2 18.2 %all-to-all-start = ((bf16[128,2,1408]{2,1,0:T(2,128)(2,1)}), bf16[128,2,1408]{2,1,0:T(2,128)(2,1)}, u32[]{:S(2)}, u32[]{:S(2)}) async-start(bf16[128,2,1408]{2,1,0:T(2,128)(2,1)} %bitcast.3), calls=%async_computation | async-start | bytes 1441792 | tf_op jit(solution)/shard_map/all_to_all | solution.py:55
  29.4 0.8 constant_dynamic-update-slice_fusion.1
  30.2 0.8 constant_dynamic-update-slice_fusion.refs_1_
  31.1 3.1 %collective-permute-start.1 = (bf16[384,1408]{1,0:T(8,128)(2,1)}, bf16[384,1408]{1,0:T(8,128)(2,1)S(1)}, u32[]{:S(2)}, u32[]{:S(2)}) collective-permute-start(bf16[384,1408]{1,0:T(8,128)(2,1)} %constant_dynamic-update-slice_fusion.refs_1_), channel_id=1, source_target_pairs={{0,16},{16,0},{1,17},{17,1},{2,18},{18,2},{3,19},{19,3},{4,20},{20... | collective-permute-start | bytes 3244040 | tf_op jit(solution)/shard_map/ppermute | solution.py:260
  34.3 1.9 %collective-permute-start.2 = (bf16[384,1408]{1,0:T(8,128)(2,1)S(1)}, bf16[384,1408]{1,0:T(8,128)(2,1)}, u32[]{:S(2)}, u32[]{:S(2)}) collective-permute-start(bf16[384,1408]{1,0:T(8,128)(2,1)S(1)} %shard_map.95.refs_2_), channel_id=1, source_target_pairs={{0,16},{16,0},{1,17},{17,1},{2,18},{18,2},{3,19},{19,3},{4,20},{20... | collective-permute-start | bytes 3244040 | tf_op jit(solution)/shard_map/ppermute | solution.py:254
  36.2 2.0 %shard_map.94.part_in = f32[16,256]{1,0:T(8,128)} custom-call(bf16[16,1408]{1,0:T(8,128)(2,1)} %bitcast.29, bf16[256,1408]{1,0:T(8,128)(2,1)} %bitcast.19, f32[16,256]{1,0:T(8,128)} %copy-done.4), custom_call_target="tpu_custom_call" | custom-call | flops 11534336 | bytes 798720 | tf_op jit(solution)/shard_map/pallas_call | solution.py:28
  38.2 11.8 %all-to-all-done.refs_0_ = bf16[128,2,1408]{2,1,0:T(2,128)(2,1)} async-done(((bf16[128,2,1408]{2,1,0:T(2,128)(2,1)}), bf16[128,2,1408]{2,1,0:T(2,128)(2,1)}, u32[]{:S(2)}, u32[]{:S(2)}) %all-to-all-start) | async-done | bytes 720928 | tf_op jit(solution)/shard_map/all_to_all | solution.py:55
  50.0 0.9 copy-done.9
  51.0 6.2 %shard_map.96 = (bf16[128,2,768]{2,1,0:T(2,128)(2,1)}, bf16[768,1408]{1,0:T(8,128)(2,1)}, bf16[768,128]{1,0:T(8,128)(2,1)}, bf16[768,128]{1,0:T(8,128)(2,1)}, bf...) custom-call(bf16[128,2,1408]{2,1,0:T(2,128)(2,1)} %all-to-all-done.refs_0_, ...), custom_call_target="tpu_custom_call" | custom-call | flops 1384120320 | bytes 8716288 | tf_op jit(solution)/shard_map/pallas_call | solution.py:28
  57.2 5.7 %collective-permute-start.3 = (bf16[768,1408]{1,0:T(8,128)(2,1)}, bf16[768,1408]{1,0:T(8,128)(2,1)}, u32[]{:S(2)}, u32[]{:S(2)}) collective-permute-start(bf16[768,1408]{1,0:T(8,128)(2,1)} %get-tuple-element.38), channel_id=1, source_target_pairs={{0,16},{16,0},{1,17},{17,1},{2,18},{18,2},{3,19},{19,3},{4,20},{20... | collective-permute-start | bytes 6488072 | tf_op jit(solution)/shard_map/ppermute | solution.py:290
  62.9 10.0 %all-to-all-start.1 = ((bf16[128,2,768]{2,1,0:T(2,128)(2,1)}), bf16[128,2,768]{2,1,0:T(2,128)(2,1)S(1)}, u32[]{:S(2)}, u32[]{:S(2)}) async-start(bf16[128,2,768]{2,1,0:T(2,128)(2,1)} %get-tuple-element.33), calls=%async_computation.1 | async-start | bytes 786432 | tf_op jit(solution)/shard_map/all_to_all | solution.py:55
  73.0 3.0 %shard_map.97 = bf16[384,1408]{1,0:T(8,128)(2,1)} custom-call(bf16[128,1408]{1,0:T(8,128)(2,1)} %get-tuple-element.34.x_in, bf16[128,1408]{1,0:T(8,128)(2,1)} %get-tuple-element.35.g_in, bf16[768,128]{1,0:T(8,128)(2,1)} %get-tuple-element.36.act_in, bf16[768,128]{1,0:T(8,128)(2,1)} %get-tuple-element.37.slope_in, ...), custom_call_target="tpu_custom_call" | custom-call | flops 138412032 | bytes 4358144 | tf_op jit(solution)/shard_map/pallas_call | solution.py:28
  75.9 4.4 %collective-permute-start.4 = (bf16[384,1408]{1,0:T(8,128)(2,1)}, bf16[384,1408]{1,0:T(8,128)(2,1)S(1)}, u32[]{:S(2)}, u32[]{:S(2)}) collective-permute-start(bf16[384,1408]{1,0:T(8,128)(2,1)} %shard_map.97), channel_id=1, source_target_pairs={{0,256},{256,0},{1,257},{257,1},{2,258},{258,2},{3,259},{259,3},{4... | collective-permute-start | bytes 3244040 | tf_op jit(solution)/shard_map/ppermute | solution.py:304
  80.3 8.1 %all-to-all-done.1.returned = bf16[128,2,768]{2,1,0:T(2,128)(2,1)S(1)} async-done(((bf16[128,2,768]{2,1,0:T(2,128)(2,1)}), bf16[128,2,768]{2,1,0:T(2,128)(2,1)S(1)}, u32[]{:S(2)}, u32[]{:S(2)}) %all-to-all-start.1) | async-done | bytes 393248 | tf_op jit(solution)/shard_map/all_to_all | solution.py:55
  88.4 1.1 shard_map.98
  89.5 13.2 %all_to_all.25 = bf16[16,2,768]{2,1,0:T(2,128)(2,1)S(1)} all-to-all(bf16[16,2,768]{2,1,0:T(2,128)(2,1)S(1)} %get-tuple-element.44), channel_id=1, replica_groups=mesh['xhi'=2,'y'=8,'core'=2,'z'=8,'xlo'=2] {'core','z'}, dimensions={0} | all-to-all | bytes 98304 | tf_op jit(solution)/shard_map/all_to_all | solution.py:55
  102.7 0.1 reduce_sum.24
  102.8 0.1 broadcast_in_dim.22
  102.8 13.8 %all_to_all.26 = bf16[32,2,768]{2,1,0:T(2,128)(2,1)S(1)} all-to-all(bf16[32,2,768]{2,1,0:T(2,128)(2,1)S(1)} %broadcast_in_dim.22), channel_id=1, replica_groups=mesh['xhi'=2,'y'=8,'core'=2,'z'=8,'xlo'=2] {'xhi','y','xlo'}, dimensions={0} | all-to-all | bytes 196608 | tf_op jit(solution)/shard_map/all_to_all | solution.py:55
  116.7 0.1 reduce_sum.25
  116.8 0.7 broadcast_in_dim.23
  117.4 5.5 %all-to-all-start.4 = ((bf16[16,2,768]{2,1,0:T(2,128)(2,1)}), bf16[16,2,768]{2,1,0:T(2,128)(2,1)S(1)}, u32[]{:S(2)}, u32[]{:S(2)}) async-start(bf16[16,2,768]{2,1,0:T(2,128)(2,1)} %broadcast_in_dim.23), calls=%async_computation.4 | async-start | bytes 98304 | tf_op jit(solution)/shard_map/all_to_all | solution.py:55
  123.0 1.2 fusion
  124.2 1.0 copy-done.8
  125.2 3.2 %shard_map.99 = (bf16[192,1408]{1,0:T(8,128)(2,1)}, bf16[192,1408]{1,0:T(8,128)(2,1)}) custom-call(bf16[128,1408]{1,0:T(8,128)(2,1)} %get-tuple-element.34.x_in, bf16[128,1408]{1,0:T(8,128)(2,1)} %get-tuple-element.35.g_in, bf16[768,128]{1,0:T(8,128)(2,1)} %get-tuple-element.36.act_in, bf16[768,128]{1,0:T(8,128)(2,1)} %get-tuple-element.37.slope_in, ...), custom_call_target="tpu_custom_call" | custom-call | flops 138412032 | bytes 5439488 | tf_op jit(solution)/shard_map/pallas_call | solution.py:28
  128.5 1.6 %all-to-all-done.4 = bf16[16,2,768]{2,1,0:T(2,128)(2,1)S(1)} async-done(((bf16[16,2,768]{2,1,0:T(2,128)(2,1)}), bf16[16,2,768]{2,1,0:T(2,128)(2,1)S(1)}, u32[]{:S(2)}, u32[]{:S(2)}) %all-to-all-start.4) | async-done | bytes 49184 | tf_op jit(solution)/shard_map/all_to_all | solution.py:55
  130.1 0.6 convert_bitcast_fusion
  (25 shorter events, 0.1 us)
Async XLA Ops:
  0.6 7.9 %copy-start = (bf16[1,256,1408]{2,1,0:T(8,128)(2,1)S(1)}, bf16[1,256,1408]{2,1,0:T(8,128)(2,1)}, u32[]{:S(2)}) copy-start(bf16[1,256,1408]{2,1,0:T(8,128)(2,1)} %param.7) | copy-start | bytes 2162692
  0.6 7.9 %copy-start.1 = (bf16[1,256,1408]{2,1,0:T(8,128)(2,1)S(1)}, bf16[1,256,1408]{2,1,0:T(8,128)(2,1)}, u32[]{:S(2)}) copy-start(bf16[1,256,1408]{2,1,0:T(8,128)(2,1)} %param.6) | copy-start | bytes 2162692
  0.7 7.9 %copy-start.2 = (bf16[1408,16]{0,1:T(8,128)(2,1)S(1)}, bf16[1408,16]{0,1:T(8,128)(2,1)}, u32[]{:S(2)}) copy-start(bf16[1408,16]{0,1:T(8,128)(2,1)} %param.9) | copy-start | bytes 135172
  3.1 31.2 %collective-permute-start = (bf16[384,1408]{1,0:T(8,128)(2,1)}, bf16[384,1408]{1,0:T(8,128)(2,1)S(1)}, u32[]{:S(2)}, u32[]{:S(2)}) collective-permute-start(bf16[384,1408]{1,0:T(8,128)(2,1)} %pad_maximum_fusion), channel_id=1, source_target_pairs={{0,256},{256,0},{1,257},{257,1},{2,258},{258,2},{3,259},{259,3},{4... | collective-permute-start | bytes 3244040 | tf_op jit(solution)/shard_map/ppermute | solution.py:253
  10.6 0.6 copy-start.4
  11.2 18.2 %copy-start.6 = (bf16[1,192,1408]{2,1,0:T(8,128)(2,1)S(1)}, bf16[1,192,1408]{2,1,0:T(8,128)(2,1)}, u32[]{:S(2)}) copy-start(bf16[1,192,1408]{2,1,0:T(8,128)(2,1)} %param.10) | copy-start | bytes 1622020
  11.2 19.0 %copy-start.7 = (bf16[1,192,1408]{2,1,0:T(8,128)(2,1)S(1)}, bf16[1,192,1408]{2,1,0:T(8,128)(2,1)}, u32[]{:S(2)}) copy-start(bf16[1,192,1408]{2,1,0:T(8,128)(2,1)} %param.11) | copy-start | bytes 1622020
  11.2 38.8 %all-to-all-start = ((bf16[128,2,1408]{2,1,0:T(2,128)(2,1)}), bf16[128,2,1408]{2,1,0:T(2,128)(2,1)}, u32[]{:S(2)}, u32[]{:S(2)}) async-start(bf16[128,2,1408]{2,1,0:T(2,128)(2,1)} %bitcast.3), calls=%async_computation | async-start | bytes 1441792 | tf_op jit(solution)/shard_map/all_to_all | solution.py:55
  31.1 18.9 %collective-permute-start.1 = (bf16[384,1408]{1,0:T(8,128)(2,1)}, bf16[384,1408]{1,0:T(8,128)(2,1)S(1)}, u32[]{:S(2)}, u32[]{:S(2)}) collective-permute-start(bf16[384,1408]{1,0:T(8,128)(2,1)} %constant_dynamic-update-slice_fusion.refs_1_), channel_id=1, source_target_pairs={{0,16},{16,0},{1,17},{17,1},{2,18},{18,2},{3,19},{19,3},{4,20},{20... | collective-permute-start | bytes 3244040 | tf_op jit(solution)/shard_map/ppermute | solution.py:260
  34.3 15.8 %copy-start.5 = (bf16[384,1408]{1,0:T(8,128)(2,1)}, bf16[384,1408]{1,0:T(8,128)(2,1)S(1)}, u32[]{:S(2)}) copy-start(bf16[384,1408]{1,0:T(8,128)(2,1)S(1)} %shard_map.95.refs_2_) | copy-start | bytes 3244036
  34.3 15.8 %collective-permute-start.2 = (bf16[384,1408]{1,0:T(8,128)(2,1)S(1)}, bf16[384,1408]{1,0:T(8,128)(2,1)}, u32[]{:S(2)}, u32[]{:S(2)}) collective-permute-start(bf16[384,1408]{1,0:T(8,128)(2,1)S(1)} %shard_map.95.refs_2_), channel_id=1, source_target_pairs={{0,16},{16,0},{1,17},{17,1},{2,18},{18,2},{3,19},{19,3},{4,20},{20... | collective-permute-start | bytes 3244040 | tf_op jit(solution)/shard_map/ppermute | solution.py:254
  50.0 1.0 copy-start.9
  57.2 15.8 %collective-permute-start.3 = (bf16[768,1408]{1,0:T(8,128)(2,1)}, bf16[768,1408]{1,0:T(8,128)(2,1)}, u32[]{:S(2)}, u32[]{:S(2)}) collective-permute-start(bf16[768,1408]{1,0:T(8,128)(2,1)} %get-tuple-element.38), channel_id=1, source_target_pairs={{0,16},{16,0},{1,17},{17,1},{2,18},{18,2},{3,19},{19,3},{4,20},{20... | collective-permute-start | bytes 6488072 | tf_op jit(solution)/shard_map/ppermute | solution.py:290
  62.9 25.5 %all-to-all-start.1 = ((bf16[128,2,768]{2,1,0:T(2,128)(2,1)}), bf16[128,2,768]{2,1,0:T(2,128)(2,1)S(1)}, u32[]{:S(2)}, u32[]{:S(2)}) async-start(bf16[128,2,768]{2,1,0:T(2,128)(2,1)} %get-tuple-element.33), calls=%async_computation.1 | async-start | bytes 786432 | tf_op jit(solution)/shard_map/all_to_all | solution.py:55
  73.0 15.4 %copy-start.3 = (f32[16,256]{1,0:T(8,128)S(1)}, f32[16,256]{1,0:T(8,128)}, u32[]{:S(2)}) copy-start(f32[16,256]{1,0:T(8,128)} %shard_map.94.part_in) | copy-start | bytes 49156
  75.9 48.3 %collective-permute-start.4 = (bf16[384,1408]{1,0:T(8,128)(2,1)}, bf16[384,1408]{1,0:T(8,128)(2,1)S(1)}, u32[]{:S(2)}, u32[]{:S(2)}) collective-permute-start(bf16[384,1408]{1,0:T(8,128)(2,1)} %shard_map.97), channel_id=1, source_target_pairs={{0,256},{256,0},{1,257},{257,1},{2,258},{258,2},{3,259},{259,3},{4... | collective-permute-start | bytes 3244040 | tf_op jit(solution)/shard_map/ppermute | solution.py:304
  117.4 12.6 %all-to-all-start.4 = ((bf16[16,2,768]{2,1,0:T(2,128)(2,1)}), bf16[16,2,768]{2,1,0:T(2,128)(2,1)S(1)}, u32[]{:S(2)}, u32[]{:S(2)}) async-start(bf16[16,2,768]{2,1,0:T(2,128)(2,1)} %broadcast_in_dim.23), calls=%async_computation.4 | async-start | bytes 98304 | tf_op jit(solution)/shard_map/all_to_all | solution.py:55
  124.2 1.0 copy-start.8

commit v9 on v8

--- a/solution.py
+++ b/solution.py
@@ -39,6 +39,14 @@
             transcendentals=0,
         ),
     )(*args)
+
+
+def join_kernel(lift, drop, out, sems):
+    copies = fetch(
+        ((lift, out.at[pl.ds(0, 192)]), (drop, out.at[pl.ds(192, 192)])), sems
+    )
+    for copy in copies:
+        copy.wait()
 
 
 def hold_kernel(src_ref, dst_ref):
@@ -121,9 +129,10 @@
     store(x, x_out)
     store(g, g_out)
     for k in order:
-        part = pl.ds(192 * k, 192)
         for load in loads[k]:
             load.wait()
+    for k in order:
+        part = pl.ds(192 * k, 192)
         preact = dot(lifts[part, :], x[...], ((1,), (1,)))
         activated_grad = dot(drops[part, :], g[...], ((1,), (1,)))
         rise = 0.5 * (1.0 + lax.erf(preact * 0.7071067811865476))
@@ -249,14 +258,20 @@
 def shards(tokens, cotangent, slot_outputs, slot_params, lift_weight, drop_weight):
     tokens, cotangent, slot_outputs = tokens[0], cotangent[0], slot_outputs[0]
     lift, drop = lift_weight[0], drop_weight[0]
-    own = jnp.concatenate([lift, drop], axis=0)
+    own = call(
+        join_kernel,
+        (shape((384, 1408), BF16),),
+        (lift, drop),
+        0,
+        hbm=True,
+        scratch=[pltpu.SemaphoreType.DMA((2,))],
+    )[0]
     over_x = hold(lax.ppermute(own, "xhi", SWAP))
     over_both = lax.ppermute(over_x, "core", SWAP)
 
     params_t = slot_params.T
     sent, dispatch, combine = route(tokens, cotangent, params_t)
-    combine, lift, drop = lax.optimization_barrier((combine, lift, drop))
-    own = jnp.concatenate([lift, drop], axis=0)
+    combine, own = lax.optimization_barrier((combine, own))
     over_core = lax.ppermute(own, "core", SWAP)
     routed = exchange(sent.reshape(128, 2, 1408), HIDDEN)
     combine_part = call(

time: 131 us -> 162 us (1.24)
  Pallas kernels: 17.6 us -> 51.2 us
  local copies, waits for them, and re-layouts: 4.99 us -> 2.34 us
  starting transfers between devices: 54.3 us -> 56.7 us
  other arithmetic: 3.2 us -> 0.81 us
    pallas_call x5 -> x6, Pallas kernels: 14.4 us -> 48.1 us  [call(): pl.pallas_call(kernel, out_shape=out, in_specs=[pl.BlockSpec(memory_space...]
    concatenate x1 -> x0, other arithmetic: 2.39 us -> none  [shards(): own = jnp.concatenate([lift, drop], axis=0)]
    unnamed x21 -> x16, local copies, waits for them, and re-layouts: 3.42 us -> 1.62 us
    ppermute x1, starting transfers between devices: 1.92 us -> 3.57 us  [shards(): over_both = lax.ppermute(over_x, 'core', SWAP)]
  transfers between devices with their start and end apart: 8 -> 8, of which waited for: 3 -> 3; matrix products, arithmetic and copies ran while one was open for 3% -> 1% of each run, Pallas kernels for 9% -> 7%
where the time goes in v9:
time: 162 us
  starting transfers between devices  56.7 us (35%)
  Pallas kernels  51.2 us (32%)
  blocking collectives  26.6 us (16%)
  waiting for transfers between devices  22 us (14%)
  local copies, waits for them, and re-layouts  2.34 us (1%)
    pallas_call x6, Pallas kernels, call(): pl.pallas_call(kernel, out_shape=out, in_specs=[pl.BlockSpec(memory_space...  48.1 us
    all_to_all x3, starting transfers between devices, exchange(): return lax.all_to_all(blocks, axes, split_axis=0, concat_axis=0, tiled=True)  34.5 us
    all_to_all x2, blocking collectives, exchange(): return lax.all_to_all(blocks, axes, split_axis=0, concat_axis=0, tiled=True)  26.6 us
    all_to_all x3, waiting for transfers between devices, exchange(): return lax.all_to_all(blocks, axes, split_axis=0, concat_axis=0, tiled=True)  22 us
    ppermute x1, starting transfers between devices, shards(): from_core = lax.ppermute(to_core, 'core', SWAP)  5.71 us
    ppermute x1, starting transfers between devices, shards(): over_x = hold(lax.ppermute(own, 'xhi', SWAP))  5.48 us
    ppermute x1, starting transfers between devices, shards(): from_x = lax.ppermute(to_x, 'xhi', SWAP)  4.34 us
    ppermute x1, starting transfers between devices, shards(): over_both = lax.ppermute(over_x, 'core', SWAP)  3.57 us
  transfers between devices with their start and end apart: 8, of which 3 were waited for; matrix products, arithmetic and copies ran while one was open for 1% of the time, Pallas kernels for 7%

profile of v9, /device:TPU:1, one launch (start us, length us, event | category | flops | bytes accessed | tf_op | source)
XLA Modules:
  0.0 161.8 jit_solution(16394536080389600970)
XLA Ops:
  0.6 0.0 copy-start
  0.7 33.9 %shard_map.94.refs_1_ = bf16[384,1408]{1,0:T(8,128)(2,1)} custom-call(bf16[192,1408]{1,0:T(8,128)(2,1)} %bitcast.25, bf16[192,1408]{1,0:T(8,128)(2,1)} %bitcast.26), custom_call_target="tpu_custom_call" | custom-call | bytes 2162688 | tf_op jit(solution)/shard_map/pallas_call | solution.py:28
  34.5 5.5 %collective-permute-start = (bf16[384,1408]{1,0:T(8,128)(2,1)}, bf16[384,1408]{1,0:T(8,128)(2,1)S(1)}, u32[]{:S(2)}, u32[]{:S(2)}) collective-permute-start(bf16[384,1408]{1,0:T(8,128)(2,1)} %shard_map.94.refs_1_), channel_id=1, source_target_pairs={{0,256},{256,0},{1,257},{257,1},{2,258},{258,2},{3,259},{259,3},{4... | collective-permute-start | bytes 3244040 | tf_op jit(solution)/shard_map/ppermute | solution.py:269
  40.1 2.0 %shard_map.93 = (bf16[8,16,2,1408]{3,2,1,0:T(2,128)(2,1)}, f32[16,256]{1,0:T(8,128)S(1)}, f32[16,256]{1,0:T(8,128)S(1)}) custom-call(bf16[256,1408]{1,0:T(8,128)(2,1)S(1)} %bitcast.21, bf16[256,1408]{1,0:T(8,128)(2,1)S(1)} %bitcast.20, bf16[16,1408]{1,0:T(8,128)(2,1)S(1)} %bitcast.23), custom_call_target="tpu_custom_call" | custom-call | flops 40000000 | bytes 3000000 | tf_op jit(solution)/shard_map/pallas_call | solution.py:89
  42.1 0.0 copy-start.4
  42.1 0.6 copy-done.4
  42.7 18.2 %all-to-all-start = ((bf16[128,2,1408]{2,1,0:T(2,128)(2,1)}), bf16[128,2,1408]{2,1,0:T(2,128)(2,1)}, u32[]{:S(2)}, u32[]{:S(2)}) async-start(bf16[128,2,1408]{2,1,0:T(2,128)(2,1)} %bitcast.3), calls=%async_computation | async-start | bytes 1441792 | tf_op jit(solution)/shard_map/all_to_all | solution.py:63
  60.9 3.1 %collective-permute-start.1 = (bf16[384,1408]{1,0:T(8,128)(2,1)S(1)}, bf16[384,1408]{1,0:T(8,128)(2,1)}, u32[]{:S(2)}, u32[]{:S(2)}) collective-permute-start(bf16[384,1408]{1,0:T(8,128)(2,1)S(1)} %copy-done.6), channel_id=1, source_target_pairs={{0,16},{16,0},{1,17},{17,1},{2,18},{18,2},{3,19},{19,3},{4,20},{20... | collective-permute-start | bytes 3244040 | tf_op jit(solution)/shard_map/ppermute | solution.py:275
  64.0 0.0 collective-permute-done.src_ref
  64.1 3.6 %collective-permute-start.2 = (bf16[384,1408]{1,0:T(8,128)(2,1)S(1)}, bf16[384,1408]{1,0:T(8,128)(2,1)}, u32[]{:S(2)}, u32[]{:S(2)}) collective-permute-start(bf16[384,1408]{1,0:T(8,128)(2,1)S(1)} %shard_map.96.refs_2_), channel_id=1, source_target_pairs={{0,16},{16,0},{1,17},{17,1},{2,18},{18,2},{3,19},{19,3},{4,20},{20... | collective-permute-start | bytes 3244040 | tf_op jit(solution)/shard_map/ppermute | solution.py:270
  67.7 2.0 %shard_map.95.part_in = f32[16,256]{1,0:T(8,128)} custom-call(bf16[16,1408]{1,0:T(8,128)(2,1)} %bitcast.27, bf16[256,1408]{1,0:T(8,128)(2,1)} %bitcast.19, f32[16,256]{1,0:T(8,128)} %copy-done.4), custom_call_target="tpu_custom_call" | custom-call | flops 11534336 | bytes 798720 | tf_op jit(solution)/shard_map/pallas_call | solution.py:28
  69.7 11.8 %all-to-all-done.refs_0_ = bf16[128,2,1408]{2,1,0:T(2,128)(2,1)} async-done(((bf16[128,2,1408]{2,1,0:T(2,128)(2,1)}), bf16[128,2,1408]{2,1,0:T(2,128)(2,1)}, u32[]{:S(2)}, u32[]{:S(2)}) %all-to-all-start) | async-done | bytes 720928 | tf_op jit(solution)/shard_map/all_to_all | solution.py:63
  81.5 6.0 %shard_map.97 = (bf16[128,2,768]{2,1,0:T(2,128)(2,1)}, bf16[768,1408]{1,0:T(8,128)(2,1)}, bf16[768,128]{1,0:T(8,128)(2,1)}, bf16[768,128]{1,0:T(8,128)(2,1)}, bf...) custom-call(bf16[128,2,1408]{2,1,0:T(2,128)(2,1)} %all-to-all-done.refs_0_, bf16[384,1408]{1,0:T(8,128)(2,1)} %shard_map.94.refs_1_, ...), custom_call_target="tpu_custom_call" | custom-call | flops 1384120320 | bytes 8716288 | tf_op jit(solution)/shard_map/pallas_call | solution.py:28
  87.5 5.7 %collective-permute-start.3 = (bf16[768,1408]{1,0:T(8,128)(2,1)}, bf16[768,1408]{1,0:T(8,128)(2,1)}, u32[]{:S(2)}, u32[]{:S(2)}) collective-permute-start(bf16[768,1408]{1,0:T(8,128)(2,1)} %get-tuple-element.36), channel_id=1, source_target_pairs={{0,16},{16,0},{1,17},{17,1},{2,18},{18,2},{3,19},{19,3},{4,20},{20... | collective-permute-start | bytes 6488072 | tf_op jit(solution)/shard_map/ppermute | solution.py:305
  93.2 10.8 %all-to-all-start.1 = ((bf16[128,2,768]{2,1,0:T(2,128)(2,1)}), bf16[128,2,768]{2,1,0:T(2,128)(2,1)S(1)}, u32[]{:S(2)}, u32[]{:S(2)}) async-start(bf16[128,2,768]{2,1,0:T(2,128)(2,1)} %get-tuple-element.31), calls=%async_computation.1 | async-start | bytes 786432 | tf_op jit(solution)/shard_map/all_to_all | solution.py:63
  104.0 0.0 copy-start.3
  104.0 3.0 %shard_map.98 = bf16[384,1408]{1,0:T(8,128)(2,1)} custom-call(bf16[128,1408]{1,0:T(8,128)(2,1)} %get-tuple-element.32.x_in, bf16[128,1408]{1,0:T(8,128)(2,1)} %get-tuple-element.33.g_in, bf16[768,128]{1,0:T(8,128)(2,1)} %get-tuple-element.34.act_in, bf16[768,128]{1,0:T(8,128)(2,1)} %get-tuple-element.35.slope_in, ...), custom_call_target="tpu_custom_call" | custom-call | flops 138412032 | bytes 4358144 | tf_op jit(solution)/shard_map/pallas_call | solution.py:28
  107.0 4.3 %collective-permute-start.4 = (bf16[384,1408]{1,0:T(8,128)(2,1)}, bf16[384,1408]{1,0:T(8,128)(2,1)S(1)}, u32[]{:S(2)}, u32[]{:S(2)}) collective-permute-start(bf16[384,1408]{1,0:T(8,128)(2,1)} %shard_map.98), channel_id=1, source_target_pairs={{0,256},{256,0},{1,257},{257,1},{2,258},{258,2},{3,259},{259,3},{4... | collective-permute-start | bytes 3244040 | tf_op jit(solution)/shard_map/ppermute | solution.py:319
  111.4 8.6 %all-to-all-done.1.returned = bf16[128,2,768]{2,1,0:T(2,128)(2,1)S(1)} async-done(((bf16[128,2,768]{2,1,0:T(2,128)(2,1)}), bf16[128,2,768]{2,1,0:T(2,128)(2,1)S(1)}, u32[]{:S(2)}, u32[]{:S(2)}) %all-to-all-start.1) | async-done | bytes 393248 | tf_op jit(solution)/shard_map/all_to_all | solution.py:63
  120.0 1.1 shard_map.99
  121.1 12.7 %all_to_all.25 = bf16[16,2,768]{2,1,0:T(2,128)(2,1)S(1)} all-to-all(bf16[16,2,768]{2,1,0:T(2,128)(2,1)S(1)} %get-tuple-element.42), channel_id=1, replica_groups=mesh['xhi'=2,'y'=8,'core'=2,'z'=8,'xlo'=2] {'core','z'}, dimensions={0} | all-to-all | bytes 98304 | tf_op jit(solution)/shard_map/all_to_all | solution.py:63
  133.8 0.1 reduce_sum.24
  133.8 0.1 broadcast_in_dim.22
  133.9 13.9 %all_to_all.26 = bf16[32,2,768]{2,1,0:T(2,128)(2,1)S(1)} all-to-all(bf16[32,2,768]{2,1,0:T(2,128)(2,1)S(1)} %broadcast_in_dim.22), channel_id=1, replica_groups=mesh['xhi'=2,'y'=8,'core'=2,'z'=8,'xlo'=2] {'xhi','y','xlo'}, dimensions={0} | all-to-all | bytes 196608 | tf_op jit(solution)/shard_map/all_to_all | solution.py:63
  147.8 0.1 reduce_sum.25
  147.9 0.7 broadcast_in_dim.23
  148.5 5.5 %all-to-all-start.4 = ((bf16[16,2,768]{2,1,0:T(2,128)(2,1)}), bf16[16,2,768]{2,1,0:T(2,128)(2,1)S(1)}, u32[]{:S(2)}, u32[]{:S(2)}) async-start(bf16[16,2,768]{2,1,0:T(2,128)(2,1)} %broadcast_in_dim.23), calls=%async_computation.4 | async-start | bytes 98304 | tf_op jit(solution)/shard_map/all_to_all | solution.py:63
  154.1 1.2 fusion
  155.3 1.0 copy-done.7
  156.3 3.2 %shard_map.100 = (bf16[192,1408]{1,0:T(8,128)(2,1)}, bf16[192,1408]{1,0:T(8,128)(2,1)}) custom-call(bf16[128,1408]{1,0:T(8,128)(2,1)} %get-tuple-element.32.x_in, bf16[128,1408]{1,0:T(8,128)(2,1)} %get-tuple-element.33.g_in, bf16[768,128]{1,0:T(8,128)(2,1)} %get-tuple-element.34.act_in, bf16[768,128]{1,0:T(8,128)(2,1)} %get-tuple-element.35.slope_in, ...), custom_call_target="tpu_custom_call" | custom-call | flops 138412032 | bytes 5439488 | tf_op jit(solution)/shard_map/pallas_call | solution.py:28
  159.5 1.6 all-to-all-done.4
  161.2 0.6 convert_bitcast_fusion
  (19 shorter events, 0.1 us)
Async XLA Ops:
  0.6 39.4 %copy-start = (bf16[1,256,1408]{2,1,0:T(8,128)(2,1)S(1)}, bf16[1,256,1408]{2,1,0:T(8,128)(2,1)}, u32[]{:S(2)}) copy-start(bf16[1,256,1408]{2,1,0:T(8,128)(2,1)} %param.7) | copy-start | bytes 2162692
  0.6 39.4 %copy-start.1 = (bf16[1,256,1408]{2,1,0:T(8,128)(2,1)S(1)}, bf16[1,256,1408]{2,1,0:T(8,128)(2,1)}, u32[]{:S(2)}) copy-start(bf16[1,256,1408]{2,1,0:T(8,128)(2,1)} %param.6) | copy-start | bytes 2162692
  0.7 39.4 %copy-start.2 = (bf16[1408,16]{0,1:T(8,128)(2,1)S(1)}, bf16[1408,16]{0,1:T(8,128)(2,1)}, u32[]{:S(2)}) copy-start(bf16[1408,16]{0,1:T(8,128)(2,1)} %param.9) | copy-start | bytes 135172
  34.5 29.5 %collective-permute-start = (bf16[384,1408]{1,0:T(8,128)(2,1)}, bf16[384,1408]{1,0:T(8,128)(2,1)S(1)}, u32[]{:S(2)}, u32[]{:S(2)}) collective-permute-start(bf16[384,1408]{1,0:T(8,128)(2,1)} %shard_map.94.refs_1_), channel_id=1, source_target_pairs={{0,256},{256,0},{1,257},{257,1},{2,258},{258,2},{3,259},{259,3},{4... | collective-permute-start | bytes 3244040 | tf_op jit(solution)/shard_map/ppermute | solution.py:269
  42.1 0.6 copy-start.4
  42.7 18.2 %copy-start.6 = (bf16[384,1408]{1,0:T(8,128)(2,1)S(1)}, bf16[384,1408]{1,0:T(8,128)(2,1)}, u32[]{:S(2)}) copy-start(bf16[384,1408]{1,0:T(8,128)(2,1)} %shard_map.94.refs_1_) | copy-start | bytes 3244036
  42.7 38.8 %all-to-all-start = ((bf16[128,2,1408]{2,1,0:T(2,128)(2,1)}), bf16[128,2,1408]{2,1,0:T(2,128)(2,1)}, u32[]{:S(2)}, u32[]{:S(2)}) async-start(bf16[128,2,1408]{2,1,0:T(2,128)(2,1)} %bitcast.3), calls=%async_computation | async-start | bytes 1441792 | tf_op jit(solution)/shard_map/all_to_all | solution.py:63
  60.9 20.6 %collective-permute-start.1 = (bf16[384,1408]{1,0:T(8,128)(2,1)S(1)}, bf16[384,1408]{1,0:T(8,128)(2,1)}, u32[]{:S(2)}, u32[]{:S(2)}) collective-permute-start(bf16[384,1408]{1,0:T(8,128)(2,1)S(1)} %copy-done.6), channel_id=1, source_target_pairs={{0,16},{16,0},{1,17},{17,1},{2,18},{18,2},{3,19},{19,3},{4,20},{20... | collective-permute-start | bytes 3244040 | tf_op jit(solution)/shard_map/ppermute | solution.py:275
  64.1 17.5 %copy-start.5 = (bf16[384,1408]{1,0:T(8,128)(2,1)}, bf16[384,1408]{1,0:T(8,128)(2,1)S(1)}, u32[]{:S(2)}) copy-start(bf16[384,1408]{1,0:T(8,128)(2,1)S(1)} %shard_map.96.refs_2_) | copy-start | bytes 3244036
  64.1 17.4 %collective-permute-start.2 = (bf16[384,1408]{1,0:T(8,128)(2,1)S(1)}, bf16[384,1408]{1,0:T(8,128)(2,1)}, u32[]{:S(2)}, u32[]{:S(2)}) collective-permute-start(bf16[384,1408]{1,0:T(8,128)(2,1)S(1)} %shard_map.96.refs_2_), channel_id=1, source_target_pairs={{0,16},{16,0},{1,17},{17,1},{2,18},{18,2},{3,19},{19,3},{4,20},{20... | collective-permute-start | bytes 3244040 | tf_op jit(solution)/shard_map/ppermute | solution.py:270
  87.5 16.5 %collective-permute-start.3 = (bf16[768,1408]{1,0:T(8,128)(2,1)}, bf16[768,1408]{1,0:T(8,128)(2,1)}, u32[]{:S(2)}, u32[]{:S(2)}) collective-permute-start(bf16[768,1408]{1,0:T(8,128)(2,1)} %get-tuple-element.36), channel_id=1, source_target_pairs={{0,16},{16,0},{1,17},{17,1},{2,18},{18,2},{3,19},{19,3},{4,20},{20... | collective-permute-start | bytes 6488072 | tf_op jit(solution)/shard_map/ppermute | solution.py:305
  93.2 26.8 %all-to-all-start.1 = ((bf16[128,2,768]{2,1,0:T(2,128)(2,1)}), bf16[128,2,768]{2,1,0:T(2,128)(2,1)S(1)}, u32[]{:S(2)}, u32[]{:S(2)}) async-start(bf16[128,2,768]{2,1,0:T(2,128)(2,1)} %get-tuple-element.31), calls=%async_computation.1 | async-start | bytes 786432 | tf_op jit(solution)/shard_map/all_to_all | solution.py:63
  104.0 16.0 %copy-start.3 = (f32[16,256]{1,0:T(8,128)S(1)}, f32[16,256]{1,0:T(8,128)}, u32[]{:S(2)}) copy-start(f32[16,256]{1,0:T(8,128)} %shard_map.95.part_in) | copy-start | bytes 49156
  107.0 48.3 %collective-permute-start.4 = (bf16[384,1408]{1,0:T(8,128)(2,1)}, bf16[384,1408]{1,0:T(8,128)(2,1)S(1)}, u32[]{:S(2)}, u32[]{:S(2)}) collective-permute-start(bf16[384,1408]{1,0:T(8,128)(2,1)} %shard_map.98), channel_id=1, source_target_pairs={{0,256},{256,0},{1,257},{257,1},{2,258},{258,2},{3,259},{259,3},{4... | collective-permute-start | bytes 3244040 | tf_op jit(solution)/shard_map/ppermute | solution.py:319
  148.5 12.6 %all-to-all-start.4 = ((bf16[16,2,768]{2,1,0:T(2,128)(2,1)}), bf16[16,2,768]{2,1,0:T(2,128)(2,1)S(1)}, u32[]{:S(2)}, u32[]{:S(2)}) async-start(bf16[16,2,768]{2,1,0:T(2,128)(2,1)} %broadcast_in_dim.23), calls=%async_computation.4 | async-start | bytes 98304 | tf_op jit(solution)/shard_map/all_to_all | solution.py:63
  155.3 1.0 copy-start.7

commit v10 on v9

--- a/solution.py
+++ b/solution.py
@@ -41,12 +41,16 @@
     )(*args)
 
 
-def join_kernel(lift, drop, out, sems):
-    copies = fetch(
-        ((lift, out.at[pl.ds(0, 192)]), (drop, out.at[pl.ds(192, 192)])), sems
-    )
-    for copy in copies:
-        copy.wait()
+def join_kernel(lift, drop, out, rows, sems):
+    top, bottom = pl.ds(0, 192), pl.ds(192, 192)
+    loads = fetch(((lift, rows.at[top]), (drop, rows.at[bottom])), sems)
+    stores = []
+    for k, part in enumerate((top, bottom)):
+        loads[k].wait()
+        stores.append(pltpu.make_async_copy(rows.at[part], out.at[part], sems.at[2 + k]))
+        stores[k].start()
+    for store in stores:
+        store.wait()
 
 
 def hold_kernel(src_ref, dst_ref):
@@ -264,7 +268,7 @@
         (lift, drop),
         0,
         hbm=True,
-        scratch=[pltpu.SemaphoreType.DMA((2,))],
+        scratch=[pltpu.VMEM((384, 1408), BF16), pltpu.SemaphoreType.DMA((4,))],
     )[0]
     over_x = hold(lax.ppermute(own, "xhi", SWAP))
     over_both = lax.ppermute(over_x, "core", SWAP)

time: 162 us -> 131 us (0.81)
  Pallas kernels: 51.2 us -> 19.5 us
    pallas_call x6, Pallas kernels: 48.1 us -> 16.4 us  [call(): pl.pallas_call(kernel, out_shape=out, in_specs=[pl.BlockSpec(memory_space...]
  transfers between devices with their start and end apart: 8 -> 8, of which waited for: 3 -> 3; matrix products, arithmetic and copies ran while one was open for 1% -> 2% of each run, Pallas kernels for 7% -> 9%
where the time goes in v10:
time: 131 us; the launch traced here: 130 us
  starting transfers between devices  56.7 us (43%)
  blocking collectives  26.6 us (20%)
  waiting for transfers between devices  22 us (17%)
  Pallas kernels  19.5 us (15%)
  local copies, waits for them, and re-layouts  2.34 us (2%)
    all_to_all x3, starting transfers between devices, exchange(): return lax.all_to_all(blocks, axes, split_axis=0, concat_axis=0, tiled=True)  34.5 us
    all_to_all x2, blocking collectives, exchange(): return lax.all_to_all(blocks, axes, split_axis=0, concat_axis=0, tiled=True)  26.6 us
    all_to_all x3, waiting for transfers between devices, exchange(): return lax.all_to_all(blocks, axes, split_axis=0, concat_axis=0, tiled=True)  22 us
    pallas_call x6, Pallas kernels, call(): pl.pallas_call(kernel, out_shape=out, in_specs=[pl.BlockSpec(memory_space...  16.4 us
    ppermute x1, starting transfers between devices, shards(): from_core = lax.ppermute(to_core, 'core', SWAP)  5.69 us
    ppermute x1, starting transfers between devices, shards(): over_x = hold(lax.ppermute(own, 'xhi', SWAP))  5.48 us
    ppermute x1, starting transfers between devices, shards(): from_x = lax.ppermute(to_x, 'xhi', SWAP)  4.36 us
    ppermute x1, starting transfers between devices, shards(): over_both = lax.ppermute(over_x, 'core', SWAP)  3.57 us
  transfers between devices with their start and end apart: 8, of which 3 were waited for; matrix products, arithmetic and copies ran while one was open for 2% of the time, Pallas kernels for 9%

profile of v10, /device:TPU:1, one launch (start us, length us, event | category | flops | bytes accessed | tf_op | source)
XLA Modules:
  0.0 130.1 jit_solution(17599023710454288522)
XLA Ops:
  0.6 0.0 copy-start
  0.7 2.2 %shard_map.94.refs_1_ = bf16[384,1408]{1,0:T(8,128)(2,1)} custom-call(bf16[192,1408]{1,0:T(8,128)(2,1)} %bitcast.25, bf16[192,1408]{1,0:T(8,128)(2,1)} %bitcast.26), custom_call_target="tpu_custom_call" | custom-call | bytes 2162688 | tf_op jit(solution)/shard_map/pallas_call | solution.py:28
  2.8 5.5 %collective-permute-start = (bf16[384,1408]{1,0:T(8,128)(2,1)}, bf16[384,1408]{1,0:T(8,128)(2,1)S(1)}, u32[]{:S(2)}, u32[]{:S(2)}) collective-permute-start(bf16[384,1408]{1,0:T(8,128)(2,1)} %shard_map.94.refs_1_), channel_id=1, source_target_pairs={{0,256},{256,0},{1,257},{257,1},{2,258},{258,2},{3,259},{259,3},{4... | collective-permute-start | bytes 3244040 | tf_op jit(solution)/shard_map/ppermute | solution.py:273
  8.4 2.0 %shard_map.93 = (bf16[8,16,2,1408]{3,2,1,0:T(2,128)(2,1)}, f32[16,256]{1,0:T(8,128)S(1)}, f32[16,256]{1,0:T(8,128)S(1)}) custom-call(bf16[256,1408]{1,0:T(8,128)(2,1)S(1)} %bitcast.21, bf16[256,1408]{1,0:T(8,128)(2,1)S(1)} %bitcast.20, bf16[16,1408]{1,0:T(8,128)(2,1)S(1)} %bitcast.23), custom_call_target="tpu_custom_call" | custom-call | flops 40000000 | bytes 3000000 | tf_op jit(solution)/shard_map/pallas_call | solution.py:93
  10.4 0.0 copy-start.4
  10.4 0.6 copy-done.4
  11.0 18.2 %all-to-all-start = ((bf16[128,2,1408]{2,1,0:T(2,128)(2,1)}), bf16[128,2,1408]{2,1,0:T(2,128)(2,1)}, u32[]{:S(2)}, u32[]{:S(2)}) async-start(bf16[128,2,1408]{2,1,0:T(2,128)(2,1)} %bitcast.3), calls=%async_computation | async-start | bytes 1441792 | tf_op jit(solution)/shard_map/all_to_all | solution.py:67
  29.2 3.1 %collective-permute-start.1 = (bf16[384,1408]{1,0:T(8,128)(2,1)S(1)}, bf16[384,1408]{1,0:T(8,128)(2,1)}, u32[]{:S(2)}, u32[]{:S(2)}) collective-permute-start(bf16[384,1408]{1,0:T(8,128)(2,1)S(1)} %copy-done.6), channel_id=1, source_target_pairs={{0,16},{16,0},{1,17},{17,1},{2,18},{18,2},{3,19},{19,3},{4,20},{20... | collective-permute-start | bytes 3244040 | tf_op jit(solution)/shard_map/ppermute | solution.py:279
  32.4 0.0 collective-permute-done.src_ref
  32.4 3.6 %collective-permute-start.2 = (bf16[384,1408]{1,0:T(8,128)(2,1)S(1)}, bf16[384,1408]{1,0:T(8,128)(2,1)}, u32[]{:S(2)}, u32[]{:S(2)}) collective-permute-start(bf16[384,1408]{1,0:T(8,128)(2,1)S(1)} %shard_map.96.refs_2_), channel_id=1, source_target_pairs={{0,16},{16,0},{1,17},{17,1},{2,18},{18,2},{3,19},{19,3},{4,20},{20... | collective-permute-start | bytes 3244040 | tf_op jit(solution)/shard_map/ppermute | solution.py:274
  36.0 2.0 %shard_map.95.part_in = f32[16,256]{1,0:T(8,128)} custom-call(bf16[16,1408]{1,0:T(8,128)(2,1)} %bitcast.27, bf16[256,1408]{1,0:T(8,128)(2,1)} %bitcast.19, f32[16,256]{1,0:T(8,128)} %copy-done.4), custom_call_target="tpu_custom_call" | custom-call | flops 11534336 | bytes 798720 | tf_op jit(solution)/shard_map/pallas_call | solution.py:28
  38.0 11.8 %all-to-all-done.refs_0_ = bf16[128,2,1408]{2,1,0:T(2,128)(2,1)} async-done(((bf16[128,2,1408]{2,1,0:T(2,128)(2,1)}), bf16[128,2,1408]{2,1,0:T(2,128)(2,1)}, u32[]{:S(2)}, u32[]{:S(2)}) %all-to-all-start) | async-done | bytes 720928 | tf_op jit(solution)/shard_map/all_to_all | solution.py:67
  49.8 6.0 %shard_map.97 = (bf16[128,2,768]{2,1,0:T(2,128)(2,1)}, bf16[768,1408]{1,0:T(8,128)(2,1)}, bf16[768,128]{1,0:T(8,128)(2,1)}, bf16[768,128]{1,0:T(8,128)(2,1)}, bf...) custom-call(bf16[128,2,1408]{2,1,0:T(2,128)(2,1)} %all-to-all-done.refs_0_, bf16[384,1408]{1,0:T(8,128)(2,1)} %shard_map.94.refs_1_, ...), custom_call_target="tpu_custom_call" | custom-call | flops 1384120320 | bytes 8716288 | tf_op jit(solution)/shard_map/pallas_call | solution.py:28
  55.8 5.7 %collective-permute-start.3 = (bf16[768,1408]{1,0:T(8,128)(2,1)}, bf16[768,1408]{1,0:T(8,128)(2,1)}, u32[]{:S(2)}, u32[]{:S(2)}) collective-permute-start(bf16[768,1408]{1,0:T(8,128)(2,1)} %get-tuple-element.36), channel_id=1, source_target_pairs={{0,16},{16,0},{1,17},{17,1},{2,18},{18,2},{3,19},{19,3},{4,20},{20... | collective-permute-start | bytes 6488072 | tf_op jit(solution)/shard_map/ppermute | solution.py:309
  61.5 10.8 %all-to-all-start.1 = ((bf16[128,2,768]{2,1,0:T(2,128)(2,1)}), bf16[128,2,768]{2,1,0:T(2,128)(2,1)S(1)}, u32[]{:S(2)}, u32[]{:S(2)}) async-start(bf16[128,2,768]{2,1,0:T(2,128)(2,1)} %get-tuple-element.31), calls=%async_computation.1 | async-start | bytes 786432 | tf_op jit(solution)/shard_map/all_to_all | solution.py:67
  72.3 0.0 copy-start.3
  72.3 3.0 %shard_map.98 = bf16[384,1408]{1,0:T(8,128)(2,1)} custom-call(bf16[128,1408]{1,0:T(8,128)(2,1)} %get-tuple-element.32.x_in, bf16[128,1408]{1,0:T(8,128)(2,1)} %get-tuple-element.33.g_in, bf16[768,128]{1,0:T(8,128)(2,1)} %get-tuple-element.34.act_in, bf16[768,128]{1,0:T(8,128)(2,1)} %get-tuple-element.35.slope_in, ...), custom_call_target="tpu_custom_call" | custom-call | flops 138412032 | bytes 4358144 | tf_op jit(solution)/shard_map/pallas_call | solution.py:28
  75.3 4.4 %collective-permute-start.4 = (bf16[384,1408]{1,0:T(8,128)(2,1)}, bf16[384,1408]{1,0:T(8,128)(2,1)S(1)}, u32[]{:S(2)}, u32[]{:S(2)}) collective-permute-start(bf16[384,1408]{1,0:T(8,128)(2,1)} %shard_map.98), channel_id=1, source_target_pairs={{0,256},{256,0},{1,257},{257,1},{2,258},{258,2},{3,259},{259,3},{4... | collective-permute-start | bytes 3244040 | tf_op jit(solution)/shard_map/ppermute | solution.py:323
  79.7 8.6 %all-to-all-done.1.returned = bf16[128,2,768]{2,1,0:T(2,128)(2,1)S(1)} async-done(((bf16[128,2,768]{2,1,0:T(2,128)(2,1)}), bf16[128,2,768]{2,1,0:T(2,128)(2,1)S(1)}, u32[]{:S(2)}, u32[]{:S(2)}) %all-to-all-start.1) | async-done | bytes 393248 | tf_op jit(solution)/shard_map/all_to_all | solution.py:67
  88.3 1.1 shard_map.99
  89.4 12.7 %all_to_all.25 = bf16[16,2,768]{2,1,0:T(2,128)(2,1)S(1)} all-to-all(bf16[16,2,768]{2,1,0:T(2,128)(2,1)S(1)} %get-tuple-element.42), channel_id=1, replica_groups=mesh['xhi'=2,'y'=8,'core'=2,'z'=8,'xlo'=2] {'core','z'}, dimensions={0} | all-to-all | bytes 98304 | tf_op jit(solution)/shard_map/all_to_all | solution.py:67
  102.1 0.1 reduce_sum.24
  102.1 0.1 broadcast_in_dim.22
  102.2 13.9 %all_to_all.26 = bf16[32,2,768]{2,1,0:T(2,128)(2,1)S(1)} all-to-all(bf16[32,2,768]{2,1,0:T(2,128)(2,1)S(1)} %broadcast_in_dim.22), channel_id=1, replica_groups=mesh['xhi'=2,'y'=8,'core'=2,'z'=8,'xlo'=2] {'xhi','y','xlo'}, dimensions={0} | all-to-all | bytes 196608 | tf_op jit(solution)/shard_map/all_to_all | solution.py:67
  116.1 0.1 reduce_sum.25
  116.2 0.7 broadcast_in_dim.23
  116.8 5.5 %all-to-all-start.4 = ((bf16[16,2,768]{2,1,0:T(2,128)(2,1)}), bf16[16,2,768]{2,1,0:T(2,128)(2,1)S(1)}, u32[]{:S(2)}, u32[]{:S(2)}) async-start(bf16[16,2,768]{2,1,0:T(2,128)(2,1)} %broadcast_in_dim.23), calls=%async_computation.4 | async-start | bytes 98304 | tf_op jit(solution)/shard_map/all_to_all | solution.py:67
  122.4 1.2 fusion
  123.6 1.0 copy-done.7
  124.6 3.2 %shard_map.100 = (bf16[192,1408]{1,0:T(8,128)(2,1)}, bf16[192,1408]{1,0:T(8,128)(2,1)}) custom-call(bf16[128,1408]{1,0:T(8,128)(2,1)} %get-tuple-element.32.x_in, bf16[128,1408]{1,0:T(8,128)(2,1)} %get-tuple-element.33.g_in, bf16[768,128]{1,0:T(8,128)(2,1)} %get-tuple-element.34.act_in, bf16[768,128]{1,0:T(8,128)(2,1)} %get-tuple-element.35.slope_in, ...), custom_call_target="tpu_custom_call" | custom-call | flops 138412032 | bytes 5439488 | tf_op jit(solution)/shard_map/pallas_call | solution.py:28
  127.8 1.6 %all-to-all-done.4 = bf16[16,2,768]{2,1,0:T(2,128)(2,1)S(1)} async-done(((bf16[16,2,768]{2,1,0:T(2,128)(2,1)}), bf16[16,2,768]{2,1,0:T(2,128)(2,1)S(1)}, u32[]{:S(2)}, u32[]{:S(2)}) %all-to-all-start.4) | async-done | bytes 49184 | tf_op jit(solution)/shard_map/all_to_all | solution.py:67
  129.5 0.6 convert_bitcast_fusion
  (19 shorter events, 0.0 us)
Async XLA Ops:
  0.6 7.7 %copy-start = (bf16[1,256,1408]{2,1,0:T(8,128)(2,1)S(1)}, bf16[1,256,1408]{2,1,0:T(8,128)(2,1)}, u32[]{:S(2)}) copy-start(bf16[1,256,1408]{2,1,0:T(8,128)(2,1)} %param.7) | copy-start | bytes 2162692
  0.6 7.7 %copy-start.1 = (bf16[1,256,1408]{2,1,0:T(8,128)(2,1)S(1)}, bf16[1,256,1408]{2,1,0:T(8,128)(2,1)}, u32[]{:S(2)}) copy-start(bf16[1,256,1408]{2,1,0:T(8,128)(2,1)} %param.6) | copy-start | bytes 2162692
  0.7 7.7 %copy-start.2 = (bf16[1408,16]{0,1:T(8,128)(2,1)S(1)}, bf16[1408,16]{0,1:T(8,128)(2,1)}, u32[]{:S(2)}) copy-start(bf16[1408,16]{0,1:T(8,128)(2,1)} %param.9) | copy-start | bytes 135172
  2.8 29.5 %collective-permute-start = (bf16[384,1408]{1,0:T(8,128)(2,1)}, bf16[384,1408]{1,0:T(8,128)(2,1)S(1)}, u32[]{:S(2)}, u32[]{:S(2)}) collective-permute-start(bf16[384,1408]{1,0:T(8,128)(2,1)} %shard_map.94.refs_1_), channel_id=1, source_target_pairs={{0,256},{256,0},{1,257},{257,1},{2,258},{258,2},{3,259},{259,3},{4... | collective-permute-start | bytes 3244040 | tf_op jit(solution)/shard_map/ppermute | solution.py:273
  10.4 0.6 copy-start.4
  11.0 18.2 %copy-start.6 = (bf16[384,1408]{1,0:T(8,128)(2,1)S(1)}, bf16[384,1408]{1,0:T(8,128)(2,1)}, u32[]{:S(2)}) copy-start(bf16[384,1408]{1,0:T(8,128)(2,1)} %shard_map.94.refs_1_) | copy-start | bytes 3244036
  11.0 38.8 %all-to-all-start = ((bf16[128,2,1408]{2,1,0:T(2,128)(2,1)}), bf16[128,2,1408]{2,1,0:T(2,128)(2,1)}, u32[]{:S(2)}, u32[]{:S(2)}) async-start(bf16[128,2,1408]{2,1,0:T(2,128)(2,1)} %bitcast.3), calls=%async_computation | async-start | bytes 1441792 | tf_op jit(solution)/shard_map/all_to_all | solution.py:67
  29.2 20.6 %collective-permute-start.1 = (bf16[384,1408]{1,0:T(8,128)(2,1)S(1)}, bf16[384,1408]{1,0:T(8,128)(2,1)}, u32[]{:S(2)}, u32[]{:S(2)}) collective-permute-start(bf16[384,1408]{1,0:T(8,128)(2,1)S(1)} %copy-done.6), channel_id=1, source_target_pairs={{0,16},{16,0},{1,17},{17,1},{2,18},{18,2},{3,19},{19,3},{4,20},{20... | collective-permute-start | bytes 3244040 | tf_op jit(solution)/shard_map/ppermute | solution.py:279
  32.4 17.5 %copy-start.5 = (bf16[384,1408]{1,0:T(8,128)(2,1)}, bf16[384,1408]{1,0:T(8,128)(2,1)S(1)}, u32[]{:S(2)}) copy-start(bf16[384,1408]{1,0:T(8,128)(2,1)S(1)} %shard_map.96.refs_2_) | copy-start | bytes 3244036
  32.4 17.4 %collective-permute-start.2 = (bf16[384,1408]{1,0:T(8,128)(2,1)S(1)}, bf16[384,1408]{1,0:T(8,128)(2,1)}, u32[]{:S(2)}, u32[]{:S(2)}) collective-permute-start(bf16[384,1408]{1,0:T(8,128)(2,1)S(1)} %shard_map.96.refs_2_), channel_id=1, source_target_pairs={{0,16},{16,0},{1,17},{17,1},{2,18},{18,2},{3,19},{19,3},{4,20},{20... | collective-permute-start | bytes 3244040 | tf_op jit(solution)/shard_map/ppermute | solution.py:274
  55.8 16.5 %collective-permute-start.3 = (bf16[768,1408]{1,0:T(8,128)(2,1)}, bf16[768,1408]{1,0:T(8,128)(2,1)}, u32[]{:S(2)}, u32[]{:S(2)}) collective-permute-start(bf16[768,1408]{1,0:T(8,128)(2,1)} %get-tuple-element.36), channel_id=1, source_target_pairs={{0,16},{16,0},{1,17},{17,1},{2,18},{18,2},{3,19},{19,3},{4,20},{20... | collective-permute-start | bytes 6488072 | tf_op jit(solution)/shard_map/ppermute | solution.py:309
  61.5 26.8 %all-to-all-start.1 = ((bf16[128,2,768]{2,1,0:T(2,128)(2,1)}), bf16[128,2,768]{2,1,0:T(2,128)(2,1)S(1)}, u32[]{:S(2)}, u32[]{:S(2)}) async-start(bf16[128,2,768]{2,1,0:T(2,128)(2,1)} %get-tuple-element.31), calls=%async_computation.1 | async-start | bytes 786432 | tf_op jit(solution)/shard_map/all_to_all | solution.py:67
  72.3 16.0 %copy-start.3 = (f32[16,256]{1,0:T(8,128)S(1)}, f32[16,256]{1,0:T(8,128)}, u32[]{:S(2)}) copy-start(f32[16,256]{1,0:T(8,128)} %shard_map.95.part_in) | copy-start | bytes 49156
  75.3 48.3 %collective-permute-start.4 = (bf16[384,1408]{1,0:T(8,128)(2,1)}, bf16[384,1408]{1,0:T(8,128)(2,1)S(1)}, u32[]{:S(2)}, u32[]{:S(2)}) collective-permute-start(bf16[384,1408]{1,0:T(8,128)(2,1)} %shard_map.98), channel_id=1, source_target_pairs={{0,256},{256,0},{1,257},{257,1},{2,258},{258,2},{3,259},{259,3},{4... | collective-permute-start | bytes 3244040 | tf_op jit(solution)/shard_map/ppermute | solution.py:323
  116.8 12.6 %all-to-all-start.4 = ((bf16[16,2,768]{2,1,0:T(2,128)(2,1)}), bf16[16,2,768]{2,1,0:T(2,128)(2,1)S(1)}, u32[]{:S(2)}, u32[]{:S(2)}) async-start(bf16[16,2,768]{2,1,0:T(2,128)(2,1)} %broadcast_in_dim.23), calls=%async_computation.4 | async-start | bytes 98304 | tf_op jit(solution)/shard_map/all_to_all | solution.py:67
  123.6 1.0 copy-start.7

commit v11 on v10

--- a/solution.py
+++ b/solution.py
@@ -269,6 +269,7 @@
         0,
         hbm=True,
         scratch=[pltpu.VMEM((384, 1408), BF16), pltpu.SemaphoreType.DMA((4,))],
+        limit=SMALL,
     )[0]
     over_x = hold(lax.ppermute(own, "xhi", SWAP))
     over_both = lax.ppermute(over_x, "core", SWAP)

time: 131 us -> 131 us (level)
  local copies, waits for them, and re-layouts: 2.34 us -> 5.28 us
  Pallas kernels: 19.5 us -> 17.6 us
    unnamed x16 -> x20, local copies, waits for them, and re-layouts: 1.62 us -> 4.55 us
    pallas_call x6, Pallas kernels: 16.4 us -> 14.5 us  [call(): pl.pallas_call(kernel, out_shape=out, in_specs=[pl.BlockSpec(memory_space...]
where the time goes in v11:
time: 131 us; the launch traced here: 130 us
  starting transfers between devices  56 us (43%)
  blocking collectives  27 us (21%)
  waiting for transfers between devices  21.7 us (17%)
  Pallas kernels  17.6 us (13%)
  local copies, waits for them, and re-layouts  5.28 us (4%)
    all_to_all x3, starting transfers between devices, exchange(): return lax.all_to_all(blocks, axes, split_axis=0, concat_axis=0, tiled=True)  33.3 us
    all_to_all x2, blocking collectives, exchange(): return lax.all_to_all(blocks, axes, split_axis=0, concat_axis=0, tiled=True)  27 us
    all_to_all x3, waiting for transfers between devices, exchange(): return lax.all_to_all(blocks, axes, split_axis=0, concat_axis=0, tiled=True)  21.7 us
    pallas_call x6, Pallas kernels, call(): pl.pallas_call(kernel, out_shape=out, in_specs=[pl.BlockSpec(memory_space...  14.5 us
    ppermute x1, starting transfers between devices, shards(): from_core = lax.ppermute(to_core, 'core', SWAP)  5.71 us
    ppermute x1, starting transfers between devices, shards(): over_x = hold(lax.ppermute(own, 'xhi', SWAP))  5.61 us
    unnamed x20, local copies, waits for them, and re-layouts  4.55 us
    ppermute x1, starting transfers between devices, shards(): from_x = lax.ppermute(to_x, 'xhi', SWAP)  4.34 us
  transfers between devices with their start and end apart: 8, of which 3 were waited for; matrix products, arithmetic and copies ran while one was open for 2% of the time, Pallas kernels for 9%

profile of v11, /device:TPU:1, one launch (start us, length us, event | category | flops | bytes accessed | tf_op | source)
XLA Modules:
  0.0 130.4 jit_solution(10186549712289074322)
XLA Ops:
  0.6 1.0 copy-done.3
  1.7 1.0 copy-done.4
  2.7 0.3 shard_map.94.refs_1_
  3.0 5.6 %collective-permute-start = (bf16[384,1408]{1,0:T(8,128)(2,1)S(1)}, bf16[384,1408]{1,0:T(8,128)(2,1)}, u32[]{:S(2)}, u32[]{:S(2)}) collective-permute-start(bf16[384,1408]{1,0:T(8,128)(2,1)S(1)} %shard_map.94.refs_1_), channel_id=1, source_target_pairs={{0,256},{256,0},{1,257},{257,1},{2,258},{258,2},{3,259},{259,3},{4... | collective-permute-start | bytes 3244040 | tf_op jit(solution)/shard_map/ppermute | solution.py:274
  8.7 2.0 %shard_map.93 = (bf16[8,16,2,1408]{3,2,1,0:T(2,128)(2,1)}, f32[16,256]{1,0:T(8,128)S(1)}, f32[16,256]{1,0:T(8,128)S(1)}) custom-call(bf16[256,1408]{1,0:T(8,128)(2,1)S(1)} %bitcast.21, bf16[256,1408]{1,0:T(8,128)(2,1)S(1)} %bitcast.20, bf16[16,1408]{1,0:T(8,128)(2,1)S(1)} %bitcast.25), custom_call_target="tpu_custom_call" | custom-call | flops 40000000 | bytes 3000000 | tf_op jit(solution)/shard_map/pallas_call | solution.py:93
  10.7 0.6 copy-done.7
  11.3 17.6 %all-to-all-start = ((bf16[128,2,1408]{2,1,0:T(2,128)(2,1)}), bf16[128,2,1408]{2,1,0:T(2,128)(2,1)S(1)}, u32[]{:S(2)}, u32[]{:S(2)}) async-start(bf16[128,2,1408]{2,1,0:T(2,128)(2,1)} %bitcast.3), calls=%async_computation | async-start | bytes 1441792 | tf_op jit(solution)/shard_map/all_to_all | solution.py:67
  28.9 3.1 %collective-permute-start.1 = (bf16[384,1408]{1,0:T(8,128)(2,1)S(1)}, bf16[384,1408]{1,0:T(8,128)(2,1)}, u32[]{:S(2)}, u32[]{:S(2)}) collective-permute-start(bf16[384,1408]{1,0:T(8,128)(2,1)S(1)} %shard_map.94.refs_1_), channel_id=1, source_target_pairs={{0,16},{16,0},{1,17},{17,1},{2,18},{18,2},{3,19},{19,3},{4,20},{20... | collective-permute-start | bytes 3244040 | tf_op jit(solution)/shard_map/ppermute | solution.py:280
  32.1 3.8 %collective-permute-start.2 = (bf16[384,1408]{1,0:T(8,128)(2,1)}, bf16[384,1408]{1,0:T(8,128)(2,1)}, u32[]{:S(2)}, u32[]{:S(2)}) collective-permute-start(bf16[384,1408]{1,0:T(8,128)(2,1)} %shard_map.96.refs_2_), channel_id=1, source_target_pairs={{0,16},{16,0},{1,17},{17,1},{2,18},{18,2},{3,19},{19,3},{4,20},{20... | collective-permute-start | bytes 3244040 | tf_op jit(solution)/shard_map/ppermute | solution.py:275
  35.9 2.0 %shard_map.95.part_in = f32[16,256]{1,0:T(8,128)} custom-call(bf16[16,1408]{1,0:T(8,128)(2,1)} %bitcast.27, bf16[256,1408]{1,0:T(8,128)(2,1)} %bitcast.19, f32[16,256]{1,0:T(8,128)} %copy-done.7), custom_call_target="tpu_custom_call" | custom-call | flops 11534336 | bytes 798720 | tf_op jit(solution)/shard_map/pallas_call | solution.py:28
  38.0 11.9 %all-to-all-done.refs_0_ = bf16[128,2,1408]{2,1,0:T(2,128)(2,1)S(1)} async-done(((bf16[128,2,1408]{2,1,0:T(2,128)(2,1)}), bf16[128,2,1408]{2,1,0:T(2,128)(2,1)S(1)}, u32[]{:S(2)}, u32[]{:S(2)}) %all-to-all-start) | async-done | bytes 720928 | tf_op jit(solution)/shard_map/all_to_all | solution.py:67
  49.9 0.8 copy-done.9
  50.7 6.0 %shard_map.97 = (bf16[128,2,768]{2,1,0:T(2,128)(2,1)}, bf16[768,1408]{1,0:T(8,128)(2,1)}, bf16[768,128]{1,0:T(8,128)(2,1)}, bf16[768,128]{1,0:T(8,128)(2,1)}, bf...) custom-call(bf16[128,2,1408]{2,1,0:T(2,128)(2,1)} %copy-done.9, bf16[384,1408]{1,0:T(8,128)(2,1)} %copy-done.2, ...), custom_call_target="tpu_custom_call" | custom-call | flops 1384120320 | bytes 8716288 | tf_op jit(solution)/shard_map/pallas_call | solution.py:28
  56.7 5.7 %collective-permute-start.3 = (bf16[768,1408]{1,0:T(8,128)(2,1)}, bf16[768,1408]{1,0:T(8,128)(2,1)}, u32[]{:S(2)}, u32[]{:S(2)}) collective-permute-start(bf16[768,1408]{1,0:T(8,128)(2,1)} %get-tuple-element.36), channel_id=1, source_target_pairs={{0,16},{16,0},{1,17},{17,1},{2,18},{18,2},{3,19},{19,3},{4,20},{20... | collective-permute-start | bytes 6488072 | tf_op jit(solution)/shard_map/ppermute | solution.py:310
  62.4 10.2 %all-to-all-start.1 = ((bf16[128,2,768]{2,1,0:T(2,128)(2,1)}), bf16[128,2,768]{2,1,0:T(2,128)(2,1)S(1)}, u32[]{:S(2)}, u32[]{:S(2)}) async-start(bf16[128,2,768]{2,1,0:T(2,128)(2,1)} %get-tuple-element.31), calls=%async_computation.1 | async-start | bytes 786432 | tf_op jit(solution)/shard_map/all_to_all | solution.py:67
  72.7 0.0 copy-start.6
  72.7 3.0 %shard_map.98 = bf16[384,1408]{1,0:T(8,128)(2,1)} custom-call(bf16[128,1408]{1,0:T(8,128)(2,1)} %get-tuple-element.32.x_in, bf16[128,1408]{1,0:T(8,128)(2,1)} %get-tuple-element.33.g_in, bf16[768,128]{1,0:T(8,128)(2,1)} %get-tuple-element.34.act_in, bf16[768,128]{1,0:T(8,128)(2,1)} %get-tuple-element.35.slope_in, ...), custom_call_target="tpu_custom_call" | custom-call | flops 138412032 | bytes 4358144 | tf_op jit(solution)/shard_map/pallas_call | solution.py:28
  75.7 4.3 %collective-permute-start.4 = (bf16[384,1408]{1,0:T(8,128)(2,1)}, bf16[384,1408]{1,0:T(8,128)(2,1)S(1)}, u32[]{:S(2)}, u32[]{:S(2)}) collective-permute-start(bf16[384,1408]{1,0:T(8,128)(2,1)} %shard_map.98), channel_id=1, source_target_pairs={{0,256},{256,0},{1,257},{257,1},{2,258},{258,2},{3,259},{259,3},{4... | collective-permute-start | bytes 3244040 | tf_op jit(solution)/shard_map/ppermute | solution.py:324
  80.0 8.2 %all-to-all-done.1.returned = bf16[128,2,768]{2,1,0:T(2,128)(2,1)S(1)} async-done(((bf16[128,2,768]{2,1,0:T(2,128)(2,1)}), bf16[128,2,768]{2,1,0:T(2,128)(2,1)S(1)}, u32[]{:S(2)}, u32[]{:S(2)}) %all-to-all-start.1) | async-done | bytes 393248 | tf_op jit(solution)/shard_map/all_to_all | solution.py:67
  88.2 1.1 shard_map.99
  89.3 13.1 %all_to_all.25 = bf16[16,2,768]{2,1,0:T(2,128)(2,1)S(1)} all-to-all(bf16[16,2,768]{2,1,0:T(2,128)(2,1)S(1)} %get-tuple-element.42), channel_id=1, replica_groups=mesh['xhi'=2,'y'=8,'core'=2,'z'=8,'xlo'=2] {'core','z'}, dimensions={0} | all-to-all | bytes 98304 | tf_op jit(solution)/shard_map/all_to_all | solution.py:67
  102.4 0.1 reduce_sum.24
  102.5 0.1 broadcast_in_dim.22
  102.6 13.8 %all_to_all.26 = bf16[32,2,768]{2,1,0:T(2,128)(2,1)S(1)} all-to-all(bf16[32,2,768]{2,1,0:T(2,128)(2,1)S(1)} %broadcast_in_dim.22), channel_id=1, replica_groups=mesh['xhi'=2,'y'=8,'core'=2,'z'=8,'xlo'=2] {'xhi','y','xlo'}, dimensions={0} | all-to-all | bytes 196608 | tf_op jit(solution)/shard_map/all_to_all | solution.py:67
  116.4 0.1 reduce_sum.25
  116.5 0.7 broadcast_in_dim.23
  117.2 5.5 %all-to-all-start.4 = ((bf16[16,2,768]{2,1,0:T(2,128)(2,1)}), bf16[16,2,768]{2,1,0:T(2,128)(2,1)S(1)}, u32[]{:S(2)}, u32[]{:S(2)}) async-start(bf16[16,2,768]{2,1,0:T(2,128)(2,1)} %broadcast_in_dim.23), calls=%async_computation.4 | async-start | bytes 98304 | tf_op jit(solution)/shard_map/all_to_all | solution.py:67
  122.7 1.2 fusion
  123.9 1.0 copy-done.8
  124.9 3.2 %shard_map.100 = (bf16[192,1408]{1,0:T(8,128)(2,1)}, bf16[192,1408]{1,0:T(8,128)(2,1)}) custom-call(bf16[128,1408]{1,0:T(8,128)(2,1)} %get-tuple-element.32.x_in, bf16[128,1408]{1,0:T(8,128)(2,1)} %get-tuple-element.33.g_in, bf16[768,128]{1,0:T(8,128)(2,1)} %get-tuple-element.34.act_in, bf16[768,128]{1,0:T(8,128)(2,1)} %get-tuple-element.35.slope_in, ...), custom_call_target="tpu_custom_call" | custom-call | flops 138412032 | bytes 5439488 | tf_op jit(solution)/shard_map/pallas_call | solution.py:28
  128.2 1.6 %all-to-all-done.4 = bf16[16,2,768]{2,1,0:T(2,128)(2,1)S(1)} async-done(((bf16[16,2,768]{2,1,0:T(2,128)(2,1)}), bf16[16,2,768]{2,1,0:T(2,128)(2,1)S(1)}, u32[]{:S(2)}, u32[]{:S(2)}) %all-to-all-start.4) | async-done | bytes 49184 | tf_op jit(solution)/shard_map/all_to_all | solution.py:67
  129.8 0.6 convert_bitcast_fusion
  (23 shorter events, 0.1 us)
Async XLA Ops:
  0.6 1.0 copy-start.3
  1.7 1.0 copy-start.4
  2.7 5.9 %copy-start = (bf16[1,256,1408]{2,1,0:T(8,128)(2,1)S(1)}, bf16[1,256,1408]{2,1,0:T(8,128)(2,1)}, u32[]{:S(2)}) copy-start(bf16[1,256,1408]{2,1,0:T(8,128)(2,1)} %param.7) | copy-start | bytes 2162692
  2.7 5.9 %copy-start.1 = (bf16[1,256,1408]{2,1,0:T(8,128)(2,1)S(1)}, bf16[1,256,1408]{2,1,0:T(8,128)(2,1)}, u32[]{:S(2)}) copy-start(bf16[1,256,1408]{2,1,0:T(8,128)(2,1)} %param.6) | copy-start | bytes 2162692
  2.7 5.9 %copy-start.5 = (bf16[1408,16]{0,1:T(8,128)(2,1)S(1)}, bf16[1408,16]{0,1:T(8,128)(2,1)}, u32[]{:S(2)}) copy-start(bf16[1408,16]{0,1:T(8,128)(2,1)} %param.9) | copy-start | bytes 135172
  3.0 25.9 %copy-start.2 = (bf16[384,1408]{1,0:T(8,128)(2,1)}, bf16[384,1408]{1,0:T(8,128)(2,1)S(1)}, u32[]{:S(2)}) copy-start(bf16[384,1408]{1,0:T(8,128)(2,1)S(1)} %shard_map.94.refs_1_) | copy-start | bytes 3244036
  3.0 29.0 %collective-permute-start = (bf16[384,1408]{1,0:T(8,128)(2,1)S(1)}, bf16[384,1408]{1,0:T(8,128)(2,1)}, u32[]{:S(2)}, u32[]{:S(2)}) collective-permute-start(bf16[384,1408]{1,0:T(8,128)(2,1)S(1)} %shard_map.94.refs_1_), channel_id=1, source_target_pairs={{0,256},{256,0},{1,257},{257,1},{2,258},{258,2},{3,259},{259,3},{4... | collective-permute-start | bytes 3244040 | tf_op jit(solution)/shard_map/ppermute | solution.py:274
  10.7 0.6 copy-start.7
  11.3 38.5 %all-to-all-start = ((bf16[128,2,1408]{2,1,0:T(2,128)(2,1)}), bf16[128,2,1408]{2,1,0:T(2,128)(2,1)S(1)}, u32[]{:S(2)}, u32[]{:S(2)}) async-start(bf16[128,2,1408]{2,1,0:T(2,128)(2,1)} %bitcast.3), calls=%async_computation | async-start | bytes 1441792 | tf_op jit(solution)/shard_map/all_to_all | solution.py:67
  28.9 21.0 %collective-permute-start.1 = (bf16[384,1408]{1,0:T(8,128)(2,1)S(1)}, bf16[384,1408]{1,0:T(8,128)(2,1)}, u32[]{:S(2)}, u32[]{:S(2)}) collective-permute-start(bf16[384,1408]{1,0:T(8,128)(2,1)S(1)} %shard_map.94.refs_1_), channel_id=1, source_target_pairs={{0,16},{16,0},{1,17},{17,1},{2,18},{18,2},{3,19},{19,3},{4,20},{20... | collective-permute-start | bytes 3244040 | tf_op jit(solution)/shard_map/ppermute | solution.py:280
  32.1 17.8 %collective-permute-start.2 = (bf16[384,1408]{1,0:T(8,128)(2,1)}, bf16[384,1408]{1,0:T(8,128)(2,1)}, u32[]{:S(2)}, u32[]{:S(2)}) collective-permute-start(bf16[384,1408]{1,0:T(8,128)(2,1)} %shard_map.96.refs_2_), channel_id=1, source_target_pairs={{0,16},{16,0},{1,17},{17,1},{2,18},{18,2},{3,19},{19,3},{4,20},{20... | collective-permute-start | bytes 3244040 | tf_op jit(solution)/shard_map/ppermute | solution.py:275
  49.9 0.9 copy-start.9
  56.7 16.0 %collective-permute-start.3 = (bf16[768,1408]{1,0:T(8,128)(2,1)}, bf16[768,1408]{1,0:T(8,128)(2,1)}, u32[]{:S(2)}, u32[]{:S(2)}) collective-permute-start(bf16[768,1408]{1,0:T(8,128)(2,1)} %get-tuple-element.36), channel_id=1, source_target_pairs={{0,16},{16,0},{1,17},{17,1},{2,18},{18,2},{3,19},{19,3},{4,20},{20... | collective-permute-start | bytes 6488072 | tf_op jit(solution)/shard_map/ppermute | solution.py:310
  62.4 25.8 %all-to-all-start.1 = ((bf16[128,2,768]{2,1,0:T(2,128)(2,1)}), bf16[128,2,768]{2,1,0:T(2,128)(2,1)S(1)}, u32[]{:S(2)}, u32[]{:S(2)}) async-start(bf16[128,2,768]{2,1,0:T(2,128)(2,1)} %get-tuple-element.31), calls=%async_computation.1 | async-start | bytes 786432 | tf_op jit(solution)/shard_map/all_to_all | solution.py:67
  72.7 15.5 %copy-start.6 = (f32[16,256]{1,0:T(8,128)S(1)}, f32[16,256]{1,0:T(8,128)}, u32[]{:S(2)}) copy-start(f32[16,256]{1,0:T(8,128)} %shard_map.95.part_in) | copy-start | bytes 49156
  75.7 48.3 %collective-permute-start.4 = (bf16[384,1408]{1,0:T(8,128)(2,1)}, bf16[384,1408]{1,0:T(8,128)(2,1)S(1)}, u32[]{:S(2)}, u32[]{:S(2)}) collective-permute-start(bf16[384,1408]{1,0:T(8,128)(2,1)} %shard_map.98), channel_id=1, source_target_pairs={{0,256},{256,0},{1,257},{257,1},{2,258},{258,2},{3,259},{259,3},{4... | collective-permute-start | bytes 3244040 | tf_op jit(solution)/shard_map/ppermute | solution.py:324
  117.2 12.6 %all-to-all-start.4 = ((bf16[16,2,768]{2,1,0:T(2,128)(2,1)}), bf16[16,2,768]{2,1,0:T(2,128)(2,1)S(1)}, u32[]{:S(2)}, u32[]{:S(2)}) async-start(bf16[16,2,768]{2,1,0:T(2,128)(2,1)} %broadcast_in_dim.23), calls=%async_computation.4 | async-start | bytes 98304 | tf_op jit(solution)/shard_map/all_to_all | solution.py:67
  123.9 1.0 copy-start.8
